TPU v7x, 32 devices: a whole 2x2x4 slice. The times are simulated.
32 devices in a mesh: col: 4 (over z), rhs: 8 (over y, x, core).
Axes of the slice: x: 2, y: 2, z: 4, core: 2. Of those that a mesh axis runs over, the one named last changes fastest.
Arguments:
- desc_rows: bfloat16 [32, 1024, 1024], P(('col', 'rhs')), may hold values from -6 to 6
- upd_factor: bfloat16 [32, 1024, 1024], P(('col', 'rhs')), may hold values from -0.03125 to 0.03125
- update_index: int32 [32, 1024], P(('col', 'rhs')), may hold values from -1 to 1023, as said below
- owner_map: int32 [32, 4], P(('col', 'rhs')), may hold values from 0 to 3, each once within a row
- sep_rhs: float32 [1024, 4096], P('rhs', 'col'), may hold values from -6 to 6
- factor_rows: bfloat16 [4096, 4096], P('col'), may hold values from -0.046875 to 0.046875
- diag_inverse: bfloat16 [4096, 1024], P('col'), may hold values from -1 to 1
Outputs:
- solved: float32 [1024, 4096], P('rhs', 'col')
Inputs may be any that keep to these rules, and one draw needn't show every extreme that they name: `update_index`: within each group of 256 slots of a descendant the live entries come first and are distinct rows of the block that owner_map names for that group; the other slots hold -1. Every descendant has at least one group with all 256 slots live.
All inputs are finite; a program needn't handle non-finite values.
Results may differ from a plain program's by a relative error of at most 0.004.
Values sent between devices are 32-bit elements; how exact they have to be, the bound alone decides.
No kernel may reach another device: no remote copies, remote signals or barrier semaphores. Data moves between devices by JAX's collectives and lax.ppermute only.
A program may use at most 128 MiB of HBM per device.

v0:
```python
import jax
import jax.numpy as jnp
from jax import lax
from jax.sharding import PartitionSpec as P


def passed_along(value, axis, steps):
    count = lax.axis_size(axis)
    first, last = (max(0, -steps), min(count, count - steps))
    return lax.ppermute(value, axis, [(source, source + steps) for source in range(first, last)])


def block_order(owner_row, count):
    places = jnp.arange(count, dtype=jnp.int32)
    matches = (owner_row[None, :] == places[:, None]).astype(jnp.int32)
    return jnp.sum(matches * places[None, :], axis=1)


def local(desc_rows, upd_factor, update_index, owner_map, sep_rhs, factor_rows, diag_inverse):
    col_count = lax.axis_size("col")
    rhs_count = lax.axis_size("rhs")
    block_size = diag_inverse.shape[0]
    tile_rows = sep_rhs.shape[0]
    full_width = factor_rows.shape[1]
    capacity = update_index.shape[1] // col_count
    source_group = block_order(owner_map[0], col_count)
    factor_grouped = jnp.take(
        upd_factor[0].reshape(block_size, col_count, capacity), source_group, axis=1
    )
    local_index = jnp.take(update_index[0].reshape(col_count, capacity), source_group, axis=0)
    updates = jnp.einsum(
        "srn,ngc->gscr",
        desc_rows[0].reshape(rhs_count, tile_rows, block_size),
        factor_grouped,
        preferred_element_type=jnp.float32,
    )
    index_copies = jnp.broadcast_to(local_index[:, None, :], (col_count, rhs_count, capacity))
    arrived, arrived_index = (
        lax.all_to_all(
            updates.reshape(col_count * rhs_count, capacity, tile_rows),
            ("col", "rhs"),
            split_axis=0,
            concat_axis=0,
            tiled=True,
        ),
        lax.all_to_all(
            index_copies.reshape(col_count * rhs_count, capacity),
            ("col", "rhs"),
            split_axis=0,
            concat_axis=0,
            tiled=True,
        ),
    )
    targets = jnp.where(arrived_index >= 0, arrived_index, block_size).reshape(-1)
    summed = jax.ops.segment_sum(
        arrived.reshape(-1, tile_rows), targets, num_segments=block_size + 1
    )
    corrected = sep_rhs - summed[:block_size].T
    own_place = lax.axis_index("col")
    result = jnp.zeros((tile_rows, block_size), jnp.float32)
    carried = jnp.zeros((tile_rows, full_width), jnp.float32)
    for station in range(col_count):
        begin = station * block_size

        def advance_rest(carry_state, begin=begin):
            pending = carry_state[1]
            reduced = corrected - pending[:, :block_size]
            solved = jnp.dot(
                reduced.astype(jnp.bfloat16), diag_inverse, preferred_element_type=jnp.float32
            )
            pending = pending + jnp.dot(
                solved.astype(jnp.bfloat16),
                factor_rows[:, begin:],
                preferred_element_type=jnp.float32,
            )
            return (solved, pending)

        result, carried = lax.cond(
            own_place == station, advance_rest, lambda carry_state: carry_state, (result, carried)
        )
        if station + 1 < col_count:
            carried = passed_along(carried[:, block_size:], "col", 1)
    return result


def solution(mesh):
    placed = (
        P(("col", "rhs"), None, None),
        P(("col", "rhs"), None, None),
        P(("col", "rhs"), None),
        P(("col", "rhs"), None),
        P("rhs", "col"),
        P("col", None),
        P("col", None),
    )
    return jax.shard_map(
        local, mesh=mesh, in_specs=placed, out_specs=P("rhs", "col"), check_vma=False
    )
```

profile of v0, /device:TPU:24, one launch (start us, length us, event | category | flops | bytes accessed | tf_op | source)
XLA Modules:
  0.0 287.4 jit_solution(6925834486932782899)
XLA Ops:
  0.0 0.0 copy-start
  0.0 0.9 select_reduce_fusion
  1.0 0.5 broadcast.90
  1.5 1.3 reduce.3
  2.8 0.6 gather_fusion
  3.4 0.1 broadcast_select_fusion
  3.5 0.7 all_to_all.11
  4.1 5.9 %all-to-all-start = ((s32[32,1,256]{2,1,0:T(1,128)}), s32[32,1,256]{2,1,0:T(1,128)S(1)}, u32[]{:S(2)}, u32[]{:S(2)}) async-start(s32[32,1,256]{2,1,0:T(1,128)} %all_to_all.11), calls=%async_computation | async-start | bytes 65536 | tf_op jit(solution)/shard_map/all_to_all | solution.py:46
  10.0 3.9 %copy.33 = bf16[1,1024,1024]{1,2,0:T(8,128)(2,1)} copy(bf16[1,1024,1024]{2,1,0:T(8,128)(2,1)} %param.16) | data formatting | bytes 4194304 | tf_op args[1]
  13.9 3.9 %copy.34 = bf16[1024,4,256]{2,0,1:T(8,128)(2,1)} copy(bf16[1024,4,256]{0,2,1:T(8,128)(2,1)} %bitcast.34) | data formatting | bytes 4194304 | tf_op jit(solution)/shard_map/reshape;squeeze | solution.py:28
  17.9 3.6 %gather_fusion.1 = bf16[4,1024,256]{2,1,0:T(8,128)(2,1)} fusion(bf16[1024,4,256]{2,0,1:T(8,128)(2,1)} %copy.34, s32[1024]{0:T(1024)S(1)} %pad_clamp_fusion), kind=kCustom, calls=%fused_computation.1 | custom fusion | bytes 4194320 | tf_op jit(solution)/shard_map/jit(_take)/gather | solution.py:27
  21.5 0.0 copy-done
  21.5 5.8 %fusion.19 = f32[4,256,8,128]{3,1,2,0:T(8,128)} fusion(bf16[8,128,1024,1]{2,1,0,3:T(8,128)(2,1)S(1)} %bitcast.33, bf16[4,1024,256]{2,1,0:T(8,128)(2,1)} %gather_fusion.1, pred[4]{0:T(512)(128)(4,1)S(1)} %compare_and_fusion), kind=kOutput, calls=%fused_computation.21 | convolution fusion | flops 2148532224 | bytes 8388612 | tf_op jit(solution)/shard_map/srn,ngc->gscr/dot_general | solution.py:31
  27.3 0.0 all-to-all-done
  27.3 0.0 copy-start.2
  27.3 5.9 %all-to-all-start.1 = ((f32[32,256,128]{2,1,0:T(8,128)}), f32[32,256,128]{2,1,0:T(8,128)}, u32[]{:S(2)}, u32[]{:S(2)}) async-start(f32[32,256,128]{2,1,0:T(8,128)} %bitcast.35), calls=%async_computation.1 | async-start | bytes 8388608 | tf_op jit(solution)/shard_map/all_to_all | solution.py:39
  33.2 0.0 copy-done.2
  33.2 1.0 copy.36
  34.2 91.3 %all-to-all-done.1 = f32[32,256,128]{2,1,0:T(8,128)} async-done(((f32[32,256,128]{2,1,0:T(8,128)}), f32[32,256,128]{2,1,0:T(8,128)}, u32[]{:S(2)}, u32[]{:S(2)}) %all-to-all-start.1) | async-done | bytes 4194336 | tf_op jit(solution)/shard_map/all_to_all | solution.py:39
  125.5 50.6 %scatter_custom_fusion = f32[1025,128]{1,0:T(8,128)S(1)} fusion(s32[8192]{0:T(1024)S(1)} %bitcast.37, f32[8192,128]{1,0:T(8,128)} %bitcast.12, f32[]{:T(128)} %constant.33.clone.1), kind=kCustom, calls=%fused_computation.28 | custom fusion | flops 1048576 | bytes 525312 | tf_op jit(solution)/shard_map/scatter-add | solution.py:55
  176.2 1.1 fusion.24
  177.3 2.4 conditional.4
  177.3 1.6 broadcast_in_dim.33
  178.8 0.8 broadcast_in_dim.32
  179.7 2.7 slice.25
  182.4 1.3 collective-permute-start
  183.7 37.3 %collective-permute-done = f32[128,3072]{1,0:T(8,128)} collective-permute-done((f32[128,3072]{1,0:T(8,128)}, f32[128,3072]{1,0:T(8,128)}, u32[]{:S(2)}, u32[]{:S(2)}) %collective-permute-start) | collective-permute-done | bytes 1572896 | tf_op jit(solution)/shard_map/ppermute | solution.py:10
  221.0 2.3 slice.26
  223.3 1.3 collective-permute-start.1
  224.6 25.2 %collective-permute-done.1 = f32[128,2048]{1,0:T(8,128)} collective-permute-done((f32[128,2048]{1,0:T(8,128)}, f32[128,2048]{1,0:T(8,128)}, u32[]{:S(2)}, u32[]{:S(2)}) %collective-permute-start.1) | collective-permute-done | bytes 1048608 | tf_op jit(solution)/shard_map/ppermute | solution.py:10
  249.8 1.9 slice.27
  251.7 1.3 collective-permute-start.2
  253.0 30.5 %collective-permute-done.2 = f32[128,1024]{1,0:T(8,128)S(1)} collective-permute-done((f32[128,1024]{1,0:T(8,128)}, f32[128,1024]{1,0:T(8,128)S(1)}, u32[]{:S(2)}, u32[]{:S(2)}) %collective-permute-start.2) | collective-permute-done | bytes 524320 | tf_op jit(solution)/shard_map/ppermute | solution.py:10
  283.4 4.0 %conditional.7 = (f32[128,1024]{1,0:T(8,128)}) conditional(s32[]{:T(128)} %convert_element_type.34, f32[128,1024]{1,0:T(8,128)} %get-tuple-element.72, (f32[128,1024]{0,1:T(8,128)S(1)}, f32[128,1024]{1,0:T(8,128)S(1)}, bf16[1024,1024]{1,0:T(8,128)(2,1)}) %tuple.43), branch_computations={%region_8.9_spmd, %region_9.10_spmd} | conditional | flops 268697600 | bytes 6815780 | solution.py:78
  283.4 0.0 copy-start.1
  283.4 0.8 copy-done.1
  284.2 0.2 copy.40
  284.4 3.0 %fusion.18 = f32[128,1024]{1,0:T(8,128)} fusion(bf16[1024,1024]{1,0:T(8,128)(2,1)} %get-tuple-element.61, f32[128,1024]{1,0:T(8,128)S(1)} %copy.40, f32[128,1024]{1,0:T(8,128)} %copy-done.1), kind=kOutput, calls=%fused_computation.20 | convolution fusion | flops 268697600 | bytes 3670016 | tf_op jit(solution)/shard_map/cond/branch_1_fun/dot_general | solution.py:68
  (8 shorter events, 0.1 us)
Async XLA Ops:
  0.0 21.5 %copy-start = (bf16[1,1024,1024]{2,1,0:T(8,128)(2,1)S(1)}, bf16[1,1024,1024]{2,1,0:T(8,128)(2,1)}, u32[]{:S(2)}) copy-start(bf16[1,1024,1024]{2,1,0:T(8,128)(2,1)} %param.15) | copy-start | bytes 6291460
  4.1 23.1 %all-to-all-start = ((s32[32,1,256]{2,1,0:T(1,128)}), s32[32,1,256]{2,1,0:T(1,128)S(1)}, u32[]{:S(2)}, u32[]{:S(2)}) async-start(s32[32,1,256]{2,1,0:T(1,128)} %all_to_all.11), calls=%async_computation | async-start | bytes 65536 | tf_op jit(solution)/shard_map/all_to_all | solution.py:46
  27.3 5.9 %copy-start.2 = (f32[128,1024]{1,0:T(8,128)S(1)}, f32[128,1024]{1,0:T(8,128)}, u32[]{:S(2)}) copy-start(f32[128,1024]{1,0:T(8,128)} %param.19) | copy-start | bytes 1572868
  27.3 98.3 %all-to-all-start.1 = ((f32[32,256,128]{2,1,0:T(8,128)}), f32[32,256,128]{2,1,0:T(8,128)}, u32[]{:S(2)}, u32[]{:S(2)}) async-start(f32[32,256,128]{2,1,0:T(8,128)} %bitcast.35), calls=%async_computation.1 | async-start | bytes 8388608 | tf_op jit(solution)/shard_map/all_to_all | solution.py:39
  182.4 38.6 %collective-permute-start = (f32[128,3072]{1,0:T(8,128)}, f32[128,3072]{1,0:T(8,128)}, u32[]{:S(2)}, u32[]{:S(2)}) collective-permute-start(f32[128,3072]{1,0:T(8,128)} %slice.25), channel_id=1, source_target_pairs={{0,8},{8,16},{16,24},{1,9},{9,17},{17,25},{2,10},{10,18},{18,26},{... | collective-permute-start | bytes 4718600 | tf_op jit(solution)/shard_map/ppermute | solution.py:10
  223.3 26.5 %collective-permute-start.1 = (f32[128,2048]{1,0:T(8,128)}, f32[128,2048]{1,0:T(8,128)}, u32[]{:S(2)}, u32[]{:S(2)}) collective-permute-start(f32[128,2048]{1,0:T(8,128)} %slice.26), channel_id=1, source_target_pairs={{0,8},{8,16},{16,24},{1,9},{9,17},{17,25},{2,10},{10,18},{18,26},{... | collective-permute-start | bytes 3145736 | tf_op jit(solution)/shard_map/ppermute | solution.py:10
  251.7 31.8 %collective-permute-start.2 = (f32[128,1024]{1,0:T(8,128)}, f32[128,1024]{1,0:T(8,128)S(1)}, u32[]{:S(2)}, u32[]{:S(2)}) collective-permute-start(f32[128,1024]{1,0:T(8,128)} %slice.27), channel_id=1, source_target_pairs={{0,8},{8,16},{16,24},{1,9},{9,17},{17,25},{2,10},{10,18},{18,26},{... | collective-permute-start | bytes 1572872 | tf_op jit(solution)/shard_map/ppermute | solution.py:10
  283.4 0.8 copy-start.1
where the time goes:
time: 288 us; the launch traced here: 287 us
  waiting for transfers between devices  184 us (64%)
  other arithmetic  54.1 us (19%)
  local copies, waits for them, and re-layouts  24.5 us (9%)
  starting transfers between devices  15.6 us (5%)
  matrix products  8.8 us (3%)
    ppermute x3, waiting for transfers between devices, passed_along(): lax.ppermute(value, axis, [(source, source + steps) for source in range(f...  92.9 us
    all_to_all x1, waiting for transfers between devices, local(): lax.all_to_all(updates.reshape(col_count * rhs_count, capacity, tile_rows...  91.3 us
    scatter-add x1, other arithmetic, local(): jax.ops.segment_sum(arrived.reshape(-1, tile_rows), targets, num_segments...  50.6 us
    slice x3, local copies, waits for them, and re-layouts, local(): carried = passed_along(carried[:, block_size:], 'col', 1)  6.93 us
    all_to_all x1, starting transfers between devices, local(): lax.all_to_all(updates.reshape(col_count * rhs_count, capacity, tile_rows...  5.88 us
    all_to_all x1, starting transfers between devices, local(): lax.all_to_all(index_copies.reshape(col_count * rhs_count, capacity), ('c...  5.87 us
    dot_general x1, matrix products, local(): jnp.einsum('srn,ngc->gscr', desc_rows[0].reshape(rhs_count, tile_rows, bl...  5.79 us
  transfers between devices with their start and end apart: 5, of which 4 were waited for; matrix products, arithmetic and copies ran while one was open for 6% of the time, Pallas kernels for 0%

commit v1 on v0

v1 whole, which is shorter than its diff:
```python
import functools

import jax
import jax.numpy as jnp
from jax import lax
from jax.experimental import pallas as pl
from jax.experimental.pallas import tpu as pltpu
from jax.sharding import PartitionSpec as P

PARAMS = pltpu.CompilerParams(vmem_limit_bytes=40 * 1024 * 1024)
INDEX_ROWS = 8
SOURCES = 4


def whole():
    return pl.BlockSpec(memory_space=pltpu.VMEM)


def contract(left, right):
    return jnp.dot(left, right, preferred_element_type=jnp.float32)


def group_of(owner_ref, block, count):
    found = jnp.int32(0)
    for place in range(count):
        found = found + jnp.where(owner_ref[0, place] == block, place, 0)
    return found


def payload_kernel(blocks, count, with_index, owner_ref, rows_ref, factor_ref, index_ref, out_ref):
    tiles, tile_rows, _ = rows_ref.shape
    capacity = factor_ref.shape[1] // count

    def window(block):
        return pl.ds(pl.multiple_of(group_of(owner_ref, block, count) * capacity, capacity), capacity)

    batch = min(4, tiles)
    for position, block in enumerate(blocks):
        factor = factor_ref[:, window(block)]

        def body(step, _, factor=factor, position=position):
            first = step * batch
            left = rows_ref[pl.ds(first, batch)].reshape(batch * tile_rows, -1)
            out_ref[pl.ds(first, batch), pl.ds(position * tile_rows, tile_rows), :] = contract(
                left, factor
            ).reshape(batch, tile_rows, capacity)
            return 0

        lax.fori_loop(0, tiles // batch, body, 0)
    if with_index:
        lists = [index_ref[:, window(block)] for block in range(count)]
        lists.append(jnp.full((INDEX_ROWS - count, capacity), -1, jnp.int32))
        table = jnp.concatenate(lists, axis=0).astype(jnp.float32)
        out_ref[:, pl.ds(len(blocks) * tile_rows, INDEX_ROWS), :] = jnp.broadcast_to(
            table[None], (tiles, INDEX_ROWS, capacity)
        )


def payload(blocks, with_index, owner, rows, factor, index, count):
    tiles, tile_rows, _ = rows.shape
    capacity = factor.shape[1] // count
    height = len(blocks) * tile_rows + (INDEX_ROWS if with_index else 0)
    return pl.pallas_call(
        functools.partial(payload_kernel, blocks, count, with_index),
        out_shape=jax.ShapeDtypeStruct((tiles, height, capacity), jnp.float32),
        in_specs=[pl.BlockSpec(memory_space=pltpu.SMEM), whole(), whole(), whole()],
        out_specs=whole(),
        compiler_params=PARAMS,
        cost_estimate=pl.CostEstimate(
            flops=2 * tiles * tile_rows * factor.shape[0] * capacity * len(blocks),
            bytes_accessed=4 * 1024 * 1024,
            transcendentals=0,
        ),
    )(owner, rows, factor, index)


def assemble_kernel(block, block_size, values_ref, index_ref, *outs):
    sources, tile_rows, capacity = values_ref.shape
    values = jnp.concatenate([values_ref[source] for source in range(sources)], axis=1)
    places = lax.broadcasted_iota(jnp.int32, (block_size, capacity), 0)
    spread = jnp.concatenate(
        [
            jnp.where(
                places == index_ref[source, pl.ds(block, 1), :].astype(jnp.int32), 1.0, 0.0
            ).astype(jnp.bfloat16)
            for source in range(sources)
        ],
        axis=1,
    )
    high = values.astype(jnp.bfloat16)
    low = (values - high.astype(jnp.float32)).astype(jnp.bfloat16)
    both = lax.dot_general(
        jnp.concatenate([high, low], axis=0),
        spread,
        (((1,), (1,)), ((), ())),
        preferred_element_type=jnp.float32,
    )
    total = both[:tile_rows] + both[tile_rows:]
    first = pl.program_id(0) == 0
    part_rows = tile_rows // len(outs)
    for part, out_ref in enumerate(outs):
        piece = total[part * part_rows : (part + 1) * part_rows]

        @pl.when(first)
        def _(out_ref=out_ref, piece=piece):
            out_ref[...] = piece

        @pl.when(jnp.logical_not(first))
        def _(out_ref=out_ref, piece=piece):
            out_ref[...] += piece


def assemble(block, position, arrived, index_holder, tile_rows, block_size, parts):
    tiles, _, capacity = arrived.shape
    index_place = index_holder.shape[1] // INDEX_ROWS - 1
    sources = min(SOURCES, tiles)
    part_rows = tile_rows // parts
    return pl.pallas_call(
        functools.partial(assemble_kernel, block, block_size),
        grid=(tiles // sources,),
        out_shape=[jax.ShapeDtypeStruct((part_rows, block_size), jnp.float32)] * parts,
        in_specs=[
            pl.BlockSpec((sources, tile_rows, capacity), lambda step: (step, position, 0)),
            pl.BlockSpec((sources, INDEX_ROWS, capacity), lambda step: (step, index_place, 0)),
        ],
        out_specs=[pl.BlockSpec((part_rows, block_size), lambda step: (0, 0))] * parts,
        compiler_params=PARAMS,
        cost_estimate=pl.CostEstimate(
            flops=4 * tiles * tile_rows * capacity * block_size,
            bytes_accessed=2 * 1024 * 1024,
            transcendentals=0,
        ),
    )(arrived, index_holder)


def station_kernel(station, terms, has_next, extra, held, *refs):
    refs = list(refs)
    right_ref = refs.pop(0)
    term_refs = [refs.pop(0) for _ in range(terms)]
    inverse_ref = refs.pop(0)
    if has_next:
        factor_ref = refs.pop(0)
        extra_refs = [refs.pop(0) for _ in range(extra)]
    held_refs = [refs.pop(0) for _ in range(held)]
    solved_ref = refs.pop(0)
    place = lax.axis_index("col")

    @pl.when(place == station)
    def _():
        reduced = right_ref[...]
        for term_ref in term_refs:
            reduced = reduced - term_ref[...]
        solved = contract(reduced.astype(jnp.bfloat16), inverse_ref[...])
        solved_ref[...] = solved
        if has_next:
            onward = contract(solved.astype(jnp.bfloat16), factor_ref[...])
            for extra_ref in extra_refs:
                onward = onward + extra_ref[...]
            refs[0][...] = onward

    for earlier, held_ref in enumerate(held_refs):

        @pl.when(place == earlier)
        def _(held_ref=held_ref):
            solved_ref[...] = held_ref[...]


def piece_spec(array, part, part_rows, width):
    if array.shape[0] == part_rows:
        return pl.BlockSpec((part_rows, width), lambda *_: (0, 0))
    return pl.BlockSpec((part_rows, width), lambda *_: (part, 0))


def station_step(station, part, parts, sep_rhs, terms, inverse, factor, extra, held):
    tile_rows, width = sep_rhs.shape
    part_rows = tile_rows // parts
    has_next = factor is not None
    rows = functools.partial(piece_spec, part=part, part_rows=part_rows, width=width)
    operands = [sep_rhs, *terms, inverse]
    specs = [rows(array) for array in (sep_rhs, *terms)]
    specs.append(pl.BlockSpec((inverse.shape[0], width), lambda *_: (0, 0)))
    if has_next:
        operands += [factor, *extra]
        specs.append(pl.BlockSpec((factor.shape[0], width), lambda *_: (0, station + 1)))
        specs += [rows(array) for array in extra]
    operands += held
    specs += [rows(array) for array in held]
    piece = jax.ShapeDtypeStruct((part_rows, width), jnp.float32)
    count = 2 if has_next else 1
    return pl.pallas_call(
        functools.partial(
            station_kernel, station, len(terms), has_next, len(extra), len(held)
        ),
        grid=(1,),
        out_shape=[piece] * count,
        in_specs=specs,
        out_specs=[pl.BlockSpec((part_rows, width), lambda *_: (0, 0))] * count,
        compiler_params=PARAMS,
        cost_estimate=pl.CostEstimate(
            flops=2 * count * part_rows * width * width,
            bytes_accessed=2 * count * width * width,
            transcendentals=0,
        ),
    )(*operands)


def onward_kernel(station, extra, solved_ref, factor_ref, *refs):
    @pl.when(lax.axis_index("col") == station)
    def _():
        onward = contract(solved_ref[...].astype(jnp.bfloat16), factor_ref[...])
        for extra_ref in refs[:extra]:
            onward = onward + extra_ref[...]
        refs[extra][...] = onward


def onward_step(station, block, part, parts, solved, factor, extra):
    part_rows, width = solved.shape
    rows = functools.partial(piece_spec, part=part, part_rows=part_rows, width=width)
    return pl.pallas_call(
        functools.partial(onward_kernel, station, len(extra)),
        grid=(1,),
        out_shape=jax.ShapeDtypeStruct((part_rows, width), jnp.float32),
        in_specs=[
            rows(solved),
            pl.BlockSpec((factor.shape[0], width), lambda *_: (0, block)),
            *[rows(array) for array in extra],
        ],
        out_specs=pl.BlockSpec((part_rows, width), lambda *_: (0, 0)),
        compiler_params=PARAMS,
        cost_estimate=pl.CostEstimate(
            flops=2 * part_rows * width * width,
            bytes_accessed=2 * width * width,
            transcendentals=0,
        ),
    )(solved, factor, *extra)


def exchange(value):
    return lax.all_to_all(value, "rhs", split_axis=0, concat_axis=0, tiled=True)


def moved(value, pairs):
    return lax.ppermute(value, "col", pairs)


def local(desc_rows, upd_factor, update_index, owner_map, sep_rhs, factor_rows, diag_inverse):
    count = lax.axis_size("col")
    tiles = lax.axis_size("rhs")
    block_size = diag_inverse.shape[0]
    tile_rows = sep_rhs.shape[0]
    parts = PARTS
    rows = desc_rows[0].reshape(tiles, tile_rows, block_size)
    make = functools.partial(
        payload, owner=owner_map, rows=rows, factor=upd_factor[0], index=update_index, count=count
    )
    first = exchange(make((0,), True))
    partial = {0: assemble(0, 0, first, first, tile_rows, block_size, parts)}
    for blocks in GROUPS:
        arrived = exchange(make(blocks, False))
        for position, block in enumerate(blocks):
            partial[block] = assemble(block, position, arrived, first, tile_rows, block_size, 1)

    gathered = {}
    for part in range(parts):
        stride, terms, value = 1, [partial[0][part]], partial[0][part]
        while stride < count:
            pairs = [(place + stride, place) for place in range(0, count - stride, 2 * stride)]
            received = moved(value, pairs)
            terms.append(received)
            stride *= 2
            if stride < count:
                value = value + received
        gathered[0, part] = terms
    for block in range(1, count):
        value = partial[block][0]
        received = None
        for source in range(count - 1, block, -1):
            sent = value if received is None else value + received
            received = moved(sent, [(source, source - 1)])
        for part in range(parts):
            gathered[block, part] = [value] + ([] if received is None else [received])

    held = {part: [] for part in range(parts)}
    for station in range(count):
        last = station + 1 == count
        for part in range(parts):
            outs = station_step(
                station, part, parts, sep_rhs, gathered[station, part], diag_inverse,
                None if last else factor_rows,
                [] if last else [partial[station + 1][0]],
                held[part] if last else [],
            )
            held[part].append(outs[0])
            if not last:
                gathered[station + 1, part].append(moved(outs[1], [(station, station + 1)]))
        for block in range(station + 2, count):
            for part in range(parts):
                onward = onward_step(
                    station, block, part, parts, held[part][station], factor_rows,
                    [partial[block][0]],
                )
                gathered[block, part].append(moved(onward, [(station, block)]))
    return jnp.concatenate([held[part][-1] for part in range(parts)], axis=0)


PARTS = 2
GROUPS = ((1,), (2, 3))


def solution(mesh):
    placed = (
        P(("col", "rhs"), None, None),
        P(("col", "rhs"), None, None),
        P(("col", "rhs"), None),
        P(("col", "rhs"), None),
        P("rhs", "col"),
        P("col", None),
        P("col", None),
    )
    return jax.shard_map(
        local, mesh=mesh, in_specs=placed, out_specs=P("rhs", "col"), check_vma=False
    )
```

time: 288 us -> 168 us (0.58)
  waiting for transfers between devices: 184 us -> 79.9 us
  other arithmetic: 54.1 us -> 1.78 us
  starting transfers between devices: 15.6 us -> 39.4 us
  Pallas kernels: 0 us -> 22 us
  matrix products: 8.8 us -> 0 us
    all_to_all x2 -> x3, waiting for transfers between devices: 91.3 us -> 22 us  [exchange(): return lax.all_to_all(value, 'rhs', split_axis=0, concat_axis=0, tiled=True)]
    scatter-add x1 -> x0, other arithmetic: 50.6 us -> none  [local(): jax.ops.segment_sum(arrived.reshape(-1, tile_rows), targets, num_segments...]
    ppermute x3 -> x19, waiting for transfers between devices: 92.9 us -> 57.9 us  [moved(): return lax.ppermute(value, 'col', pairs)]
    ppermute x3 -> x19, starting transfers between devices: 3.84 us -> 26.4 us  [moved(): return lax.ppermute(value, 'col', pairs)]
    pallas_call x0 -> x21, Pallas kernels: none -> 22 us  [the longest x4 10.6 us: assemble(): pl.pallas_call(functools.partial(assemble_kernel, block, block_size), gri...]
    unnamed x7 -> x38, local copies, waits for them, and re-layouts: 5.46 us -> 22.9 us
    dot_general x2 -> x0, matrix products: 8.8 us -> none  [the longest x1 5.79 us: local(): jnp.einsum('srn,ngc->gscr', desc_rows[0].reshape(rhs_count, tile_rows, bl...]
    slice x3 -> x0, local copies, waits for them, and re-layouts: 6.93 us -> none  [local(): carried = passed_along(carried[:, block_size:], 'col', 1)]
  transfers between devices with their start and end apart: 5 -> 22, of which waited for: 4 -> 8; matrix products, arithmetic and copies ran while one was open for 6% -> 1% of each run, Pallas kernels for 0% -> 12%
where the time goes in v1:
time: 168 us; the launch traced here: 167 us
  waiting for transfers between devices  79.9 us (48%)
  starting transfers between devices  39.4 us (23%)
  local copies, waits for them, and re-layouts  22.9 us (14%)
  Pallas kernels  22 us (13%)
  other arithmetic  1.78 us (1%)
    ppermute x19, waiting for transfers between devices, moved(): return lax.ppermute(value, 'col', pairs)  57.9 us
    ppermute x19, starting transfers between devices, moved(): return lax.ppermute(value, 'col', pairs)  26.4 us
    unnamed x38, local copies, waits for them, and re-layouts  22.9 us
    all_to_all x3, waiting for transfers between devices, exchange(): return lax.all_to_all(value, 'rhs', split_axis=0, concat_axis=0, tiled=True)  22 us
    all_to_all x3, starting transfers between devices, exchange(): return lax.all_to_all(value, 'rhs', split_axis=0, concat_axis=0, tiled=True)  13 us
    pallas_call x4, Pallas kernels, assemble(): pl.pallas_call(functools.partial(assemble_kernel, block, block_size), gri...  10.6 us
    pallas_call x3, Pallas kernels, payload(): pl.pallas_call(functools.partial(payload_kernel, blocks, count, with_inde...  5.47 us
    pallas_call x8, Pallas kernels, station_step(): pl.pallas_call(functools.partial(station_kernel, station, len(terms), has...  4.9 us
  transfers between devices with their start and end apart: 22, of which 8 were waited for; matrix products, arithmetic and copies ran while one was open for 1% of the time, Pallas kernels for 12%

profile of v1, /device:TPU:24, one launch (start us, length us, event | category | flops | bytes accessed | tf_op | source)
XLA Modules:
  0.0 166.5 jit_solution(7295996681437807168)
XLA Ops:
  0.0 1.6 copy-done.5
  1.6 1.6 copy-done.7
  3.2 0.7 copy-done.15
  3.9 0.7 copy-done.16
  4.5 1.5 shard_map.77
  6.0 1.0 copy-done.14
  7.0 4.4 %all-to-all-start.2 = ((f32[8,128,256]{2,1,0:T(8,128)}), f32[8,128,256]{2,1,0:T(8,128)}, u32[]{:S(2)}, u32[]{:S(2)}) async-start(f32[8,128,256]{2,1,0:T(8,128)} %copy-done.14), calls=%async_computation.2 | async-start | bytes 2097152 | tf_op jit(solution)/shard_map/all_to_all | solution.py:239
  11.4 1.6 copy-done.8
  13.0 1.5 shard_map.74
  14.5 1.0 copy-done.13
  15.6 11.3 %all-to-all-done.2.values_ref = f32[8,128,256]{2,1,0:T(8,128)} async-done(((f32[8,128,256]{2,1,0:T(8,128)}), f32[8,128,256]{2,1,0:T(8,128)}, u32[]{:S(2)}, u32[]{:S(2)}) %all-to-all-start.2) | async-done | bytes 1048608 | tf_op jit(solution)/shard_map/all_to_all | solution.py:239
  26.8 4.3 %all-to-all-start.1 = ((f32[8,136,256]{2,1,0:T(8,128)}), f32[8,136,256]{2,1,0:T(8,128)}, u32[]{:S(2)}, u32[]{:S(2)}) async-start(f32[8,136,256]{2,1,0:T(8,128)} %copy-done.13), calls=%async_computation.1 | async-start | bytes 2228224 | tf_op jit(solution)/shard_map/all_to_all | solution.py:239
  31.1 1.6 copy-done.9
  32.7 2.5 %shard_map.73 = f32[8,256,256]{2,1,0:T(8,128)S(1)} custom-call(s32[1,4]{1,0:T(1,128)S(1)} %copy-done.16, bf16[8,128,1024]{2,1,0:T(8,128)(2,1)S(1)} %bitcast.6, bf16[1024,1024]{1,0:T(8,128)(2,1)S(1)} %bitcast.9, s32[1,1024]{1,0:T(1,128)S(1)} %copy-done.15), custom_call_target="tpu_custom_call" | custom-call | flops 1073741824 | bytes 4194304 | tf_op jit(solution)/shard_map/pallas_call | solution.py:63
  35.2 1.3 copy-done.12
  36.5 10.7 %all-to-all-done.1.index_ref.values_ref = f32[8,136,256]{2,1,0:T(8,128)} async-done(((f32[8,136,256]{2,1,0:T(8,128)}), f32[8,136,256]{2,1,0:T(8,128)}, u32[]{:S(2)}, u32[]{:S(2)}) %all-to-all-start.1) | async-done | bytes 1114144 | tf_op jit(solution)/shard_map/all_to_all | solution.py:239
  47.2 4.4 %all-to-all-start = ((f32[8,256,256]{2,1,0:T(8,128)}), f32[8,256,256]{2,1,0:T(8,128)}, u32[]{:S(2)}, u32[]{:S(2)}) async-start(f32[8,256,256]{2,1,0:T(8,128)} %copy-done.12), calls=%async_computation | async-start | bytes 4194304 | tf_op jit(solution)/shard_map/all_to_all | solution.py:239
  51.6 2.7 %shard_map.78.refs_6_.refs_1_ = f32[128,1024]{1,0:T(8,128)S(1)} custom-call(f32[8,128,256]{2,1,0:T(8,128)} %all-to-all-done.2.values_ref, f32[8,136,256]{2,1,0:T(8,128)} %all-to-all-done.1.index_ref.values_ref), custom_call_target="tpu_custom_call" | custom-call | flops 1073741824 | bytes 2097152 | tf_op jit(solution)/shard_map/pallas_call | solution.py:118
  54.2 2.4 %collective-permute-start.3 = (f32[128,1024]{1,0:T(8,128)S(1)}, f32[128,1024]{1,0:T(8,128)S(1)}, u32[]{:S(2)}, u32[]{:S(2)}) collective-permute-start(f32[128,1024]{1,0:T(8,128)S(1)} %shard_map.78.refs_6_.refs_1_), channel_id=1, source_target_pairs={{24,16},{25,17},{26,18},{27,19},{28,20},{29,21},{30,22},{31,23}} | collective-permute-start | bytes 1572872 | tf_op jit(solution)/shard_map/ppermute | solution.py:243
  56.6 2.7 %shard_map.76 = (f32[64,1024]{1,0:T(8,128)S(1)}, f32[64,1024]{1,0:T(8,128)S(1)}) custom-call(f32[8,136,256]{2,1,0:T(8,128)} %all-to-all-done.1.index_ref.values_ref, f32[8,136,256]{2,1,0:T(8,128)} %all-to-all-done.1.index_ref.values_ref), custom_call_target="tpu_custom_call" | custom-call | flops 1073741824 | bytes 2097152 | tf_op jit(solution)/shard_map/pallas_call | solution.py:118
  59.4 1.4 collective-permute-start.11
  60.8 1.3 collective-permute-start
  62.1 12.4 %collective-permute-done.11.refs_2_ = f32[64,1024]{1,0:T(8,128)S(1)} collective-permute-done((f32[64,1024]{1,0:T(8,128)S(1)}, f32[64,1024]{1,0:T(8,128)S(1)}, u32[]{:S(2)}, u32[]{:S(2)}) %collective-permute-start.11) | collective-permute-done | bytes 262176 | tf_op jit(solution)/shard_map/ppermute | solution.py:243
  74.5 0.7 collective-permute-start.12
  75.2 4.3 %collective-permute-done.refs_2_ = f32[64,1024]{1,0:T(8,128)S(1)} collective-permute-done((f32[64,1024]{1,0:T(8,128)S(1)}, f32[64,1024]{1,0:T(8,128)S(1)}, u32[]{:S(2)}, u32[]{:S(2)}) %collective-permute-start) | collective-permute-done | bytes 262176 | tf_op jit(solution)/shard_map/ppermute | solution.py:243
  79.6 0.7 collective-permute-start.1
  80.3 0.9 add.10
  81.1 1.5 collective-permute-start.4
  82.6 3.4 %copy-done = bf16[1024,4096]{1,0:T(8,128)(2,1)S(1)} copy-done((bf16[1024,4096]{1,0:T(8,128)(2,1)S(1)}, bf16[1024,4096]{1,0:T(8,128)(2,1)}, u32[]{:S(2)}) %copy-start) | copy-done | bytes 8388632
  86.0 0.8 shard_map.87
  86.8 0.7 collective-permute-start.14
  87.5 3.4 %copy-done.1 = bf16[1024,4096]{1,0:T(8,128)(2,1)S(1)} copy-done((bf16[1024,4096]{1,0:T(8,128)(2,1)S(1)}, bf16[1024,4096]{1,0:T(8,128)(2,1)}, u32[]{:S(2)}) %copy-start.1) | copy-done | bytes 8388632
  90.9 0.8 shard_map.79
  91.7 1.4 collective-permute-start.5
  93.1 2.6 %shard_map.81.refs_6_.refs_0_.refs_1_ = f32[128,1024]{1,0:T(8,128)S(1)} custom-call(f32[8,256,256]{2,1,0:T(8,128)} %all-to-all-done.values_ref, f32[8,136,256]{2,1,0:T(8,128)} %all-to-all-done.1.index_ref.values_ref), custom_call_target="tpu_custom_call" | custom-call | flops 1073741824 | bytes 2097152 | tf_op jit(solution)/shard_map/pallas_call | solution.py:118
  95.8 5.7 %collective-permute-start.7 = (f32[128,1024]{1,0:T(8,128)S(1)}, f32[128,1024]{1,0:T(8,128)S(1)}, u32[]{:S(2)}, u32[]{:S(2)}) collective-permute-start(f32[128,1024]{1,0:T(8,128)S(1)} %shard_map.81.refs_6_.refs_0_.refs_1_), channel_id=1, source_target_pairs={{24,16},{25,17},{26,18},{27,19},{28,20},{29,21},{30,22},{31,23}} | collective-permute-start | bytes 1572872 | tf_op jit(solution)/shard_map/ppermute | solution.py:243
  101.5 3.4 %copy-done.2 = bf16[1024,4096]{1,0:T(8,128)(2,1)S(1)} copy-done((bf16[1024,4096]{1,0:T(8,128)(2,1)S(1)}, bf16[1024,4096]{1,0:T(8,128)(2,1)}, u32[]{:S(2)}) %copy-start.2) | copy-done | bytes 8388632
  105.0 0.8 collective-permute-start.16
  105.8 0.1 shard_map.84
  106.0 0.8 collective-permute-start.8
  106.8 0.2 slice-done
  107.1 1.3 slice-done.1
  108.4 0.2 copy-done.11
  108.6 1.0 shard_map.89
  109.5 0.7 collective-permute-start.17
  110.2 1.0 shard_map.82
  111.3 0.7 collective-permute-start.9
  111.9 2.7 %shard_map.75.refs_0_.refs_7_.refs_1_ = f32[128,1024]{1,0:T(8,128)S(1)} custom-call(f32[8,256,256]{2,1,0:T(8,128)} %all-to-all-done.values_ref, f32[8,136,256]{2,1,0:T(8,128)} %all-to-all-done.1.index_ref.values_ref), custom_call_target="tpu_custom_call" | custom-call | flops 1073741824 | bytes 2097152 | tf_op jit(solution)/shard_map/pallas_call | solution.py:118
  114.8 1.3 collective-permute-start.13
  116.3 0.3 shard_map.83
  116.7 1.3 collective-permute-start.2
  118.0 1.3 collective-permute-start.15
  119.3 0.1 shard_map.92
  119.4 1.3 collective-permute-start.6
  120.8 1.3 collective-permute-start.18
  122.1 0.1 shard_map.85
  122.2 5.5 %collective-permute-done.13.refs_2_ = f32[64,1024]{1,0:T(8,128)S(1)} collective-permute-done((f32[64,1024]{1,0:T(8,128)S(1)}, f32[64,1024]{1,0:T(8,128)S(1)}, u32[]{:S(2)}, u32[]{:S(2)}) %collective-permute-start.13) | collective-permute-done | bytes 262176 | tf_op jit(solution)/shard_map/ppermute | solution.py:243
  127.7 1.3 collective-permute-start.10
  129.0 19.5 %collective-permute-done.15.refs_3_ = f32[64,1024]{1,0:T(8,128)S(1)} collective-permute-done((f32[64,1024]{1,0:T(8,128)S(1)}, f32[64,1024]{1,0:T(8,128)S(1)}, u32[]{:S(2)}, u32[]{:S(2)}) %collective-permute-start.15) | collective-permute-done | bytes 262176 | tf_op jit(solution)/shard_map/ppermute | solution.py:243
  148.5 11.1 %collective-permute-done.18.refs_4_ = f32[64,1024]{1,0:T(8,128)S(1)} collective-permute-done((f32[64,1024]{1,0:T(8,128)S(1)}, f32[64,1024]{1,0:T(8,128)S(1)}, u32[]{:S(2)}, u32[]{:S(2)}) %collective-permute-start.18) | collective-permute-done | bytes 262176 | tf_op jit(solution)/shard_map/ppermute | solution.py:243
  159.6 0.5 shard_map.93
  160.2 5.0 %collective-permute-done.10.refs_4_ = f32[64,1024]{1,0:T(8,128)S(1)} collective-permute-done((f32[64,1024]{1,0:T(8,128)S(1)}, f32[64,1024]{1,0:T(8,128)S(1)}, u32[]{:S(2)}, u32[]{:S(2)}) %collective-permute-start.10) | collective-permute-done | bytes 262176 | tf_op jit(solution)/shard_map/ppermute | solution.py:243
  165.2 0.5 shard_map.86
  165.7 0.8 pad_maximum_fusion
  (44 shorter events, 0.7 us)
Async XLA Ops:
  0.0 1.6 copy-start.5
  1.6 1.6 copy-start.7
  3.2 0.7 copy-start.15
  3.9 0.7 copy-start.16
  6.0 1.0 copy-start.14
  7.0 4.4 %copy-start.6 = (bf16[1,1024,1024]{2,1,0:T(8,128)(2,1)S(1)}, bf16[1,1024,1024]{2,1,0:T(8,128)(2,1)}, u32[]{:S(2)}) copy-start(bf16[1,1024,1024]{2,1,0:T(8,128)(2,1)} %param.7) | copy-start | bytes 6291460
  7.0 19.8 %all-to-all-start.2 = ((f32[8,128,256]{2,1,0:T(8,128)}), f32[8,128,256]{2,1,0:T(8,128)}, u32[]{:S(2)}, u32[]{:S(2)}) async-start(f32[8,128,256]{2,1,0:T(8,128)} %copy-done.14), calls=%async_computation.2 | async-start | bytes 2097152 | tf_op jit(solution)/shard_map/all_to_all | solution.py:239
  11.4 1.6 copy-start.8
  14.5 1.0 copy-start.13
  26.8 20.4 %all-to-all-start.1 = ((f32[8,136,256]{2,1,0:T(8,128)}), f32[8,136,256]{2,1,0:T(8,128)}, u32[]{:S(2)}, u32[]{:S(2)}) async-start(f32[8,136,256]{2,1,0:T(8,128)} %copy-done.13), calls=%async_computation.1 | async-start | bytes 2228224 | tf_op jit(solution)/shard_map/all_to_all | solution.py:239
  31.1 1.6 copy-start.9
  35.1 1.3 copy-start.12
  47.2 45.9 %all-to-all-start = ((f32[8,256,256]{2,1,0:T(8,128)}), f32[8,256,256]{2,1,0:T(8,128)}, u32[]{:S(2)}, u32[]{:S(2)}) async-start(f32[8,256,256]{2,1,0:T(8,128)} %copy-done.12), calls=%async_computation | async-start | bytes 4194304 | tf_op jit(solution)/shard_map/all_to_all | solution.py:239
  54.2 33.3 %copy-start.10 = (f32[128,1024]{1,0:T(8,128)}, f32[128,1024]{1,0:T(8,128)S(1)}, u32[]{:S(2)}) copy-start(f32[128,1024]{1,0:T(8,128)S(1)} %shard_map.78.refs_6_.refs_1_) | copy-start | bytes 1572868
  54.2 26.0 %collective-permute-start.3 = (f32[128,1024]{1,0:T(8,128)S(1)}, f32[128,1024]{1,0:T(8,128)S(1)}, u32[]{:S(2)}, u32[]{:S(2)}) collective-permute-start(f32[128,1024]{1,0:T(8,128)S(1)} %shard_map.78.refs_6_.refs_1_), channel_id=1, source_target_pairs={{24,16},{25,17},{26,18},{27,19},{28,20},{29,21},{30,22},{31,23}} | collective-permute-start | bytes 1572872 | tf_op jit(solution)/shard_map/ppermute | solution.py:243
  59.3 23.3 %copy-start.3 = (bf16[1024,1024]{1,0:T(8,128)(2,1)S(1)}, bf16[1024,1024]{1,0:T(8,128)(2,1)}, u32[]{:S(2)}) copy-start(bf16[1024,1024]{1,0:T(8,128)(2,1)} %refs_5_.15) | copy-start | bytes 6291460
  59.3 23.3 %copy-start.4 = (f32[128,1024]{1,0:T(8,128)S(1)}, f32[128,1024]{1,0:T(8,128)}, u32[]{:S(2)}) copy-start(f32[128,1024]{1,0:T(8,128)} %refs_0_.15) | copy-start | bytes 1572868
  59.4 15.1 %collective-permute-start.11 = (f32[64,1024]{1,0:T(8,128)S(1)}, f32[64,1024]{1,0:T(8,128)S(1)}, u32[]{:S(2)}, u32[]{:S(2)}) collective-permute-start(f32[64,1024]{1,0:T(8,128)S(1)} %get-tuple-element.26.refs_1_), channel_id=1, source_target_pairs={{8,0},{24,16},{9,1},{25,17},{10,2},{26,18},{11,3},{27,19},{12,4},{... | collective-permute-start | bytes 786440 | tf_op jit(solution)/shard_map/ppermute | solution.py:243
  60.8 18.7 %collective-permute-start = (f32[64,1024]{1,0:T(8,128)S(1)}, f32[64,1024]{1,0:T(8,128)S(1)}, u32[]{:S(2)}, u32[]{:S(2)}) collective-permute-start(f32[64,1024]{1,0:T(8,128)S(1)} %get-tuple-element.19.refs_1_), channel_id=1, source_target_pairs={{8,0},{24,16},{9,1},{25,17},{10,2},{26,18},{11,3},{27,19},{12,4},{... | collective-permute-start | bytes 786440 | tf_op jit(solution)/shard_map/ppermute | solution.py:243
  74.5 8.1 %collective-permute-start.12 = (f32[64,1024]{1,0:T(8,128)S(1)}, f32[64,1024]{1,0:T(8,128)S(1)}, u32[]{:S(2)}, u32[]{:S(2)}) collective-permute-start(f32[64,1024]{1,0:T(8,128)S(1)} %add.11), channel_id=1, source_target_pairs={{16,0},{17,1},{18,2},{19,3},{20,4},{21,5},{22,6},{23,7}} | collective-permute-start | bytes 786440 | tf_op jit(solution)/shard_map/ppermute | solution.py:243
  79.6 7.9 %collective-permute-start.1 = (f32[64,1024]{1,0:T(8,128)S(1)}, f32[64,1024]{1,0:T(8,128)S(1)}, u32[]{:S(2)}, u32[]{:S(2)}) collective-permute-start(f32[64,1024]{1,0:T(8,128)S(1)} %add.9), channel_id=1, source_target_pairs={{16,0},{17,1},{18,2},{19,3},{20,4},{21,5},{22,6},{23,7}} | collective-permute-start | bytes 786440 | tf_op jit(solution)/shard_map/ppermute | solution.py:243
  81.1 25.7 %collective-permute-start.4 = (f32[128,1024]{1,0:T(8,128)}, f32[128,1024]{1,0:T(8,128)}, u32[]{:S(2)}, u32[]{:S(2)}) collective-permute-start(f32[128,1024]{1,0:T(8,128)} %add.10), channel_id=1, source_target_pairs={{16,8},{17,9},{18,10},{19,11},{20,12},{21,13},{22,14},{23,15}} | collective-permute-start | bytes 1572872 | tf_op jit(solution)/shard_map/ppermute | solution.py:243
  82.6 3.4 %copy-start = (bf16[1024,4096]{1,0:T(8,128)(2,1)S(1)}, bf16[1024,4096]{1,0:T(8,128)(2,1)}, u32[]{:S(2)}) copy-start(bf16[1024,4096]{1,0:T(8,128)(2,1)} %refs_6_.3) | copy-start | bytes 25165828
  86.8 19.2 %collective-permute-start.14 = (f32[64,1024]{1,0:T(8,128)}, f32[64,1024]{1,0:T(8,128)S(1)}, u32[]{:S(2)}, u32[]{:S(2)}) collective-permute-start(f32[64,1024]{1,0:T(8,128)} %get-tuple-element.28), channel_id=1, source_target_pairs={{0,8},{1,9},{2,10},{3,11},{4,12},{5,13},{6,14},{7,15}} | collective-permute-start | bytes 786440 | tf_op jit(solution)/shard_map/ppermute | solution.py:243
  87.5 3.4 %copy-start.1 = (bf16[1024,4096]{1,0:T(8,128)(2,1)S(1)}, bf16[1024,4096]{1,0:T(8,128)(2,1)}, u32[]{:S(2)}) copy-start(bf16[1024,4096]{1,0:T(8,128)(2,1)} %refs_6_.3) | copy-start | bytes 25165828
  91.7 18.5 %collective-permute-start.5 = (f32[64,1024]{1,0:T(8,128)}, f32[64,1024]{1,0:T(8,128)}, u32[]{:S(2)}, u32[]{:S(2)}) collective-permute-start(f32[64,1024]{1,0:T(8,128)} %get-tuple-element.21), channel_id=1, source_target_pairs={{0,8},{1,9},{2,10},{3,11},{4,12},{5,13},{6,14},{7,15}} | collective-permute-start | bytes 786440 | tf_op jit(solution)/shard_map/ppermute | solution.py:243
  95.8 22.2 %collective-permute-start.7 = (f32[128,1024]{1,0:T(8,128)S(1)}, f32[128,1024]{1,0:T(8,128)S(1)}, u32[]{:S(2)}, u32[]{:S(2)}) collective-permute-start(f32[128,1024]{1,0:T(8,128)S(1)} %shard_map.81.refs_6_.refs_0_.refs_1_), channel_id=1, source_target_pairs={{24,16},{25,17},{26,18},{27,19},{28,20},{29,21},{30,22},{31,23}} | collective-permute-start | bytes 1572872 | tf_op jit(solution)/shard_map/ppermute | solution.py:243
  101.5 3.4 %copy-start.2 = (bf16[1024,4096]{1,0:T(8,128)(2,1)S(1)}, bf16[1024,4096]{1,0:T(8,128)(2,1)}, u32[]{:S(2)}) copy-start(bf16[1024,4096]{1,0:T(8,128)(2,1)} %refs_6_.3) | copy-start | bytes 25165828
  104.9 2.2 %slice-start = ((s8[8388608]{0:T(1024)(128)(4,1)}), s8[4194304]{0:T(1024)(128)(4,1)S(1)}, s32[]{:S(2)}) async-start(s8[8388608]{0:T(1024)(128)(4,1)} %bitcast.2), calls=%async_computation.3 | async-start | bytes 8388608
  105.0 3.4 %slice-start.1 = ((s8[8388608]{0:T(1024)(128)(4,1)}), s8[4194304]{0:T(1024)(128)(4,1)S(1)}, s32[]{:S(2)}) async-start(s8[8388608]{0:T(1024)(128)(4,1)} %bitcast.2), calls=%async_computation.4 | async-start | bytes 8388608
  105.0 9.7 %collective-permute-start.16 = (f32[64,1024]{1,0:T(8,128)S(1)}, f32[64,1024]{1,0:T(8,128)S(1)}, u32[]{:S(2)}, u32[]{:S(2)}) collective-permute-start(f32[64,1024]{1,0:T(8,128)S(1)} %shard_map.91), channel_id=1, source_target_pairs={{0,16},{1,17},{2,18},{3,19},{4,20},{5,21},{6,22},{7,23}} | collective-permute-start | bytes 786440 | tf_op jit(solution)/shard_map/ppermute | solution.py:243
  105.8 2.7 %copy-start.11 = (f32[128,1024]{1,0:T(8,128)S(1)}, f32[128,1024]{1,0:T(8,128)}, u32[]{:S(2)}) copy-start(f32[128,1024]{1,0:T(8,128)} %copy-done.10) | copy-start | bytes 1572868
  106.0 13.4 %collective-permute-start.8 = (f32[64,1024]{1,0:T(8,128)S(1)}, f32[64,1024]{1,0:T(8,128)S(1)}, u32[]{:S(2)}, u32[]{:S(2)}) collective-permute-start(f32[64,1024]{1,0:T(8,128)S(1)} %shard_map.84), channel_id=1, source_target_pairs={{0,16},{1,17},{2,18},{3,19},{4,20},{5,21},{6,22},{7,23}} | collective-permute-start | bytes 786440 | tf_op jit(solution)/shard_map/ppermute | solution.py:243
  109.5 7.1 %collective-permute-start.17 = (f32[64,1024]{1,0:T(8,128)S(1)}, f32[64,1024]{1,0:T(8,128)S(1)}, u32[]{:S(2)}, u32[]{:S(2)}) collective-permute-start(f32[64,1024]{1,0:T(8,128)S(1)} %get-tuple-element.30), channel_id=1, source_target_pairs={{8,16},{9,17},{10,18},{11,19},{12,20},{13,21},{14,22},{15,23}} | collective-permute-start | bytes 786440 | tf_op jit(solution)/shard_map/ppermute | solution.py:243
  111.3 9.5 %collective-permute-start.9 = (f32[64,1024]{1,0:T(8,128)S(1)}, f32[64,1024]{1,0:T(8,128)S(1)}, u32[]{:S(2)}, u32[]{:S(2)}) collective-permute-start(f32[64,1024]{1,0:T(8,128)S(1)} %get-tuple-element.23), channel_id=1, source_target_pairs={{8,16},{9,17},{10,18},{11,19},{12,20},{13,21},{14,22},{15,23}} | collective-permute-start | bytes 786440 | tf_op jit(solution)/shard_map/ppermute | solution.py:243
  114.8 13.0 %collective-permute-start.13 = (f32[64,1024]{1,0:T(8,128)S(1)}, f32[64,1024]{1,0:T(8,128)S(1)}, u32[]{:S(2)}, u32[]{:S(2)}) collective-permute-start(f32[64,1024]{1,0:T(8,128)S(1)} %shard_map.88), channel_id=1, source_target_pairs={{0,24},{1,25},{2,26},{3,27},{4,28},{5,29},{6,30},{7,31}} | collective-permute-start | bytes 786440 | tf_op jit(solution)/shard_map/ppermute | solution.py:243
  116.7 43.5 %collective-permute-start.2 = (f32[64,1024]{1,0:T(8,128)S(1)}, f32[64,1024]{1,0:T(8,128)S(1)}, u32[]{:S(2)}, u32[]{:S(2)}) collective-permute-start(f32[64,1024]{1,0:T(8,128)S(1)} %shard_map.80), channel_id=1, source_target_pairs={{0,24},{1,25},{2,26},{3,27},{4,28},{5,29},{6,30},{7,31}} | collective-permute-start | bytes 786440 | tf_op jit(solution)/shard_map/ppermute | solution.py:243
  118.0 30.5 %collective-permute-start.15 = (f32[64,1024]{1,0:T(8,128)S(1)}, f32[64,1024]{1,0:T(8,128)S(1)}, u32[]{:S(2)}, u32[]{:S(2)}) collective-permute-start(f32[64,1024]{1,0:T(8,128)S(1)} %shard_map.90), channel_id=1, source_target_pairs={{8,24},{9,25},{10,26},{11,27},{12,28},{13,29},{14,30},{15,31}} | collective-permute-start | bytes 786440 | tf_op jit(solution)/shard_map/ppermute | solution.py:243
  119.4 40.7 %collective-permute-start.6 = (f32[64,1024]{1,0:T(8,128)S(1)}, f32[64,1024]{1,0:T(8,128)S(1)}, u32[]{:S(2)}, u32[]{:S(2)}) collective-permute-start(f32[64,1024]{1,0:T(8,128)S(1)} %shard_map.83), channel_id=1, source_target_pairs={{8,24},{9,25},{10,26},{11,27},{12,28},{13,29},{14,30},{15,31}} | collective-permute-start | bytes 786440 | tf_op jit(solution)/shard_map/ppermute | solution.py:243
  120.8 38.9 %collective-permute-start.18 = (f32[64,1024]{1,0:T(8,128)S(1)}, f32[64,1024]{1,0:T(8,128)S(1)}, u32[]{:S(2)}, u32[]{:S(2)}) collective-permute-start(f32[64,1024]{1,0:T(8,128)S(1)} %get-tuple-element.31), channel_id=1, source_target_pairs={{16,24},{17,25},{18,26},{19,27},{20,28},{21,29},{22,30},{23,31}} | collective-permute-start | bytes 786440 | tf_op jit(solution)/shard_map/ppermute | solution.py:243
  127.7 37.5 %collective-permute-start.10 = (f32[64,1024]{1,0:T(8,128)S(1)}, f32[64,1024]{1,0:T(8,128)S(1)}, u32[]{:S(2)}, u32[]{:S(2)}) collective-permute-start(f32[64,1024]{1,0:T(8,128)S(1)} %get-tuple-element.24), channel_id=1, source_target_pairs={{16,24},{17,25},{18,26},{19,27},{20,28},{21,29},{22,30},{23,31}} | collective-permute-start | bytes 786440 | tf_op jit(solution)/shard_map/ppermute | solution.py:243

commit v2 on v0

v2 whole, which is shorter than its diff:
```python
import functools

import jax
import jax.numpy as jnp
from jax import lax
from jax.experimental import pallas as pl
from jax.experimental.pallas import tpu as pltpu
from jax.sharding import PartitionSpec as P

MIB = 1024 * 1024
CORES = 2
INDEX_ROWS = 8
SOURCES = 4
PARTS = 1


def params(mib):
    return pltpu.CompilerParams(vmem_limit_bytes=mib * MIB)


def cost(flops, bytes_accessed):
    return pl.CostEstimate(flops=0, bytes_accessed=0, transcendentals=0)


def in_vmem():
    return pl.BlockSpec(memory_space=pltpu.VMEM)


def in_hbm():
    return pl.BlockSpec(memory_space=pltpu.HBM)


def after(values, earlier):
    values, earlier = tuple(values), tuple(earlier)
    return lax.optimization_barrier(values + earlier)[: len(values)]


def contract(left, right):
    return jnp.dot(left, right, preferred_element_type=jnp.float32)


def group_of(owner_ref, block, count):
    found = jnp.int32(0)
    for place in range(count):
        found = found + jnp.where(owner_ref[0, place] == block, place, 0)
    return found


def payload_kernel(blocks, count, with_index, owner_ref, rows_ref, factor_ref, index_ref, *outs):
    tiles, tile_rows, _ = rows_ref.shape
    chips = tiles // CORES
    capacity = factor_ref.shape[1] // count
    own = lax.axis_index("rhs")
    chip, core = lax.div(own, CORES), lax.rem(own, CORES)

    def window(block):
        return pl.ds(pl.multiple_of(group_of(owner_ref, block, count) * capacity, capacity), capacity)

    for position, block in enumerate(blocks):
        factor = factor_ref[:, window(block)]
        for offset in range(chips):
            target = jnp.bitwise_xor(chip, offset) * CORES
            left = jnp.concatenate(
                [rows_ref[target + core], rows_ref[target + (CORES - 1) - core]], axis=0
            )
            outs[position * chips + offset][: CORES * tile_rows, :] = contract(left, factor)
    if with_index:
        lists = [index_ref[:, window(block)] for block in range(count)]
        lists.append(jnp.full((INDEX_ROWS - count, capacity), -1, jnp.int32))
        table = jnp.concatenate(lists, axis=0).astype(jnp.float32)
        for out_ref in outs:
            out_ref[CORES * tile_rows :, :] = table


def payload(blocks, with_index, owner, rows, factor, index, count):
    tiles, tile_rows, depth = rows.shape
    chips = tiles // CORES
    capacity = factor.shape[1] // count
    height = CORES * tile_rows + (INDEX_ROWS if with_index else 0)
    piece = jax.ShapeDtypeStruct((height, capacity), jnp.float32)
    outs = pl.pallas_call(
        functools.partial(payload_kernel, blocks, count, with_index),
        out_shape=[piece] * (chips * len(blocks)),
        in_specs=[pl.BlockSpec(memory_space=pltpu.SMEM), in_vmem(), in_vmem(), in_vmem()],
        out_specs=[in_vmem()] * (chips * len(blocks)),
        compiler_params=params(32),
        cost_estimate=cost(2 * tiles * tile_rows * depth * capacity * len(blocks), 4 * MIB),
    )(owner, rows, factor, index)
    return [outs[position * chips : (position + 1) * chips] for position in range(len(blocks))]


def assemble_kernel(block, block_size, tile_rows, chips, *refs):
    values_refs, index_refs, outs = refs[:chips], refs[chips : 2 * chips], refs[2 * chips :]
    capacity = values_refs[0].shape[1]
    height = CORES * tile_rows
    places = lax.broadcasted_iota(jnp.int32, (block_size, capacity), 0)
    total = None
    for first in range(0, chips, SOURCES):
        chosen = range(first, min(chips, first + SOURCES))
        values = jnp.concatenate([values_refs[chip][:height, :] for chip in chosen], axis=1)
        spread = jnp.concatenate(
            [
                jnp.where(
                    places
                    == index_refs[chip][pl.ds(height + block, 1), :].astype(jnp.int32),
                    1.0,
                    0.0,
                ).astype(jnp.bfloat16)
                for chip in chosen
            ],
            axis=1,
        )
        high = values.astype(jnp.bfloat16)
        low = (values - high.astype(jnp.float32)).astype(jnp.bfloat16)
        both = lax.dot_general(
            jnp.concatenate([high, low], axis=0),
            spread,
            (((1,), (1,)), ((), ())),
            preferred_element_type=jnp.float32,
        )
        both = both[:height] + both[height:]
        total = both if total is None else total + both
    outs[0][...] = total[:tile_rows]
    outs[1][...] = total[tile_rows:]


def assemble(block, arrived, holders, tile_rows, block_size):
    chips = len(arrived)
    capacity = arrived[0].shape[1]
    piece = jax.ShapeDtypeStruct((tile_rows, block_size), jnp.float32)
    return pl.pallas_call(
        functools.partial(assemble_kernel, block, block_size, tile_rows, chips),
        out_shape=[piece] * CORES,
        in_specs=[in_vmem()] * (2 * chips),
        out_specs=[in_vmem()] * CORES,
        compiler_params=params(24),
        cost_estimate=cost(4 * CORES * chips * tile_rows * capacity * block_size, 2 * MIB),
    )(*arrived, *holders)


def stage_kernel(factor_ref, inverse_ref, *refs):
    outs, semaphores = refs[:-1], refs[-1]
    width = inverse_ref.shape[1]
    sources = [inverse_ref] + [
        factor_ref.at[:, pl.ds(block * width, width)] for block in range(1, len(outs))
    ]
    copies = [
        pltpu.make_async_copy(source, out, semaphores.at[place])
        for place, (source, out) in enumerate(zip(sources, outs))
    ]
    for copy in copies:
        copy.start()
    for copy in copies:
        copy.wait()


def stage(factor, inverse, count):
    depth, width = inverse.shape
    piece = jax.ShapeDtypeStruct((depth, width), inverse.dtype)
    return pl.pallas_call(
        stage_kernel,
        out_shape=[piece] * count,
        in_specs=[in_hbm()] * 2,
        out_specs=[in_vmem()] * count,
        scratch_shapes=[pltpu.SemaphoreType.DMA((count,))],
        compiler_params=params(16),
        cost_estimate=cost(0, 16 * MIB),
    )(factor, inverse)


def rows_of(ref, part, part_rows):
    if ref.shape[0] == part_rows:
        return ref[...]
    return ref[pl.ds(part * part_rows, part_rows), :]


def station_kernel(station, part, terms, has_next, extra, held, right_ref, inverse_ref, *refs):
    refs = list(refs)
    term_refs = [refs.pop(0) for _ in range(terms)]
    factor_ref = refs.pop(0) if has_next else None
    extra_refs = [refs.pop(0) for _ in range(extra)]
    held_refs = [refs.pop(0) for _ in range(held)]
    solved_ref = refs.pop(0)
    part_rows = solved_ref.shape[0]
    place = lax.axis_index("col")

    @pl.when(place == station)
    def _():
        reduced = rows_of(right_ref, part, part_rows)
        for term_ref in term_refs:
            reduced = reduced - rows_of(term_ref, part, part_rows)
        solved = contract(reduced.astype(jnp.bfloat16), inverse_ref[...])
        solved_ref[...] = solved
        if has_next:
            onward = contract(solved.astype(jnp.bfloat16), factor_ref[...])
            for extra_ref in extra_refs:
                onward = onward + rows_of(extra_ref, part, part_rows)
            refs[0][...] = onward

    for earlier, held_ref in enumerate(held_refs):

        @pl.when(place == earlier)
        def _(held_ref=held_ref):
            solved_ref[...] = held_ref[...]


def station_step(station, part, right, inverse, terms, factor, extra, held):
    part_rows, width = right.shape[0] // PARTS, right.shape[1]
    operands = [right, inverse, *terms, *([] if factor is None else [factor]), *extra, *held]
    piece = jax.ShapeDtypeStruct((part_rows, width), jnp.float32)
    count = 1 if factor is None else 2
    return pl.pallas_call(
        functools.partial(
            station_kernel, station, part, len(terms), factor is not None, len(extra), len(held)
        ),
        out_shape=[piece] * count,
        in_specs=[in_vmem()] * len(operands),
        out_specs=[in_vmem()] * count,
        compiler_params=params(16),
        cost_estimate=cost(2 * count * part_rows * width * width, 2 * MIB),
    )(*operands)


def onward_kernel(station, part, solved_ref, factor_ref, *refs):
    @pl.when(lax.axis_index("col") == station)
    def _():
        onward = contract(solved_ref[...].astype(jnp.bfloat16), factor_ref[...])
        for extra_ref in refs[:-1]:
            onward = onward + rows_of(extra_ref, part, onward.shape[0])
        refs[-1][...] = onward


def onward_step(station, part, solved, factor, extra):
    part_rows, width = solved.shape
    return pl.pallas_call(
        functools.partial(onward_kernel, station, part),
        out_shape=jax.ShapeDtypeStruct((part_rows, width), jnp.float32),
        in_specs=[in_vmem()] * (2 + len(extra)),
        out_specs=in_vmem(),
        compiler_params=params(16),
        cost_estimate=cost(2 * part_rows * width * width, 2 * MIB),
    )(solved, factor, *extra)


def local(desc_rows, upd_factor, update_index, owner_map, sep_rhs, factor_rows, diag_inverse):
    count = lax.axis_size("col")
    tiles = lax.axis_size("rhs")
    chips = tiles // CORES
    block_size = diag_inverse.shape[0]
    tile_rows = sep_rhs.shape[0]
    part_rows = tile_rows // PARTS
    parts = range(PARTS)

    def across(value, offset):
        pairs = [(place, place ^ (offset * CORES)) for place in range(tiles)]
        return lax.ppermute(value, "rhs", pairs)

    def other_core(value):
        return lax.ppermute(value, "rhs", [(place, place ^ 1) for place in range(tiles)])

    def moved(value, pairs):
        return lax.ppermute(value, "col", pairs)

    token = []

    def ordered(values):
        return list(after(values, token)) if token else list(values)

    def done_with(value):
        token[:] = [value]

    rows = desc_rows[0].reshape(tiles, tile_rows, block_size)
    make = functools.partial(
        payload, owner=owner_map, factor=upd_factor[0], index=update_index, count=count
    )
    first_payload = make((0,), True, rows=rows)[0]
    done_with(first_payload[0])
    rest = make(tuple(range(1, count)), False, rows=ordered([rows])[0])
    payloads = [first_payload, *rest]
    done_with(rest[0][0])
    weights = stage(*ordered([factor_rows, diag_inverse]), count)
    inverse, couplings = weights[0], weights[1:]
    done_with(inverse)

    arriving = {}

    def send_block(block, gates):
        sent = payloads[block]
        pieces = [sent[0]]
        for offset in range(1, chips):
            value = sent[offset]
            if gates is not None:
                value = after([value], [gates[offset]])[0]
            pieces.append(across(value, offset))
        arriving[block] = pieces

    partial = {}
    terms = {block: [[] for _ in parts] for block in range(count)}

    crossing = {}

    def assemble_block(block):
        values = ordered(arriving[block])
        mine, other = assemble(block, values, arriving[0], tile_rows, block_size)
        done_with(mine)
        if block + 1 < count:
            gate = other if block == 0 else terms[0][-1][min(block, len(terms[0][-1]) - 1)]
            send_block(block + 1, [gate] * chips)
        crossing[block] = (mine, other_core(other))

    def close_block(block):
        partial[block] = []
        for part in parts:
            mine, received = ordered(crossing[block])
            window = slice(part * part_rows, (part + 1) * part_rows)
            partial[block].append(mine[window] + received[window])
            done_with(partial[block][-1])

    flows, pending = {}, {}

    def hops_of(block):
        hops, stride = [], 1
        if block == 0:
            while stride < count:
                hops.append([(p + stride, p) for p in range(0, count - stride, 2 * stride)])
                stride *= 2
        else:
            hops = [[(p, p - 1)] for p in range(count - 1, block, -1)]
        return hops

    def start_flow(block):
        flows[block] = [hops_of(block), list(partial[block])]
        for part in parts:
            terms[block][part].append(partial[block][part])
        hop(block)

    def hop(block, chosen=parts):
        hops, values = flows[block]
        if not hops:
            return
        for part in chosen:
            if (block, part) in pending:
                base, received = ordered(pending.pop((block, part)))
                values[part] = base + received
                done_with(values[part])
            received = moved(values[part], hops[0])
            if block == 0 or len(hops) == 1:
                terms[block][part].append(received)
            pending[block, part] = (values[part] if block == 0 else partial[block][part], received)
        if PARTS - 1 in chosen:
            hops.pop(0)

    held = {part: [] for part in parts}

    def solve(station):
        last = station + 1 == count
        for part in parts:
            extra = [] if last else [partial[station + 1][part]]
            wanted = ordered(terms[station][part])
            outs = station_step(
                station, part, sep_rhs, inverse, wanted, None if last else couplings[station],
                extra, held[part] if last else [],
            )
            done_with(outs[0])
            held[part].append(outs[0])
            if not last:
                terms[station + 1][part].append(moved(outs[1], [(station, station + 1)]))

    def pass_on(station, block):
        for part in parts:
            solved = ordered([held[part][station]])[0]
            value = onward_step(
                station, part, solved, couplings[block - 1], [partial[block][part]]
            )
            done_with(value)
            terms[block][part].append(moved(value, [(station, block)]))

    passed = set()

    def pass_ready(station, block):
        for earlier in range(min(station + 1, block - 1)):
            if (earlier, block) not in passed:
                passed.add((earlier, block))
                pass_on(earlier, block)

    send_block(0, None)
    following = 0
    for block in range(count):
        if following < block and not flows[following][0]:
            solve(following)
            following += 1
        if block:
            hop(0, parts[:1])
        assemble_block(block)
        if block:
            hop(0, parts[1:])
        for earlier in range(1, block):
            hop(earlier)
        close_block(block)
        for later in range(2, block + 1):
            pass_ready(following - 1, later)
        start_flow(block)
    for station in range(following, count):
        pass_ready(station - 1, station)
        solve(station)
    return jnp.concatenate([held[part][-1] for part in parts], axis=0)


def solution(mesh):
    placed = (
        P(("col", "rhs"), None, None),
        P(("col", "rhs"), None, None),
        P(("col", "rhs"), None),
        P(("col", "rhs"), None),
        P("rhs", "col"),
        P("col", None),
        P("col", None),
    )
    return jax.shard_map(
        local, mesh=mesh, in_specs=placed, out_specs=P("rhs", "col"), check_vma=False
    )
```

time: 288 us -> 145 us (0.50)
  waiting for transfers between devices: 184 us -> 95.9 us
  other arithmetic: 54.1 us -> 0.35 us
  local copies, waits for them, and re-layouts: 24.5 us -> 6.12 us
  starting transfers between devices: 15.6 us -> 30.2 us
  Pallas kernels: 0 us -> 11.3 us
  matrix products: 8.8 us -> 0 us
    all_to_all x2 -> x0, waiting for transfers between devices: 91.3 us -> none  [the longest x1 91.3 us: local(): lax.all_to_all(updates.reshape(col_count * rhs_count, capacity, tile_rows...]
    scatter-add x1 -> x0, other arithmetic: 50.6 us -> none  [local(): jax.ops.segment_sum(arrived.reshape(-1, tile_rows), targets, num_segments...]
    ppermute x3 -> x27, starting transfers between devices: 3.84 us -> 30.2 us  [the longest x11 15.7 us: moved(): return lax.ppermute(value, 'col', pairs)]
    all_to_all x2 -> x0, starting transfers between devices: 11.7 us -> none  [the longest x1 5.88 us: local(): lax.all_to_all(updates.reshape(col_count * rhs_count, capacity, tile_rows...]
    pallas_call x0 -> x14, Pallas kernels: none -> 11.3 us  [the longest x4 5.14 us: assemble(): pl.pallas_call(functools.partial(assemble_kernel, block, block_size, tile...]
    dot_general x2 -> x0, matrix products: 8.8 us -> none  [the longest x1 5.79 us: local(): jnp.einsum('srn,ngc->gscr', desc_rows[0].reshape(rhs_count, tile_rows, bl...]
    slice x3 -> x0, local copies, waits for them, and re-layouts: 6.93 us -> none  [local(): carried = passed_along(carried[:, block_size:], 'col', 1)]
    gather x2 -> x0, local copies, waits for them, and re-layouts: 4.16 us -> none  [the longest x1 3.59 us: local(): jnp.take(upd_factor[0].reshape(block_size, col_count, capacity), source_g...]
  transfers between devices with their start and end apart: 5 -> 27, of which waited for: 4 -> 15; matrix products, arithmetic and copies ran while one was open for 6% -> 0% of each run, Pallas kernels for 0% -> 3%
where the time goes in v2:
time: 145 us; the launch traced here: 144 us
  waiting for transfers between devices  95.9 us (66%)
  starting transfers between devices  30.2 us (21%)
  Pallas kernels  11.3 us (8%)
  local copies, waits for them, and re-layouts  6.12 us (4%)
    ppermute x11, waiting for transfers between devices, moved(): return lax.ppermute(value, 'col', pairs)  61.4 us
    ppermute x12, waiting for transfers between devices, across(): return lax.ppermute(value, 'rhs', pairs)  32.2 us
    ppermute x11, starting transfers between devices, moved(): return lax.ppermute(value, 'col', pairs)  15.7 us
    ppermute x12, starting transfers between devices, across(): return lax.ppermute(value, 'rhs', pairs)  14.2 us
    unnamed x14, local copies, waits for them, and re-layouts  6.12 us
    pallas_call x4, Pallas kernels, assemble(): pl.pallas_call(functools.partial(assemble_kernel, block, block_size, tile...  5.14 us
    pallas_call x2, Pallas kernels, payload(): pl.pallas_call(functools.partial(payload_kernel, blocks, count, with_inde...  3.62 us
  transfers between devices with their start and end apart: 27, of which 15 were waited for; matrix products, arithmetic and copies ran while one was open for 0% of the time, Pallas kernels for 3%

profile of v2, /device:TPU:24, one launch (start us, length us, event | category | flops | bytes accessed | tf_op | source)
XLA Modules:
  0.0 144.1 jit_solution(16613417478113190478)
XLA Ops:
  0.0 1.6 %copy-done.1 = bf16[1,1024,1024]{2,1,0:T(8,128)(2,1)S(1)} copy-done((bf16[1,1024,1024]{2,1,0:T(8,128)(2,1)S(1)}, bf16[1,1024,1024]{2,1,0:T(8,128)(2,1)}, u32[]{:S(2)}) %copy-start.1) | copy-done | bytes 2097176
  1.6 1.6 %copy-done.2 = bf16[1,1024,1024]{2,1,0:T(8,128)(2,1)S(1)} copy-done((bf16[1,1024,1024]{2,1,0:T(8,128)(2,1)S(1)}, bf16[1,1024,1024]{2,1,0:T(8,128)(2,1)}, u32[]{:S(2)}) %copy-start.2) | copy-done | bytes 2097176
  3.2 0.7 copy-done.5
  3.9 0.7 copy-done.6
  4.5 1.3 shard_map.73
  5.8 1.6 %collective-permute-start = (f32[264,256]{1,0:T(8,128)S(1)}, f32[264,256]{1,0:T(8,128)S(1)}, u32[]{:S(2)}, u32[]{:S(2)}) collective-permute-start(f32[264,256]{1,0:T(8,128)S(1)} %get-tuple-element.102), channel_id=1, source_target_pairs={{0,2},{1,3},{2,0},{3,1},{4,6},{5,7},{6,4},{7,5},{8,10},{9,11},{10,... | collective-permute-start | bytes 811016 | tf_op jit(solution)/shard_map/ppermute | solution.py:256
  7.4 1.5 %collective-permute-start.1 = (f32[264,256]{1,0:T(8,128)S(1)}, f32[264,256]{1,0:T(8,128)S(1)}, u32[]{:S(2)}, u32[]{:S(2)}) collective-permute-start(f32[264,256]{1,0:T(8,128)S(1)} %get-tuple-element.103), channel_id=1, source_target_pairs={{0,4},{1,5},{2,6},{3,7},{4,0},{5,1},{6,2},{7,3},{8,12},{9,13},{10,... | collective-permute-start | bytes 811016 | tf_op jit(solution)/shard_map/ppermute | solution.py:256
  8.9 0.5 collective-permute-start.2
  9.4 2.4 %shard_map.74 = (f32[256,256]{1,0:T(8,128)S(1)}, f32[256,256]{1,0:T(8,128)S(1)}, f32[256,256]{1,0:T(8,128)S(1)}, f32[256,256]{1,0:T(8,128)S(1)}, f32[256,256]{1,...) custom-call(s32[1,4]{1,0:T(1,128)S(1)} %copy-done.6, ...), custom_call_target="tpu_custom_call" | custom-call | tf_op jit(solution)/shard_map/pallas_call | solution.py:81
  11.7 0.0 copy-start.4
  11.7 1.6 %copy-done.4 = bf16[1024,1024]{1,0:T(8,128)(2,1)S(1)} copy-done((bf16[1024,1024]{1,0:T(8,128)(2,1)S(1)}, bf16[1024,1024]{1,0:T(8,128)(2,1)}, u32[]{:S(2)}) %copy-start.4) | copy-done | bytes 2097176
  13.3 1.1 shard_map.75
  14.5 0.8 collective-permute-done.refs_1_.refs_5_
  15.2 5.9 %collective-permute-done.1.refs_2_.refs_6_ = f32[264,256]{1,0:T(8,128)S(1)} collective-permute-done((f32[264,256]{1,0:T(8,128)S(1)}, f32[264,256]{1,0:T(8,128)S(1)}, u32[]{:S(2)}, u32[]{:S(2)}) %collective-permute-start.1) | collective-permute-done | bytes 270368 | tf_op jit(solution)/shard_map/ppermute | solution.py:256
  21.1 0.0 collective-permute-done.2.refs_3_.refs_7_
  21.1 1.3 shard_map.76
  22.4 0.1 collective-permute-start.3
  22.5 1.9 %collective-permute-done.3 = f32[128,1024]{1,0:T(8,128)S(1)} collective-permute-done((f32[128,1024]{1,0:T(8,128)S(1)}, f32[128,1024]{1,0:T(8,128)S(1)}, u32[]{:S(2)}, u32[]{:S(2)}) %collective-permute-start.3) | collective-permute-done | bytes 524320 | tf_op jit(solution)/shard_map/ppermute | solution.py:259
  24.4 0.1 add.18.refs_0_
  24.4 2.4 %collective-permute-start.4 = (f32[128,1024]{1,0:T(8,128)S(1)}, f32[128,1024]{1,0:T(8,128)S(1)}, u32[]{:S(2)}, u32[]{:S(2)}) collective-permute-start(f32[128,1024]{1,0:T(8,128)S(1)} %add.18.refs_0_), channel_id=1, source_target_pairs={{8,0},{24,16},{9,1},{25,17},{10,2},{26,18},{11,3},{27,19},{12,4},{... | collective-permute-start | bytes 1572872 | tf_op jit(solution)/shard_map/ppermute | solution.py:262
  26.8 1.3 collective-permute-start.6
  28.1 0.8 collective-permute-start.7
  28.9 1.4 collective-permute-start.8
  30.4 7.9 %collective-permute-done.4.refs_1_ = f32[128,1024]{1,0:T(8,128)S(1)} collective-permute-done((f32[128,1024]{1,0:T(8,128)S(1)}, f32[128,1024]{1,0:T(8,128)S(1)}, u32[]{:S(2)}, u32[]{:S(2)}) %collective-permute-start.4) | collective-permute-done | bytes 524320 | tf_op jit(solution)/shard_map/ppermute | solution.py:262
  38.3 0.1 add.19
  38.3 0.0 copy-start.3
  38.3 1.6 %collective-permute-done.7.refs_2_ = f32[256,256]{1,0:T(8,128)S(1)} collective-permute-done((f32[256,256]{1,0:T(8,128)S(1)}, f32[256,256]{1,0:T(8,128)S(1)}, u32[]{:S(2)}, u32[]{:S(2)}) %collective-permute-start.7) | collective-permute-done | bytes 262176 | tf_op jit(solution)/shard_map/ppermute | solution.py:256
  39.9 1.6 %collective-permute-done.8.refs_3_ = f32[256,256]{1,0:T(8,128)S(1)} collective-permute-done((f32[256,256]{1,0:T(8,128)S(1)}, f32[256,256]{1,0:T(8,128)S(1)}, u32[]{:S(2)}, u32[]{:S(2)}) %collective-permute-start.8) | collective-permute-done | bytes 262176 | tf_op jit(solution)/shard_map/ppermute | solution.py:256
  41.5 1.3 shard_map.77
  42.8 0.1 collective-permute-start.9
  42.9 0.7 collective-permute-start.5
  43.6 0.9 collective-permute-start.15
  44.5 0.3 collective-permute-done.9
  44.8 0.1 add.20.refs_4_.refs_0_
  44.9 2.9 %collective-permute-start.14 = (f32[128,1024]{1,0:T(8,128)S(1)}, f32[128,1024]{1,0:T(8,128)S(1)}, u32[]{:S(2)}, u32[]{:S(2)}) collective-permute-start(f32[128,1024]{1,0:T(8,128)S(1)} %add.20.refs_4_.refs_0_), channel_id=1, source_target_pairs={{24,16},{25,17},{26,18},{27,19},{28,20},{29,21},{30,22},{31,23}} | collective-permute-start | bytes 1572872 | tf_op jit(solution)/shard_map/ppermute | solution.py:262
  47.8 1.5 %collective-permute-start.16 = (f32[256,256]{1,0:T(8,128)S(1)}, f32[256,256]{1,0:T(8,128)S(1)}, u32[]{:S(2)}, u32[]{:S(2)}) collective-permute-start(f32[256,256]{1,0:T(8,128)S(1)} %get-tuple-element.146), channel_id=1, source_target_pairs={{0,4},{1,5},{2,6},{3,7},{4,0},{5,1},{6,2},{7,3},{8,12},{9,13},{10,... | collective-permute-start | bytes 786440 | tf_op jit(solution)/shard_map/ppermute | solution.py:256
  49.3 1.2 collective-permute-start.17
  50.5 2.3 %collective-permute-done.15.refs_1_ = f32[256,256]{1,0:T(8,128)S(1)} collective-permute-done((f32[256,256]{1,0:T(8,128)S(1)}, f32[256,256]{1,0:T(8,128)S(1)}, u32[]{:S(2)}, u32[]{:S(2)}) %collective-permute-start.15) | collective-permute-done | bytes 262176 | tf_op jit(solution)/shard_map/ppermute | solution.py:256
  52.8 8.6 %collective-permute-done.16.refs_2_ = f32[256,256]{1,0:T(8,128)S(1)} collective-permute-done((f32[256,256]{1,0:T(8,128)S(1)}, f32[256,256]{1,0:T(8,128)S(1)}, u32[]{:S(2)}, u32[]{:S(2)}) %collective-permute-start.16) | collective-permute-done | bytes 262176 | tf_op jit(solution)/shard_map/ppermute | solution.py:256
  61.3 1.3 shard_map.79
  62.6 0.1 collective-permute-start.19
  62.7 0.7 collective-permute-start.13
  63.4 0.1 add.21
  63.5 0.7 collective-permute-start.18
  64.2 1.2 collective-permute-start.10
  65.4 1.2 collective-permute-start.11
  66.6 1.2 collective-permute-start.12
  67.8 0.1 add.22.refs_0_.refs_4_.refs_1_
  67.9 5.5 %collective-permute-done.10.refs_1_ = f32[256,256]{1,0:T(8,128)S(1)} collective-permute-done((f32[256,256]{1,0:T(8,128)S(1)}, f32[256,256]{1,0:T(8,128)S(1)}, u32[]{:S(2)}, u32[]{:S(2)}) %collective-permute-start.10) | collective-permute-done | bytes 262176 | tf_op jit(solution)/shard_map/ppermute | solution.py:256
  73.4 4.8 %collective-permute-done.11.refs_2_ = f32[256,256]{1,0:T(8,128)S(1)} collective-permute-done((f32[256,256]{1,0:T(8,128)S(1)}, f32[256,256]{1,0:T(8,128)S(1)}, u32[]{:S(2)}, u32[]{:S(2)}) %collective-permute-start.11) | collective-permute-done | bytes 262176 | tf_op jit(solution)/shard_map/ppermute | solution.py:256
  78.2 1.3 collective-permute-done.12.refs_3_
  79.4 1.3 shard_map.82
  80.7 0.1 collective-permute-start.20
  80.8 0.7 collective-permute-start.23
  81.5 3.1 %collective-permute-start.24 = (f32[128,1024]{1,0:T(8,128)S(1)}, f32[128,1024]{1,0:T(8,128)S(1)}, u32[]{:S(2)}, u32[]{:S(2)}) collective-permute-start(f32[128,1024]{1,0:T(8,128)S(1)} %add.22.refs_0_.refs_4_.refs_1_), channel_id=1, source_target_pairs={{24,16},{25,17},{26,18},{27,19},{28,20},{29,21},{30,22},{31,23}} | collective-permute-start | bytes 1572872 | tf_op jit(solution)/shard_map/ppermute | solution.py:262
  84.6 0.7 collective-permute-start.25
  85.3 0.1 add.23.refs_0_.refs_5_.refs_2_
  85.4 1.3 collective-permute-start.21
  86.7 1.3 collective-permute-start.22
  88.0 8.3 %collective-permute-done.24.refs_2_ = f32[128,1024]{1,0:T(8,128)S(1)} collective-permute-done((f32[128,1024]{1,0:T(8,128)S(1)}, f32[128,1024]{1,0:T(8,128)S(1)}, u32[]{:S(2)}, u32[]{:S(2)}) %collective-permute-start.24) | collective-permute-done | bytes 524320 | tf_op jit(solution)/shard_map/ppermute | solution.py:262
  96.4 1.3 collective-permute-start.26
  97.7 34.0 %collective-permute-done.22.refs_1_ = f32[128,1024]{1,0:T(8,128)S(1)} collective-permute-done((f32[128,1024]{1,0:T(8,128)S(1)}, f32[128,1024]{1,0:T(8,128)S(1)}, u32[]{:S(2)}, u32[]{:S(2)}) %collective-permute-start.22) | collective-permute-done | bytes 524320 | tf_op jit(solution)/shard_map/ppermute | solution.py:262
  131.7 11.1 %collective-permute-done.26.refs_3_ = f32[128,1024]{1,0:T(8,128)S(1)} collective-permute-done((f32[128,1024]{1,0:T(8,128)S(1)}, f32[128,1024]{1,0:T(8,128)S(1)}, u32[]{:S(2)}, u32[]{:S(2)}) %collective-permute-start.26) | collective-permute-done | bytes 524320 | tf_op jit(solution)/shard_map/ppermute | solution.py:262
  142.8 1.3 shard_map.86
  (24 shorter events, 0.1 us)
Async XLA Ops:
  0.0 1.6 %copy-start.1 = (bf16[1,1024,1024]{2,1,0:T(8,128)(2,1)S(1)}, bf16[1,1024,1024]{2,1,0:T(8,128)(2,1)}, u32[]{:S(2)}) copy-start(bf16[1,1024,1024]{2,1,0:T(8,128)(2,1)} %param.7) | copy-start | bytes 6291460
  1.6 1.6 %copy-start.2 = (bf16[1,1024,1024]{2,1,0:T(8,128)(2,1)S(1)}, bf16[1,1024,1024]{2,1,0:T(8,128)(2,1)}, u32[]{:S(2)}) copy-start(bf16[1,1024,1024]{2,1,0:T(8,128)(2,1)} %param.8) | copy-start | bytes 6291460
  3.2 0.7 copy-start.5
  3.9 0.7 copy-start.6
  4.5 7.2 %copy-start = (bf16[1024,4096]{1,0:T(8,128)(2,1)S(1)}, bf16[1024,4096]{1,0:T(8,128)(2,1)}, u32[]{:S(2)}) copy-start(bf16[1024,4096]{1,0:T(8,128)(2,1)} %factor_ref) | copy-start | bytes 25165828
  5.8 9.4 %collective-permute-start = (f32[264,256]{1,0:T(8,128)S(1)}, f32[264,256]{1,0:T(8,128)S(1)}, u32[]{:S(2)}, u32[]{:S(2)}) collective-permute-start(f32[264,256]{1,0:T(8,128)S(1)} %get-tuple-element.102), channel_id=1, source_target_pairs={{0,2},{1,3},{2,0},{3,1},{4,6},{5,7},{6,4},{7,5},{8,10},{9,11},{10,... | collective-permute-start | bytes 811016 | tf_op jit(solution)/shard_map/ppermute | solution.py:256
  7.4 13.7 %collective-permute-start.1 = (f32[264,256]{1,0:T(8,128)S(1)}, f32[264,256]{1,0:T(8,128)S(1)}, u32[]{:S(2)}, u32[]{:S(2)}) collective-permute-start(f32[264,256]{1,0:T(8,128)S(1)} %get-tuple-element.103), channel_id=1, source_target_pairs={{0,4},{1,5},{2,6},{3,7},{4,0},{5,1},{6,2},{7,3},{8,12},{9,13},{10,... | collective-permute-start | bytes 811016 | tf_op jit(solution)/shard_map/ppermute | solution.py:256
  8.9 12.2 %collective-permute-start.2 = (f32[264,256]{1,0:T(8,128)S(1)}, f32[264,256]{1,0:T(8,128)S(1)}, u32[]{:S(2)}, u32[]{:S(2)}) collective-permute-start(f32[264,256]{1,0:T(8,128)S(1)} %get-tuple-element.104), channel_id=1, source_target_pairs={{0,6},{1,7},{2,4},{3,5},{4,2},{5,3},{6,0},{7,1},{8,14},{9,15},{10,... | collective-permute-start | bytes 811016 | tf_op jit(solution)/shard_map/ppermute | solution.py:256
  11.7 1.6 %copy-start.4 = (bf16[1024,1024]{1,0:T(8,128)(2,1)S(1)}, bf16[1024,1024]{1,0:T(8,128)(2,1)}, u32[]{:S(2)}) copy-start(bf16[1024,1024]{1,0:T(8,128)(2,1)} %inverse_ref) | copy-start | bytes 6291460
  22.4 2.0 %collective-permute-start.3 = (f32[128,1024]{1,0:T(8,128)S(1)}, f32[128,1024]{1,0:T(8,128)S(1)}, u32[]{:S(2)}, u32[]{:S(2)}) collective-permute-start(f32[128,1024]{1,0:T(8,128)S(1)} %get-tuple-element.110), channel_id=1, source_target_pairs={{0,1},{1,0},{2,3},{3,2},{4,5},{5,4},{6,7},{7,6},{8,9},{9,8},{10,11... | collective-permute-start | bytes 1572872 | tf_op jit(solution)/shard_map/ppermute | solution.py:259
  24.4 13.8 %collective-permute-start.4 = (f32[128,1024]{1,0:T(8,128)S(1)}, f32[128,1024]{1,0:T(8,128)S(1)}, u32[]{:S(2)}, u32[]{:S(2)}) collective-permute-start(f32[128,1024]{1,0:T(8,128)S(1)} %add.18.refs_0_), channel_id=1, source_target_pairs={{8,0},{24,16},{9,1},{25,17},{10,2},{26,18},{11,3},{27,19},{12,4},{... | collective-permute-start | bytes 1572872 | tf_op jit(solution)/shard_map/ppermute | solution.py:262
  26.8 11.5 %collective-permute-start.6 = (f32[256,256]{1,0:T(8,128)S(1)}, f32[256,256]{1,0:T(8,128)S(1)}, u32[]{:S(2)}, u32[]{:S(2)}) collective-permute-start(f32[256,256]{1,0:T(8,128)S(1)} %get-tuple-element.116), channel_id=1, source_target_pairs={{0,2},{1,3},{2,0},{3,1},{4,6},{5,7},{6,4},{7,5},{8,10},{9,11},{10,... | collective-permute-start | bytes 786440 | tf_op jit(solution)/shard_map/ppermute | solution.py:256
  28.1 11.8 %collective-permute-start.7 = (f32[256,256]{1,0:T(8,128)S(1)}, f32[256,256]{1,0:T(8,128)S(1)}, u32[]{:S(2)}, u32[]{:S(2)}) collective-permute-start(f32[256,256]{1,0:T(8,128)S(1)} %get-tuple-element.118), channel_id=1, source_target_pairs={{0,4},{1,5},{2,6},{3,7},{4,0},{5,1},{6,2},{7,3},{8,12},{9,13},{10,... | collective-permute-start | bytes 786440 | tf_op jit(solution)/shard_map/ppermute | solution.py:256
  28.9 12.6 %collective-permute-start.8 = (f32[256,256]{1,0:T(8,128)S(1)}, f32[256,256]{1,0:T(8,128)S(1)}, u32[]{:S(2)}, u32[]{:S(2)}) collective-permute-start(f32[256,256]{1,0:T(8,128)S(1)} %get-tuple-element.120), channel_id=1, source_target_pairs={{0,6},{1,7},{2,4},{3,5},{4,2},{5,3},{6,0},{7,1},{8,14},{9,15},{10,... | collective-permute-start | bytes 786440 | tf_op jit(solution)/shard_map/ppermute | solution.py:256
  38.3 12.1 %copy-start.3 = (f32[128,1024]{1,0:T(8,128)S(1)}, f32[128,1024]{1,0:T(8,128)}, u32[]{:S(2)}) copy-start(f32[128,1024]{1,0:T(8,128)} %right_ref.7) | copy-start | bytes 1572868
  42.8 2.0 %collective-permute-start.9 = (f32[128,1024]{1,0:T(8,128)S(1)}, f32[128,1024]{1,0:T(8,128)S(1)}, u32[]{:S(2)}, u32[]{:S(2)}) collective-permute-start(f32[128,1024]{1,0:T(8,128)S(1)} %get-tuple-element.126), channel_id=1, source_target_pairs={{0,1},{1,0},{2,3},{3,2},{4,5},{5,4},{6,7},{7,6},{8,9},{9,8},{10,11... | collective-permute-start | bytes 1572872 | tf_op jit(solution)/shard_map/ppermute | solution.py:259
  42.9 7.6 %collective-permute-start.5 = (f32[128,1024]{1,0:T(8,128)S(1)}, f32[128,1024]{1,0:T(8,128)S(1)}, u32[]{:S(2)}, u32[]{:S(2)}) collective-permute-start(f32[128,1024]{1,0:T(8,128)S(1)} %add.19), channel_id=1, source_target_pairs={{16,0},{17,1},{18,2},{19,3},{20,4},{21,5},{22,6},{23,7}} | collective-permute-start | bytes 1572872 | tf_op jit(solution)/shard_map/ppermute | solution.py:262
  43.6 9.2 %collective-permute-start.15 = (f32[256,256]{1,0:T(8,128)S(1)}, f32[256,256]{1,0:T(8,128)S(1)}, u32[]{:S(2)}, u32[]{:S(2)}) collective-permute-start(f32[256,256]{1,0:T(8,128)S(1)} %get-tuple-element.144), channel_id=1, source_target_pairs={{0,2},{1,3},{2,0},{3,1},{4,6},{5,7},{6,4},{7,5},{8,10},{9,11},{10,... | collective-permute-start | bytes 786440 | tf_op jit(solution)/shard_map/ppermute | solution.py:256
  44.9 18.6 %collective-permute-start.14 = (f32[128,1024]{1,0:T(8,128)S(1)}, f32[128,1024]{1,0:T(8,128)S(1)}, u32[]{:S(2)}, u32[]{:S(2)}) collective-permute-start(f32[128,1024]{1,0:T(8,128)S(1)} %add.20.refs_4_.refs_0_), channel_id=1, source_target_pairs={{24,16},{25,17},{26,18},{27,19},{28,20},{29,21},{30,22},{31,23}} | collective-permute-start | bytes 1572872 | tf_op jit(solution)/shard_map/ppermute | solution.py:262
  47.8 13.5 %collective-permute-start.16 = (f32[256,256]{1,0:T(8,128)S(1)}, f32[256,256]{1,0:T(8,128)S(1)}, u32[]{:S(2)}, u32[]{:S(2)}) collective-permute-start(f32[256,256]{1,0:T(8,128)S(1)} %get-tuple-element.146), channel_id=1, source_target_pairs={{0,4},{1,5},{2,6},{3,7},{4,0},{5,1},{6,2},{7,3},{8,12},{9,13},{10,... | collective-permute-start | bytes 786440 | tf_op jit(solution)/shard_map/ppermute | solution.py:256
  49.3 12.1 %collective-permute-start.17 = (f32[256,256]{1,0:T(8,128)S(1)}, f32[256,256]{1,0:T(8,128)S(1)}, u32[]{:S(2)}, u32[]{:S(2)}) collective-permute-start(f32[256,256]{1,0:T(8,128)S(1)} %get-tuple-element.148), channel_id=1, source_target_pairs={{0,6},{1,7},{2,4},{3,5},{4,2},{5,3},{6,0},{7,1},{8,14},{9,15},{10,... | collective-permute-start | bytes 786440 | tf_op jit(solution)/shard_map/ppermute | solution.py:256
  62.6 3.9 %collective-permute-start.19 = (f32[128,1024]{1,0:T(8,128)S(1)}, f32[128,1024]{1,0:T(8,128)S(1)}, u32[]{:S(2)}, u32[]{:S(2)}) collective-permute-start(f32[128,1024]{1,0:T(8,128)S(1)} %get-tuple-element.156), channel_id=1, source_target_pairs={{0,1},{1,0},{2,3},{3,2},{4,5},{5,4},{6,7},{7,6},{8,9},{9,8},{10,11... | collective-permute-start | bytes 1572872 | tf_op jit(solution)/shard_map/ppermute | solution.py:259
  62.7 5.1 %collective-permute-start.13 = (f32[128,1024]{1,0:T(8,128)S(1)}, f32[128,1024]{1,0:T(8,128)S(1)}, u32[]{:S(2)}, u32[]{:S(2)}) collective-permute-start(f32[128,1024]{1,0:T(8,128)S(1)} %get-tuple-element.141), channel_id=1, source_target_pairs={{0,8},{1,9},{2,10},{3,11},{4,12},{5,13},{6,14},{7,15}} | collective-permute-start | bytes 1572872 | tf_op jit(solution)/shard_map/ppermute | solution.py:262
  63.5 4.4 %collective-permute-start.18 = (f32[128,1024]{1,0:T(8,128)S(1)}, f32[128,1024]{1,0:T(8,128)S(1)}, u32[]{:S(2)}, u32[]{:S(2)}) collective-permute-start(f32[128,1024]{1,0:T(8,128)S(1)} %add.21), channel_id=1, source_target_pairs={{16,8},{17,9},{18,10},{19,11},{20,12},{21,13},{22,14},{23,15}} | collective-permute-start | bytes 1572872 | tf_op jit(solution)/shard_map/ppermute | solution.py:262
  64.2 9.2 %collective-permute-start.10 = (f32[256,256]{1,0:T(8,128)S(1)}, f32[256,256]{1,0:T(8,128)S(1)}, u32[]{:S(2)}, u32[]{:S(2)}) collective-permute-start(f32[256,256]{1,0:T(8,128)S(1)} %get-tuple-element.136), channel_id=1, source_target_pairs={{0,2},{1,3},{2,0},{3,1},{4,6},{5,7},{6,4},{7,5},{8,10},{9,11},{10,... | collective-permute-start | bytes 786440 | tf_op jit(solution)/shard_map/ppermute | solution.py:256
  65.4 12.8 %collective-permute-start.11 = (f32[256,256]{1,0:T(8,128)S(1)}, f32[256,256]{1,0:T(8,128)S(1)}, u32[]{:S(2)}, u32[]{:S(2)}) collective-permute-start(f32[256,256]{1,0:T(8,128)S(1)} %get-tuple-element.138), channel_id=1, source_target_pairs={{0,4},{1,5},{2,6},{3,7},{4,0},{5,1},{6,2},{7,3},{8,12},{9,13},{10,... | collective-permute-start | bytes 786440 | tf_op jit(solution)/shard_map/ppermute | solution.py:256
  66.6 12.8 %collective-permute-start.12 = (f32[256,256]{1,0:T(8,128)S(1)}, f32[256,256]{1,0:T(8,128)S(1)}, u32[]{:S(2)}, u32[]{:S(2)}) collective-permute-start(f32[256,256]{1,0:T(8,128)S(1)} %get-tuple-element.140), channel_id=1, source_target_pairs={{0,6},{1,7},{2,4},{3,5},{4,2},{5,3},{6,0},{7,1},{8,14},{9,15},{10,... | collective-permute-start | bytes 786440 | tf_op jit(solution)/shard_map/ppermute | solution.py:256
  80.7 4.6 %collective-permute-start.20 = (f32[128,1024]{1,0:T(8,128)S(1)}, f32[128,1024]{1,0:T(8,128)S(1)}, u32[]{:S(2)}, u32[]{:S(2)}) collective-permute-start(f32[128,1024]{1,0:T(8,128)S(1)} %get-tuple-element.170), channel_id=1, source_target_pairs={{0,1},{1,0},{2,3},{3,2},{4,5},{5,4},{6,7},{7,6},{8,9},{9,8},{10,11... | collective-permute-start | bytes 1572872 | tf_op jit(solution)/shard_map/ppermute | solution.py:259
  80.8 7.2 %collective-permute-start.23 = (f32[128,1024]{1,0:T(8,128)S(1)}, f32[128,1024]{1,0:T(8,128)S(1)}, u32[]{:S(2)}, u32[]{:S(2)}) collective-permute-start(f32[128,1024]{1,0:T(8,128)S(1)} %shard_map.80), channel_id=1, source_target_pairs={{0,16},{1,17},{2,18},{3,19},{4,20},{5,21},{6,22},{7,23}} | collective-permute-start | bytes 1572872 | tf_op jit(solution)/shard_map/ppermute | solution.py:262
  81.5 14.9 %collective-permute-start.24 = (f32[128,1024]{1,0:T(8,128)S(1)}, f32[128,1024]{1,0:T(8,128)S(1)}, u32[]{:S(2)}, u32[]{:S(2)}) collective-permute-start(f32[128,1024]{1,0:T(8,128)S(1)} %add.22.refs_0_.refs_4_.refs_1_), channel_id=1, source_target_pairs={{24,16},{25,17},{26,18},{27,19},{28,20},{29,21},{30,22},{31,23}} | collective-permute-start | bytes 1572872 | tf_op jit(solution)/shard_map/ppermute | solution.py:262
  84.6 11.8 %collective-permute-start.25 = (f32[128,1024]{1,0:T(8,128)S(1)}, f32[128,1024]{1,0:T(8,128)S(1)}, u32[]{:S(2)}, u32[]{:S(2)}) collective-permute-start(f32[128,1024]{1,0:T(8,128)S(1)} %get-tuple-element.176), channel_id=1, source_target_pairs={{8,16},{9,17},{10,18},{11,19},{12,20},{13,21},{14,22},{15,23}} | collective-permute-start | bytes 1572872 | tf_op jit(solution)/shard_map/ppermute | solution.py:262
  85.4 46.3 %collective-permute-start.21 = (f32[128,1024]{1,0:T(8,128)S(1)}, f32[128,1024]{1,0:T(8,128)S(1)}, u32[]{:S(2)}, u32[]{:S(2)}) collective-permute-start(f32[128,1024]{1,0:T(8,128)S(1)} %shard_map.83), channel_id=1, source_target_pairs={{0,24},{1,25},{2,26},{3,27},{4,28},{5,29},{6,30},{7,31}} | collective-permute-start | bytes 1572872 | tf_op jit(solution)/shard_map/ppermute | solution.py:262
  86.7 45.0 %collective-permute-start.22 = (f32[128,1024]{1,0:T(8,128)S(1)}, f32[128,1024]{1,0:T(8,128)S(1)}, u32[]{:S(2)}, u32[]{:S(2)}) collective-permute-start(f32[128,1024]{1,0:T(8,128)S(1)} %shard_map.84), channel_id=1, source_target_pairs={{8,24},{9,25},{10,26},{11,27},{12,28},{13,29},{14,30},{15,31}} | collective-permute-start | bytes 1572872 | tf_op jit(solution)/shard_map/ppermute | solution.py:262
  96.4 46.5 %collective-permute-start.26 = (f32[128,1024]{1,0:T(8,128)S(1)}, f32[128,1024]{1,0:T(8,128)S(1)}, u32[]{:S(2)}, u32[]{:S(2)}) collective-permute-start(f32[128,1024]{1,0:T(8,128)S(1)} %get-tuple-element.181), channel_id=1, source_target_pairs={{16,24},{17,25},{18,26},{19,27},{20,28},{21,29},{22,30},{23,31}} | collective-permute-start | bytes 1572872 | tf_op jit(solution)/shard_map/ppermute | solution.py:262

commit v3 on v2

--- a/solution.py
+++ b/solution.py
@@ -11,7 +11,7 @@
 CORES = 2
 INDEX_ROWS = 8
 SOURCES = 4
-PARTS = 1
+PARTS = 2
 
 
 def params(mib):
@@ -46,9 +46,11 @@
     return found
 
 
-def payload_kernel(blocks, count, with_index, owner_ref, rows_ref, factor_ref, index_ref, *outs):
+def payload_kernel(blocks, parts, count, with_index, owner_ref, rows_ref, factor_ref, index_ref, *refs):
+    outs, (rows_held, factor_held, semaphores) = refs[:-3], refs[-3:]
     tiles, tile_rows, _ = rows_ref.shape
     chips = tiles // CORES
+    part_rows = tile_rows // parts
     capacity = factor_ref.shape[1] // count
     own = lax.axis_index("rhs")
     chip, core = lax.div(own, CORES), lax.rem(own, CORES)
@@ -56,57 +58,98 @@
     def window(block):
         return pl.ds(pl.multiple_of(group_of(owner_ref, block, count) * capacity, capacity), capacity)
 
-    for position, block in enumerate(blocks):
-        factor = factor_ref[:, window(block)]
-        for offset in range(chips):
-            target = jnp.bitwise_xor(chip, offset) * CORES
-            left = jnp.concatenate(
-                [rows_ref[target + core], rows_ref[target + (CORES - 1) - core]], axis=0
+    def target(offset):
+        return jnp.bitwise_xor(chip, offset) * CORES
+
+    copies = [
+        pltpu.make_async_copy(
+            factor_ref.at[:, window(block)], factor_held.at[position], semaphores.at[position]
+        )
+        for position, block in enumerate(blocks)
+    ]
+    for offset in range(chips):
+        place = pl.ds(target(offset), CORES)
+        copies.append(
+            pltpu.make_async_copy(
+                rows_ref.at[place], rows_held.at[place], semaphores.at[len(blocks) + offset]
             )
-            outs[position * chips + offset][: CORES * tile_rows, :] = contract(left, factor)
+        )
+    for copy in copies:
+        copy.start()
     if with_index:
         lists = [index_ref[:, window(block)] for block in range(count)]
         lists.append(jnp.full((INDEX_ROWS - count, capacity), -1, jnp.int32))
         table = jnp.concatenate(lists, axis=0).astype(jnp.float32)
-        for out_ref in outs:
-            out_ref[CORES * tile_rows :, :] = table
-
-
-def payload(blocks, with_index, owner, rows, factor, index, count):
+        for out_ref in outs[:CORES]:
+            for offset in range(chips):
+                out_ref[0, offset, part_rows:, :] = table
+    for position in range(len(blocks)):
+        copies[position].wait()
+        for offset in range(chips):
+            if position == 0:
+                copies[len(blocks) + offset].wait()
+            left = jnp.concatenate(
+                [
+                    rows_held[target(offset) + core],
+                    rows_held[target(offset) + (CORES - 1) - core],
+                ],
+                axis=0,
+            )
+            product = contract(left, factor_held[position])
+            for part in range(parts):
+                for side in range(CORES):
+                    begin = side * tile_rows + part * part_rows
+                    outs[part * CORES + side][position, offset, :part_rows, :] = product[
+                        begin : begin + part_rows
+                    ]
+
+
+def payload(blocks, parts, with_index, owner, rows, factor, index, count):
     tiles, tile_rows, depth = rows.shape
     chips = tiles // CORES
     capacity = factor.shape[1] // count
-    height = CORES * tile_rows + (INDEX_ROWS if with_index else 0)
-    piece = jax.ShapeDtypeStruct((height, capacity), jnp.float32)
-    outs = pl.pallas_call(
-        functools.partial(payload_kernel, blocks, count, with_index),
-        out_shape=[piece] * (chips * len(blocks)),
-        in_specs=[pl.BlockSpec(memory_space=pltpu.SMEM), in_vmem(), in_vmem(), in_vmem()],
-        out_specs=[in_vmem()] * (chips * len(blocks)),
-        compiler_params=params(32),
+    height = tile_rows // parts
+    pieces = []
+    for part in range(parts):
+        extra = INDEX_ROWS if with_index and part == 0 else 0
+        piece = jax.ShapeDtypeStruct((len(blocks), chips, height + extra, capacity), jnp.float32)
+        pieces += [piece] * CORES
+    return pl.pallas_call(
+        functools.partial(payload_kernel, blocks, parts, count, with_index),
+        name=f"payload_block{blocks[0]}",
+        out_shape=pieces,
+        in_specs=[pl.BlockSpec(memory_space=pltpu.SMEM), in_hbm(), in_hbm(), in_vmem()],
+        out_specs=[in_vmem()] * len(pieces),
+        scratch_shapes=[
+            pltpu.VMEM(rows.shape, rows.dtype),
+            pltpu.VMEM((len(blocks), depth, capacity), factor.dtype),
+            pltpu.SemaphoreType.DMA((len(blocks) + chips,)),
+        ],
+        compiler_params=params(40),
         cost_estimate=cost(2 * tiles * tile_rows * depth * capacity * len(blocks), 4 * MIB),
     )(owner, rows, factor, index)
-    return [outs[position * chips : (position + 1) * chips] for position in range(len(blocks))]
-
-
-def assemble_kernel(block, block_size, tile_rows, chips, *refs):
+
+
+def assemble_kernel(block, block_size, height, chips, *refs):
     values_refs, index_refs, outs = refs[:chips], refs[chips : 2 * chips], refs[2 * chips :]
-    capacity = values_refs[0].shape[1]
-    height = CORES * tile_rows
+    capacity = values_refs[0].shape[2]
+    index_row = index_refs[0].shape[1] - INDEX_ROWS + block
     places = lax.broadcasted_iota(jnp.int32, (block_size, capacity), 0)
+    sources = [(chip, core) for chip in range(chips) for core in range(CORES)]
     total = None
-    for first in range(0, chips, SOURCES):
-        chosen = range(first, min(chips, first + SOURCES))
-        values = jnp.concatenate([values_refs[chip][:height, :] for chip in chosen], axis=1)
+    for first in range(0, len(sources), SOURCES):
+        chosen = sources[first : first + SOURCES]
+        values = jnp.concatenate(
+            [values_refs[chip][core, :height, :] for chip, core in chosen], axis=1
+        )
         spread = jnp.concatenate(
             [
                 jnp.where(
-                    places
-                    == index_refs[chip][pl.ds(height + block, 1), :].astype(jnp.int32),
+                    places == index_refs[chip][core, pl.ds(index_row, 1), :].astype(jnp.int32),
                     1.0,
                     0.0,
                 ).astype(jnp.bfloat16)
-                for chip in chosen
+                for chip, core in chosen
             ],
             axis=1,
         )
@@ -120,21 +163,23 @@
         )
         both = both[:height] + both[height:]
         total = both if total is None else total + both
-    outs[0][...] = total[:tile_rows]
-    outs[1][...] = total[tile_rows:]
-
-
-def assemble(block, arrived, holders, tile_rows, block_size):
+    part_rows = height // len(outs)
+    for part, out_ref in enumerate(outs):
+        out_ref[...] = total[part * part_rows : (part + 1) * part_rows]
+
+
+def assemble(block, arrived, holders, height, parts, block_size):
     chips = len(arrived)
-    capacity = arrived[0].shape[1]
-    piece = jax.ShapeDtypeStruct((tile_rows, block_size), jnp.float32)
+    capacity = arrived[0].shape[2]
+    piece = jax.ShapeDtypeStruct((height // parts, block_size), jnp.float32)
     return pl.pallas_call(
-        functools.partial(assemble_kernel, block, block_size, tile_rows, chips),
-        out_shape=[piece] * CORES,
+        functools.partial(assemble_kernel, block, block_size, height, chips),
+        name=f"assemble_block{block}",
+        out_shape=[piece] * parts,
         in_specs=[in_vmem()] * (2 * chips),
-        out_specs=[in_vmem()] * CORES,
+        out_specs=[in_vmem()] * parts,
         compiler_params=params(24),
-        cost_estimate=cost(4 * CORES * chips * tile_rows * capacity * block_size, 2 * MIB),
+        cost_estimate=cost(4 * CORES * chips * height * capacity * block_size, 2 * MIB),
     )(*arrived, *holders)
 
 
@@ -159,6 +204,7 @@
     piece = jax.ShapeDtypeStruct((depth, width), inverse.dtype)
     return pl.pallas_call(
         stage_kernel,
+        name="stage",
         out_shape=[piece] * count,
         in_specs=[in_hbm()] * 2,
         out_specs=[in_vmem()] * count,
@@ -213,6 +259,7 @@
         functools.partial(
             station_kernel, station, part, len(terms), factor is not None, len(extra), len(held)
         ),
+        name=f"solve{station}_part{part}",
         out_shape=[piece] * count,
         in_specs=[in_vmem()] * len(operands),
         out_specs=[in_vmem()] * count,
@@ -234,6 +281,7 @@
     part_rows, width = solved.shape
     return pl.pallas_call(
         functools.partial(onward_kernel, station, part),
+        name=f"onward{station}_part{part}",
         out_shape=jax.ShapeDtypeStruct((part_rows, width), jnp.float32),
         in_specs=[in_vmem()] * (2 + len(extra)),
         out_specs=in_vmem(),
@@ -273,48 +321,57 @@
     make = functools.partial(
         payload, owner=owner_map, factor=upd_factor[0], index=update_index, count=count
     )
-    first_payload = make((0,), True, rows=rows)[0]
-    done_with(first_payload[0])
-    rest = make(tuple(range(1, count)), False, rows=ordered([rows])[0])
-    payloads = [first_payload, *rest]
-    done_with(rest[0][0])
+
+    def both_cores(mine, other, name):
+        with jax.named_scope(f"cores_{name}"):
+            received = other_core(other)
+        return [jnp.stack([mine[offset], received[offset]]) for offset in range(chips)]
+
+    def send(pieces, gate, name):
+        arrived = [pieces[0]]
+        for offset in range(1, chips):
+            value = pieces[offset]
+            if gate is not None:
+                value = after([value], [gate])[0]
+            with jax.named_scope(f"plane{offset}_{name}"):
+                arrived.append(across(value, offset))
+        return arrived
+
+    partial = {0: []}
+    terms = {block: [[] for _ in parts] for block in range(count)}
+    made = make((0,), PARTS, True, rows=rows)
+    ready = [
+        both_cores(made[part * CORES][0], made[part * CORES + 1][0], f"block0_part{part}")
+        for part in parts
+    ]
+    done_with(ready[0][0])
+    arrivals = [send(ready[0], None, "block0_part0")]
+    made = make(tuple(range(1, count)), 1, False, rows=ordered([rows])[0])
+    done_with(made[0])
     weights = stage(*ordered([factor_rows, diag_inverse]), count)
     inverse, couplings = weights[0], weights[1:]
     done_with(inverse)
-
-    arriving = {}
-
-    def send_block(block, gates):
-        sent = payloads[block]
-        pieces = [sent[0]]
-        for offset in range(1, chips):
-            value = sent[offset]
-            if gates is not None:
-                value = after([value], [gates[offset]])[0]
-            pieces.append(across(value, offset))
-        arriving[block] = pieces
-
-    partial = {}
-    terms = {block: [[] for _ in parts] for block in range(count)}
-
-    crossing = {}
+    payloads = [
+        both_cores(made[0][position], made[1][position], f"block{position + 1}")
+        for position in range(count - 1)
+    ]
+    token += [pieces[0] for pieces in payloads]
+    token += [pieces[0] for pieces in ready[1:]]
+    for part in parts:
+        if part:
+            arrivals.append(send(ready[part], arrivals[-1][1], f"block0_part{part}"))
+        values = ordered(arrivals[part])
+        partial[0] += assemble(0, values, arrivals[0], part_rows, 1, block_size)
+        done_with(partial[0][part])
+    holders = arrivals[0]
+    arriving = {1: send(payloads[0], arrivals[-1][1], "block1")}
 
     def assemble_block(block):
         values = ordered(arriving[block])
-        mine, other = assemble(block, values, arriving[0], tile_rows, block_size)
-        done_with(mine)
+        partial[block] = assemble(block, values, holders, tile_rows, PARTS, block_size)
+        done_with(partial[block][0])
         if block + 1 < count:
-            gate = other if block == 0 else terms[0][-1][min(block, len(terms[0][-1]) - 1)]
-            send_block(block + 1, [gate] * chips)
-        crossing[block] = (mine, other_core(other))
-
-    def close_block(block):
-        partial[block] = []
-        for part in parts:
-            mine, received = ordered(crossing[block])
-            window = slice(part * part_rows, (part + 1) * part_rows)
-            partial[block].append(mine[window] + received[window])
-            done_with(partial[block][-1])
+            arriving[block + 1] = send(payloads[block], arriving[block][1], f"block{block + 1}")
 
     flows, pending = {}, {}
 
@@ -341,9 +398,11 @@
         for part in chosen:
             if (block, part) in pending:
                 base, received = ordered(pending.pop((block, part)))
-                values[part] = base + received
+                with jax.named_scope(f"relay_block{block}_part{part}"):
+                    values[part] = base + received
                 done_with(values[part])
-            received = moved(values[part], hops[0])
+            with jax.named_scope(f"down_block{block}_part{part}_left{len(hops)}"):
+                received = moved(values[part], hops[0])
             if block == 0 or len(hops) == 1:
                 terms[block][part].append(received)
             pending[block, part] = (values[part] if block == 0 else partial[block][part], received)
@@ -364,42 +423,47 @@
             done_with(outs[0])
             held[part].append(outs[0])
             if not last:
-                terms[station + 1][part].append(moved(outs[1], [(station, station + 1)]))
+                with jax.named_scope(f"up_from{station}_block{station + 1}_part{part}"):
+                    terms[station + 1][part].append(moved(outs[1], [(station, station + 1)]))
+
+    relayed = {}
 
     def pass_on(station, block):
+        onto = block if station + 2 == block else station + 1
         for part in parts:
             solved = ordered([held[part][station]])[0]
-            value = onward_step(
-                station, part, solved, couplings[block - 1], [partial[block][part]]
-            )
+            extra = [partial[block][part]]
+            if (block, part) in relayed:
+                extra.append(relayed.pop((block, part)))
+            value = onward_step(station, part, solved, couplings[block - 1], extra)
             done_with(value)
-            terms[block][part].append(moved(value, [(station, block)]))
+            with jax.named_scope(f"up_from{station}_block{block}_part{part}"):
+                received = moved(value, [(station, onto)])
+            if onto == block:
+                terms[block][part].append(received)
+            else:
+                relayed[block, part] = received
 
     passed = set()
 
     def pass_ready(station, block):
-        for earlier in range(min(station + 1, block - 1)):
+        for earlier in range(min(station + 1, following, block - 1)):
             if (earlier, block) not in passed:
                 passed.add((earlier, block))
                 pass_on(earlier, block)
 
-    send_block(0, None)
+    start_flow(0)
     following = 0
-    for block in range(count):
+    for block in range(1, count):
+        for earlier in range(block):
+            hop(earlier)
+        assemble_block(block)
+        start_flow(block)
         if following < block and not flows[following][0]:
+            pass_ready(max(following - 2, 0), block)
+            pass_ready(following - 1, following)
             solve(following)
             following += 1
-        if block:
-            hop(0, parts[:1])
-        assemble_block(block)
-        if block:
-            hop(0, parts[1:])
-        for earlier in range(1, block):
-            hop(earlier)
-        close_block(block)
-        for later in range(2, block + 1):
-            pass_ready(following - 1, later)
-        start_flow(block)
     for station in range(following, count):
         pass_ready(station - 1, station)
         solve(station)

time: 145 us -> 123 us (0.85)
  waiting for transfers between devices: 95.9 us -> 42.6 us
  starting transfers between devices: 30.2 us -> 57.1 us
  Pallas kernels: 11.3 us -> 15.6 us
    ppermute x11 -> x22, waiting for transfers between devices: 61.4 us -> 27.6 us  [moved(): return lax.ppermute(value, 'col', pairs)]
    ppermute x11 -> x22, starting transfers between devices: 15.7 us -> 39 us  [moved(): return lax.ppermute(value, 'col', pairs)]
    ppermute x12 -> x15, waiting for transfers between devices: 32.2 us -> 13.7 us  [across(): return lax.ppermute(value, 'rhs', pairs)]
    pallas_call x10 -> x14, Pallas kernels: 9.94 us -> 14.6 us  [the longest x5 6.87 us: assemble(): pl.pallas_call(functools.partial(assemble_kernel, block, block_size, heig...]
    ppermute x12 -> x15, starting transfers between devices: 14.2 us -> 17.3 us  [across(): return lax.ppermute(value, 'rhs', pairs)]
    unnamed x14 -> x16, local copies, waits for them, and re-layouts: 6.12 us -> 4.55 us
  transfers between devices with their start and end apart: 27 -> 42, of which waited for: 15 -> 14; matrix products, arithmetic and copies ran while one was open for 0% -> 1% of each run, Pallas kernels for 3% -> 7%
where the time goes in v3:
time: 123 us; the launch traced here: 122 us
  starting transfers between devices  57.1 us (46%)
  waiting for transfers between devices  42.6 us (35%)
  Pallas kernels  15.6 us (13%)
  local copies, waits for them, and re-layouts  5.06 us (4%)
  other arithmetic  1.27 us (1%)
    ppermute x22, starting transfers between devices, moved(): return lax.ppermute(value, 'col', pairs)  39 us
    ppermute x22, waiting for transfers between devices, moved(): return lax.ppermute(value, 'col', pairs)  27.6 us
    ppermute x15, starting transfers between devices, across(): return lax.ppermute(value, 'rhs', pairs)  17.3 us
    ppermute x15, waiting for transfers between devices, across(): return lax.ppermute(value, 'rhs', pairs)  13.7 us
    pallas_call x5, Pallas kernels, assemble(): pl.pallas_call(functools.partial(assemble_kernel, block, block_size, heig...  6.87 us
    pallas_call x2, Pallas kernels, payload(): pl.pallas_call(functools.partial(payload_kernel, blocks, parts, count, wi...  6.6 us
    unnamed x16, local copies, waits for them, and re-layouts  4.55 us
  transfers between devices with their start and end apart: 42, of which 14 were waited for; matrix products, arithmetic and copies ran while one was open for 1% of the time, Pallas kernels for 7%

profile of v3, /device:TPU:24, one launch (start us, length us, event | category | flops | bytes accessed | tf_op | source)
XLA Modules:
  0.0 122.4 jit_solution(2818623883675068753)
XLA Ops:
  0.0 1.6 %copy-done.1 = bf16[1,1024,1024]{2,1,0:T(8,128)(2,1)S(1)} copy-done((bf16[1,1024,1024]{2,1,0:T(8,128)(2,1)S(1)}, bf16[1,1024,1024]{2,1,0:T(8,128)(2,1)}, u32[]{:S(2)}) %copy-start.1) | copy-done | bytes 2097176
  1.6 1.6 %copy-done.2 = bf16[1,1024,1024]{2,1,0:T(8,128)(2,1)S(1)} copy-done((bf16[1,1024,1024]{2,1,0:T(8,128)(2,1)S(1)}, bf16[1,1024,1024]{2,1,0:T(8,128)(2,1)}, u32[]{:S(2)}) %copy-start.2) | copy-done | bytes 2097176
  3.2 0.7 copy-done.4
  3.9 0.7 copy-done.5
  4.5 2.5 %payload_block0.1 = (f32[1,4,72,256]{3,2,1,0:T(8,128)S(1)}, f32[1,4,72,256]{3,2,1,0:T(8,128)S(1)}, f32[1,4,64,256]{3,2,1,0:T(8,128)S(1)}, f32[1,4,64,256]{3,2,1,0:T(8,128)S(1)}) custom-call(s32[1,4]{1,0:T(1,128)S(1)} %copy-done.5, bf16[8,128,1024]{2,1,0:T(8,128)(2,1)S(1)} %bitcast.52, bf16[1024,1024]{1,0:T(8,128)(2,1)S(1)} %bitcast.54, s32[1,1024]{1,0:T(1,128)S(1)} %copy-done.4), custom_call_target="tpu_custom_call" | custom-call | tf_op jit(solution)/shard_map/payload_block0/pallas_call | solution.py:117
  7.1 0.5 collective-permute-start
  7.7 1.0 collective-permute-done.4
  8.7 0.3 collective-permute-done
  9.1 4.1 %payload_block1.1 = (f32[3,4,128,256]{3,2,1,0:T(8,128)S(1)}, f32[3,4,128,256]{3,2,1,0:T(8,128)S(1)}) custom-call(s32[1,4]{1,0:T(1,128)S(1)} %copy-done.5, bf16[8,128,1024]{2,1,0:T(8,128)(2,1)S(1)} %bitcast.53, bf16[1024,1024]{1,0:T(8,128)(2,1)S(1)} %bitcast.55, s32[1,1024]{1,0:T(1,128)S(1)} %copy-done.4), custom_call_target="tpu_custom_call" | custom-call | tf_op jit(solution)/shard_map/payload_block1/pallas_call | solution.py:117
  13.6 1.6 %collective-permute-start.5 = (f32[2,72,256]{2,1,0:T(8,128)S(1)}, f32[2,72,256]{2,1,0:T(8,128)S(1)}, u32[]{:S(2)}, u32[]{:S(2)}) collective-permute-start(f32[2,72,256]{2,1,0:T(8,128)S(1)} %pad_maximum_fusion.14), channel_id=1, source_target_pairs={{0,2},{1,3},{2,0},{3,1},{4,6},{5,7},{6,4},{7,5},{8,10},{9,11},{10,... | collective-permute-start | bytes 442376 | tf_op jit(solution)/shard_map/plane1_block0_part0/ppermute | solution.py:304
  15.2 1.6 %collective-permute-start.16 = (f32[2,72,256]{2,1,0:T(8,128)S(1)}, f32[2,72,256]{2,1,0:T(8,128)S(1)}, u32[]{:S(2)}, u32[]{:S(2)}) collective-permute-start(f32[2,72,256]{2,1,0:T(8,128)S(1)} %pad_maximum_fusion.15), channel_id=1, source_target_pairs={{0,4},{1,5},{2,6},{3,7},{4,0},{5,1},{6,2},{7,3},{8,12},{9,13},{10,... | collective-permute-start | bytes 442376 | tf_op jit(solution)/shard_map/plane2_block0_part0/ppermute | solution.py:304
  16.8 0.5 collective-permute-start.17
  17.4 1.0 stage.1
  18.6 1.8 %collective-permute-done.5.refs_1_.refs_5_ = f32[2,72,256]{2,1,0:T(8,128)S(1)} collective-permute-done((f32[2,72,256]{2,1,0:T(8,128)S(1)}, f32[2,72,256]{2,1,0:T(8,128)S(1)}, u32[]{:S(2)}, u32[]{:S(2)}) %collective-permute-start.5) | collective-permute-done | bytes 147488 | tf_op jit(solution)/shard_map/plane1_block0_part0/ppermute | solution.py:304
  20.4 1.5 %collective-permute-start.6 = (f32[2,64,256]{2,1,0:T(8,128)S(1)}, f32[2,64,256]{2,1,0:T(8,128)S(1)}, u32[]{:S(2)}, u32[]{:S(2)}) collective-permute-start(f32[2,64,256]{2,1,0:T(8,128)S(1)} %get-tuple-element.118), channel_id=1, source_target_pairs={{0,2},{1,3},{2,0},{3,1},{4,6},{5,7},{6,4},{7,5},{8,10},{9,11},{10,... | collective-permute-start | bytes 393224 | tf_op jit(solution)/shard_map/plane1_block0_part1/ppermute | solution.py:304
  22.0 4.3 %collective-permute-done.6.refs_1_ = f32[2,64,256]{2,1,0:T(8,128)S(1)} collective-permute-done((f32[2,64,256]{2,1,0:T(8,128)S(1)}, f32[2,64,256]{2,1,0:T(8,128)S(1)}, u32[]{:S(2)}, u32[]{:S(2)}) %collective-permute-start.6) | collective-permute-done | bytes 131104 | tf_op jit(solution)/shard_map/plane1_block0_part1/ppermute | solution.py:304
  26.3 1.5 %collective-permute-start.14 = (f32[2,64,256]{2,1,0:T(8,128)S(1)}, f32[2,64,256]{2,1,0:T(8,128)S(1)}, u32[]{:S(2)}, u32[]{:S(2)}) collective-permute-start(f32[2,64,256]{2,1,0:T(8,128)S(1)} %get-tuple-element.126), channel_id=1, source_target_pairs={{0,4},{1,5},{2,6},{3,7},{4,0},{5,1},{6,2},{7,3},{8,12},{9,13},{10,... | collective-permute-start | bytes 393224 | tf_op jit(solution)/shard_map/plane2_block0_part1/ppermute | solution.py:304
  27.8 1.4 %collective-permute-start.15 = (f32[2,64,256]{2,1,0:T(8,128)S(1)}, f32[2,64,256]{2,1,0:T(8,128)S(1)}, u32[]{:S(2)}, u32[]{:S(2)}) collective-permute-start(f32[2,64,256]{2,1,0:T(8,128)S(1)} %pad_maximum_fusion.20), channel_id=1, source_target_pairs={{0,6},{1,7},{2,4},{3,5},{4,2},{5,3},{6,0},{7,1},{8,14},{9,15},{10,... | collective-permute-start | bytes 393224 | tf_op jit(solution)/shard_map/plane3_block0_part1/ppermute | solution.py:304
  29.3 0.6 collective-permute-start.7
  30.1 1.5 %assemble_block0.2.refs_0_ = f32[64,1024]{1,0:T(8,128)S(1)} custom-call(f32[2,72,256]{2,1,0:T(8,128)S(1)} %pad_maximum_fusion.13.refs_0_.refs_4_, f32[2,72,256]{2,1,0:T(8,128)S(1)} %collective-permute-done.5.refs_1_.refs_5_, f32[2,72,256]{2,1,0:T(8,128)S(1)} %collective-permute-done.16.refs_2_.refs_6_, ...), custom_call_target="tpu_custom_call" | custom-call | tf_op jit(solution)/shard_map/assemble_block0/pallas_call | solution.py:175
  31.6 2.4 %collective-permute-start.19 = (f32[64,1024]{1,0:T(8,128)S(1)}, f32[64,1024]{1,0:T(8,128)S(1)}, u32[]{:S(2)}, u32[]{:S(2)}) collective-permute-start(f32[64,1024]{1,0:T(8,128)S(1)} %assemble_block0.2.refs_0_), channel_id=1, source_target_pairs={{8,0},{24,16},{9,1},{25,17},{10,2},{26,18},{11,3},{27,19},{12,4},{... | collective-permute-start | bytes 786440 | tf_op jit(solution)/shard_map/down_block0_part0_left2/ppermute | solution.py:310
  34.0 1.6 %collective-permute-start.12 = (f32[2,128,256]{2,1,0:T(8,128)S(1)}, f32[2,128,256]{2,1,0:T(8,128)S(1)}, u32[]{:S(2)}, u32[]{:S(2)}) collective-permute-start(f32[2,128,256]{2,1,0:T(8,128)S(1)} %get-tuple-element.124), channel_id=1, source_target_pairs={{0,4},{1,5},{2,6},{3,7},{4,0},{5,1},{6,2},{7,3},{8,12},{9,13},{10,... | collective-permute-start | bytes 786440 | tf_op jit(solution)/shard_map/plane2_block1/ppermute | solution.py:304
  35.6 1.4 %collective-permute-start.13 = (f32[2,128,256]{2,1,0:T(8,128)S(1)}, f32[2,128,256]{2,1,0:T(8,128)S(1)}, u32[]{:S(2)}, u32[]{:S(2)}) collective-permute-start(f32[2,128,256]{2,1,0:T(8,128)S(1)} %pad_maximum_fusion.9), channel_id=1, source_target_pairs={{0,6},{1,7},{2,4},{3,5},{4,2},{5,3},{6,0},{7,1},{8,14},{9,15},{10,... | collective-permute-start | bytes 786440 | tf_op jit(solution)/shard_map/plane3_block1/ppermute | solution.py:304
  37.0 1.5 %assemble_block0.3.refs_0_ = f32[64,1024]{1,0:T(8,128)S(1)} custom-call(f32[2,64,256]{2,1,0:T(8,128)S(1)} %pad_maximum_fusion.18.refs_0_, f32[2,64,256]{2,1,0:T(8,128)S(1)} %collective-permute-done.6.refs_1_, f32[2,64,256]{2,1,0:T(8,128)S(1)} %collective-permute-done.14.refs_2_, f32[2,64,256]{2,1,0:T(8,128)S(1)} %collective-permute-done.15.refs_3_, ...), custom_call_target="tpu_custom_call" | custom-call | tf_op jit(solution)/shard_map/assemble_block0/pallas_call | solution.py:175
  38.5 2.1 %collective-permute-start.18 = (f32[64,1024]{1,0:T(8,128)S(1)}, f32[64,1024]{1,0:T(8,128)S(1)}, u32[]{:S(2)}, u32[]{:S(2)}) collective-permute-start(f32[64,1024]{1,0:T(8,128)S(1)} %assemble_block0.3.refs_0_), channel_id=1, source_target_pairs={{8,0},{24,16},{9,1},{25,17},{10,2},{26,18},{11,3},{27,19},{12,4},{... | collective-permute-start | bytes 786440 | tf_op jit(solution)/shard_map/down_block0_part1_left2/ppermute | solution.py:310
  40.6 0.7 collective-permute-start.8
  41.4 0.8 collective-permute-start.21
  42.2 2.3 %collective-permute-done.18.refs_1_ = f32[64,1024]{1,0:T(8,128)S(1)} collective-permute-done((f32[64,1024]{1,0:T(8,128)S(1)}, f32[64,1024]{1,0:T(8,128)S(1)}, u32[]{:S(2)}, u32[]{:S(2)}) %collective-permute-start.18) | collective-permute-done | bytes 262176 | tf_op jit(solution)/shard_map/down_block0_part1_left2/ppermute | solution.py:310
  44.4 1.2 collective-permute-start.28
  45.7 1.8 %collective-permute-done.12.refs_2_ = f32[2,128,256]{2,1,0:T(8,128)S(1)} collective-permute-done((f32[2,128,256]{2,1,0:T(8,128)S(1)}, f32[2,128,256]{2,1,0:T(8,128)S(1)}, u32[]{:S(2)}, u32[]{:S(2)}) %collective-permute-start.12) | collective-permute-done | bytes 262176 | tf_op jit(solution)/shard_map/plane2_block1/ppermute | solution.py:304
  47.5 0.7 collective-permute-start.20
  48.2 1.3 %assemble_block1.1 = (f32[64,1024]{1,0:T(8,128)S(1)}, f32[64,1024]{1,0:T(8,128)S(1)}) custom-call(f32[2,128,256]{2,1,0:T(8,128)S(1)} %pad_maximum_fusion.7.refs_0_, f32[2,128,256]{2,1,0:T(8,128)S(1)} %collective-permute-done.7.refs_1_, f32[2,128,256]{2,1,0:T(8,128)S(1)} %collective-permute-done.12.refs_2_, ...), custom_call_target="tpu_custom_call" | custom-call | tf_op jit(solution)/shard_map/assemble_block1/pallas_call | solution.py:175
  49.5 12.6 %collective-permute-start.23 = (f32[64,1024]{1,0:T(8,128)S(1)}, f32[64,1024]{1,0:T(8,128)S(1)}, u32[]{:S(2)}, u32[]{:S(2)}) collective-permute-start(f32[64,1024]{1,0:T(8,128)S(1)} %get-tuple-element.176.refs_4_.refs_0_), channel_id=1, source_target_pairs={{24,16},{25,17},{26,18},{27,19},{28,20},{29,21},{30,22},{31,23}} | collective-permute-start | bytes 786440 | tf_op jit(solution)/shard_map/down_block1_part1_left2/ppermute | solution.py:310
  62.1 1.3 %collective-permute-start.24 = (f32[64,1024]{1,0:T(8,128)S(1)}, f32[64,1024]{1,0:T(8,128)S(1)}, u32[]{:S(2)}, u32[]{:S(2)}) collective-permute-start(f32[64,1024]{1,0:T(8,128)S(1)} %get-tuple-element.172.refs_4_.refs_0_), channel_id=1, source_target_pairs={{24,16},{25,17},{26,18},{27,19},{28,20},{29,21},{30,22},{31,23}} | collective-permute-start | bytes 786440 | tf_op jit(solution)/shard_map/down_block1_part0_left2/ppermute | solution.py:310
  63.6 2.3 %collective-permute-start.9 = (f32[2,128,256]{2,1,0:T(8,128)S(1)}, f32[2,128,256]{2,1,0:T(8,128)S(1)}, u32[]{:S(2)}, u32[]{:S(2)}) collective-permute-start(f32[2,128,256]{2,1,0:T(8,128)S(1)} %get-tuple-element.121), channel_id=1, source_target_pairs={{0,2},{1,3},{2,0},{3,1},{4,6},{5,7},{6,4},{7,5},{8,10},{9,11},{10,... | collective-permute-start | bytes 786440 | tf_op jit(solution)/shard_map/plane1_block3/ppermute | solution.py:304
  66.0 2.8 %collective-permute-done.24 = f32[64,1024]{1,0:T(8,128)S(1)} collective-permute-done((f32[64,1024]{1,0:T(8,128)S(1)}, f32[64,1024]{1,0:T(8,128)S(1)}, u32[]{:S(2)}, u32[]{:S(2)}) %collective-permute-start.24) | collective-permute-done | bytes 262176 | tf_op jit(solution)/shard_map/down_block1_part0_left2/ppermute | solution.py:310
  68.8 0.7 collective-permute-start.27
  69.5 0.7 collective-permute-start.26
  70.2 0.7 collective-permute-start.25
  70.9 2.5 %collective-permute-done.29.refs_3_ = f32[2,128,256]{2,1,0:T(8,128)S(1)} collective-permute-done((f32[2,128,256]{2,1,0:T(8,128)S(1)}, f32[2,128,256]{2,1,0:T(8,128)S(1)}, u32[]{:S(2)}, u32[]{:S(2)}) %collective-permute-start.29) | collective-permute-done | bytes 262176 | tf_op jit(solution)/shard_map/plane3_block2/ppermute | solution.py:304
  73.4 0.8 collective-permute-start.22
  74.3 1.3 %assemble_block2.1 = (f32[64,1024]{1,0:T(8,128)S(1)}, f32[64,1024]{1,0:T(8,128)S(1)}) custom-call(f32[2,128,256]{2,1,0:T(8,128)S(1)} %pad_maximum_fusion.10.refs_0_, f32[2,128,256]{2,1,0:T(8,128)S(1)} %collective-permute-done.8.refs_1_, f32[2,128,256]{2,1,0:T(8,128)S(1)} %collective-permute-done.28.refs_2_, ...), custom_call_target="tpu_custom_call" | custom-call | tf_op jit(solution)/shard_map/assemble_block2/pallas_call | solution.py:175
  75.8 1.3 %collective-permute-start.10 = (f32[2,128,256]{2,1,0:T(8,128)S(1)}, f32[2,128,256]{2,1,0:T(8,128)S(1)}, u32[]{:S(2)}, u32[]{:S(2)}) collective-permute-start(f32[2,128,256]{2,1,0:T(8,128)S(1)} %get-tuple-element.122), channel_id=1, source_target_pairs={{0,4},{1,5},{2,6},{3,7},{4,0},{5,1},{6,2},{7,3},{8,12},{9,13},{10,... | collective-permute-start | bytes 786440 | tf_op jit(solution)/shard_map/plane2_block3/ppermute | solution.py:304
  77.0 0.7 collective-permute-start.31
  77.8 3.4 %collective-permute-start.30 = (f32[64,1024]{1,0:T(8,128)S(1)}, f32[64,1024]{1,0:T(8,128)S(1)}, u32[]{:S(2)}, u32[]{:S(2)}) collective-permute-start(f32[64,1024]{1,0:T(8,128)S(1)} %get-tuple-element.190.refs_0_.refs_4_), channel_id=1, source_target_pairs={{24,16},{25,17},{26,18},{27,19},{28,20},{29,21},{30,22},{31,23}} | collective-permute-start | bytes 786440 | tf_op jit(solution)/shard_map/down_block2_part0_left1/ppermute | solution.py:310
  81.2 0.7 collective-permute-start.32
  81.9 3.0 %collective-permute-done.10.refs_2_ = f32[2,128,256]{2,1,0:T(8,128)S(1)} collective-permute-done((f32[2,128,256]{2,1,0:T(8,128)S(1)}, f32[2,128,256]{2,1,0:T(8,128)S(1)}, u32[]{:S(2)}, u32[]{:S(2)}) %collective-permute-start.10) | collective-permute-done | bytes 262176 | tf_op jit(solution)/shard_map/plane2_block3/ppermute | solution.py:304
  85.0 0.7 collective-permute-start.35
  85.6 3.7 %collective-permute-start.34 = (f32[64,1024]{1,0:T(8,128)S(1)}, f32[64,1024]{1,0:T(8,128)S(1)}, u32[]{:S(2)}, u32[]{:S(2)}) collective-permute-start(f32[64,1024]{1,0:T(8,128)S(1)} %get-tuple-element.197.refs_0_.refs_4_), channel_id=1, source_target_pairs={{24,16},{25,17},{26,18},{27,19},{28,20},{29,21},{30,22},{31,23}} | collective-permute-start | bytes 786440 | tf_op jit(solution)/shard_map/down_block2_part1_left1/ppermute | solution.py:310
  89.3 0.7 collective-permute-start.36
  90.0 1.3 %assemble_block3.1 = (f32[64,1024]{1,0:T(8,128)S(1)}, f32[64,1024]{1,0:T(8,128)S(1)}) custom-call(f32[2,128,256]{2,1,0:T(8,128)S(1)} %pad_maximum_fusion.1.refs_0_, f32[2,128,256]{2,1,0:T(8,128)S(1)} %collective-permute-done.9.refs_1_, f32[2,128,256]{2,1,0:T(8,128)S(1)} %collective-permute-done.10.refs_2_, ...), custom_call_target="tpu_custom_call" | custom-call | tf_op jit(solution)/shard_map/assemble_block3/pallas_call | solution.py:175
  91.4 0.7 collective-permute-start.37
  92.1 0.7 collective-permute-start.39
  92.8 0.4 collective-permute-done.34.refs_1_
  93.2 1.3 %collective-permute-start.38 = (f32[64,1024]{1,0:T(8,128)S(1)}, f32[64,1024]{1,0:T(8,128)S(1)}, u32[]{:S(2)}, u32[]{:S(2)}) collective-permute-start(f32[64,1024]{1,0:T(8,128)S(1)} %onward1_part0.1), channel_id=1, source_target_pairs={{8,24},{9,25},{10,26},{11,27},{12,28},{13,29},{14,30},{15,31}} | collective-permute-start | bytes 786440 | tf_op jit(solution)/shard_map/up_from1_block3_part0/ppermute | solution.py:310
  94.5 1.3 %collective-permute-start.33 = (f32[64,1024]{1,0:T(8,128)S(1)}, f32[64,1024]{1,0:T(8,128)S(1)}, u32[]{:S(2)}, u32[]{:S(2)}) collective-permute-start(f32[64,1024]{1,0:T(8,128)S(1)} %get-tuple-element.194), channel_id=1, source_target_pairs={{16,24},{17,25},{18,26},{19,27},{20,28},{21,29},{22,30},{23,31}} | collective-permute-start | bytes 786440 | tf_op jit(solution)/shard_map/up_from2_block3_part0/ppermute | solution.py:310
  95.8 1.3 %collective-permute-start.41 = (f32[64,1024]{1,0:T(8,128)S(1)}, f32[64,1024]{1,0:T(8,128)S(1)}, u32[]{:S(2)}, u32[]{:S(2)}) collective-permute-start(f32[64,1024]{1,0:T(8,128)S(1)} %onward1_part1.1), channel_id=1, source_target_pairs={{8,24},{9,25},{10,26},{11,27},{12,28},{13,29},{14,30},{15,31}} | collective-permute-start | bytes 786440 | tf_op jit(solution)/shard_map/up_from1_block3_part1/ppermute | solution.py:310
  97.1 1.3 %collective-permute-start.40 = (f32[64,1024]{1,0:T(8,128)S(1)}, f32[64,1024]{1,0:T(8,128)S(1)}, u32[]{:S(2)}, u32[]{:S(2)}) collective-permute-start(f32[64,1024]{1,0:T(8,128)S(1)} %get-tuple-element.207), channel_id=1, source_target_pairs={{16,24},{17,25},{18,26},{19,27},{20,28},{21,29},{22,30},{23,31}} | collective-permute-start | bytes 786440 | tf_op jit(solution)/shard_map/up_from2_block3_part1/ppermute | solution.py:310
  98.4 9.4 %collective-permute-done.38.refs_2_ = f32[64,1024]{1,0:T(8,128)S(1)} collective-permute-done((f32[64,1024]{1,0:T(8,128)S(1)}, f32[64,1024]{1,0:T(8,128)S(1)}, u32[]{:S(2)}, u32[]{:S(2)}) %collective-permute-start.38) | collective-permute-done | bytes 262176 | tf_op jit(solution)/shard_map/up_from1_block3_part0/ppermute | solution.py:310
  107.9 8.5 %collective-permute-done.33.refs_1_ = f32[64,1024]{1,0:T(8,128)S(1)} collective-permute-done((f32[64,1024]{1,0:T(8,128)S(1)}, f32[64,1024]{1,0:T(8,128)S(1)}, u32[]{:S(2)}, u32[]{:S(2)}) %collective-permute-start.33) | collective-permute-done | bytes 262176 | tf_op jit(solution)/shard_map/up_from2_block3_part0/ppermute | solution.py:310
  116.3 0.5 solve3_part0.1
  116.8 4.2 %collective-permute-done.40.refs_1_ = f32[64,1024]{1,0:T(8,128)S(1)} collective-permute-done((f32[64,1024]{1,0:T(8,128)S(1)}, f32[64,1024]{1,0:T(8,128)S(1)}, u32[]{:S(2)}, u32[]{:S(2)}) %collective-permute-start.40) | collective-permute-done | bytes 262176 | tf_op jit(solution)/shard_map/up_from2_block3_part1/ppermute | solution.py:310
  121.0 0.5 solve3_part1.1
  121.5 0.8 pad_maximum_fusion
  (89 shorter events, 1.7 us)
Async XLA Ops:
  0.0 1.6 %copy-start.1 = (bf16[1,1024,1024]{2,1,0:T(8,128)(2,1)S(1)}, bf16[1,1024,1024]{2,1,0:T(8,128)(2,1)}, u32[]{:S(2)}) copy-start(bf16[1,1024,1024]{2,1,0:T(8,128)(2,1)} %param.7) | copy-start | bytes 6291460
  1.6 1.6 %copy-start.2 = (bf16[1,1024,1024]{2,1,0:T(8,128)(2,1)S(1)}, bf16[1,1024,1024]{2,1,0:T(8,128)(2,1)}, u32[]{:S(2)}) copy-start(bf16[1,1024,1024]{2,1,0:T(8,128)(2,1)} %param.8) | copy-start | bytes 6291460
  3.2 0.7 copy-start.4
  3.9 0.7 copy-start.5
  4.5 12.8 %slice-start = ((s8[8388608]{0:T(1024)(128)(4,1)}), s8[4194304]{0:T(1024)(128)(4,1)S(1)}, s32[]{:S(2)}) async-start(s8[8388608]{0:T(1024)(128)(4,1)} %bitcast.50), calls=%async_computation | async-start | bytes 8388608
  7.1 1.6 %collective-permute-start.4 = (f32[4,64,256]{2,1,0:T(8,128)S(1)}, f32[4,64,256]{2,1,0:T(8,128)S(1)}, u32[]{:S(2)}, u32[]{:S(2)}) collective-permute-start(f32[4,64,256]{2,1,0:T(8,128)S(1)} %bitcast.57), channel_id=1, source_target_pairs={{0,1},{1,0},{2,3},{3,2},{4,5},{5,4},{6,7},{7,6},{8,9},{9,8},{10,11... | collective-permute-start | bytes 786440 | tf_op jit(solution)/shard_map/cores_block0_part1/ppermute | solution.py:307
  7.1 1.9 %collective-permute-start = (f32[4,72,256]{2,1,0:T(8,128)S(1)}, f32[4,72,256]{2,1,0:T(8,128)S(1)}, u32[]{:S(2)}, u32[]{:S(2)}) collective-permute-start(f32[4,72,256]{2,1,0:T(8,128)S(1)} %bitcast.56), channel_id=1, source_target_pairs={{0,1},{1,0},{2,3},{3,2},{4,5},{5,4},{6,7},{7,6},{8,9},{9,8},{10,11... | collective-permute-start | bytes 884744 | tf_op jit(solution)/shard_map/cores_block0_part0/ppermute | solution.py:307
  9.1 8.2 %slice-start.1 = ((s8[8388608]{0:T(1024)(128)(4,1)}), s8[4194304]{0:T(1024)(128)(4,1)S(1)}, s32[]{:S(2)}) async-start(s8[8388608]{0:T(1024)(128)(4,1)} %bitcast.50), calls=%async_computation.1 | async-start | bytes 8388608
  13.2 4.2 %copy-start.3 = (bf16[1024,1024]{1,0:T(8,128)(2,1)S(1)}, bf16[1024,1024]{1,0:T(8,128)(2,1)}, u32[]{:S(2)}) copy-start(bf16[1024,1024]{1,0:T(8,128)(2,1)} %inverse_ref) | copy-start | bytes 6291460
  13.4 7.0 %collective-permute-start.3 = (f32[4,128,256]{2,1,0:T(8,128)S(1)}, f32[4,128,256]{2,1,0:T(8,128)S(1)}, u32[]{:S(2)}, u32[]{:S(2)}) collective-permute-start(f32[4,128,256]{2,1,0:T(8,128)S(1)} %get-tuple-element.223), channel_id=1, source_target_pairs={{0,1},{1,0},{2,3},{3,2},{4,5},{5,4},{6,7},{7,6},{8,9},{9,8},{10,11... | collective-permute-start | bytes 1572872 | tf_op jit(solution)/shard_map/cores_block1/ppermute | solution.py:307
  13.6 6.7 %collective-permute-start.5 = (f32[2,72,256]{2,1,0:T(8,128)S(1)}, f32[2,72,256]{2,1,0:T(8,128)S(1)}, u32[]{:S(2)}, u32[]{:S(2)}) collective-permute-start(f32[2,72,256]{2,1,0:T(8,128)S(1)} %pad_maximum_fusion.14), channel_id=1, source_target_pairs={{0,2},{1,3},{2,0},{3,1},{4,6},{5,7},{6,4},{7,5},{8,10},{9,11},{10,... | collective-permute-start | bytes 442376 | tf_op jit(solution)/shard_map/plane1_block0_part0/ppermute | solution.py:304
  15.2 14.8 %collective-permute-start.16 = (f32[2,72,256]{2,1,0:T(8,128)S(1)}, f32[2,72,256]{2,1,0:T(8,128)S(1)}, u32[]{:S(2)}, u32[]{:S(2)}) collective-permute-start(f32[2,72,256]{2,1,0:T(8,128)S(1)} %pad_maximum_fusion.15), channel_id=1, source_target_pairs={{0,4},{1,5},{2,6},{3,7},{4,0},{5,1},{6,2},{7,3},{8,12},{9,13},{10,... | collective-permute-start | bytes 442376 | tf_op jit(solution)/shard_map/plane2_block0_part0/ppermute | solution.py:304
  16.8 13.2 %collective-permute-start.17 = (f32[2,72,256]{2,1,0:T(8,128)S(1)}, f32[2,72,256]{2,1,0:T(8,128)S(1)}, u32[]{:S(2)}, u32[]{:S(2)}) collective-permute-start(f32[2,72,256]{2,1,0:T(8,128)S(1)} %pad_maximum_fusion.16), channel_id=1, source_target_pairs={{0,6},{1,7},{2,4},{3,5},{4,2},{5,3},{6,0},{7,1},{8,14},{9,15},{10,... | collective-permute-start | bytes 442376 | tf_op jit(solution)/shard_map/plane3_block0_part0/ppermute | solution.py:304
  17.4 10.5 %collective-permute-start.2 = (f32[4,128,256]{2,1,0:T(8,128)S(1)}, f32[4,128,256]{2,1,0:T(8,128)S(1)}, u32[]{:S(2)}, u32[]{:S(2)}) collective-permute-start(f32[4,128,256]{2,1,0:T(8,128)S(1)} %get-tuple-element.224), channel_id=1, source_target_pairs={{0,1},{1,0},{2,3},{3,2},{4,5},{5,4},{6,7},{7,6},{8,9},{9,8},{10,11... | collective-permute-start | bytes 1572872 | tf_op jit(solution)/shard_map/cores_block2/ppermute | solution.py:307
  20.4 8.9 %collective-permute-start.1 = (f32[4,128,256]{2,1,0:T(8,128)S(1)}, f32[4,128,256]{2,1,0:T(8,128)S(1)}, u32[]{:S(2)}, u32[]{:S(2)}) collective-permute-start(f32[4,128,256]{2,1,0:T(8,128)S(1)} %get-tuple-element.225), channel_id=1, source_target_pairs={{0,1},{1,0},{2,3},{3,2},{4,5},{5,4},{6,7},{7,6},{8,9},{9,8},{10,11... | collective-permute-start | bytes 1572872 | tf_op jit(solution)/shard_map/cores_block3/ppermute | solution.py:307
  20.4 5.9 %collective-permute-start.6 = (f32[2,64,256]{2,1,0:T(8,128)S(1)}, f32[2,64,256]{2,1,0:T(8,128)S(1)}, u32[]{:S(2)}, u32[]{:S(2)}) collective-permute-start(f32[2,64,256]{2,1,0:T(8,128)S(1)} %get-tuple-element.118), channel_id=1, source_target_pairs={{0,2},{1,3},{2,0},{3,1},{4,6},{5,7},{6,4},{7,5},{8,10},{9,11},{10,... | collective-permute-start | bytes 393224 | tf_op jit(solution)/shard_map/plane1_block0_part1/ppermute | solution.py:304
  26.3 9.3 %collective-permute-start.14 = (f32[2,64,256]{2,1,0:T(8,128)S(1)}, f32[2,64,256]{2,1,0:T(8,128)S(1)}, u32[]{:S(2)}, u32[]{:S(2)}) collective-permute-start(f32[2,64,256]{2,1,0:T(8,128)S(1)} %get-tuple-element.126), channel_id=1, source_target_pairs={{0,4},{1,5},{2,6},{3,7},{4,0},{5,1},{6,2},{7,3},{8,12},{9,13},{10,... | collective-permute-start | bytes 393224 | tf_op jit(solution)/shard_map/plane2_block0_part1/ppermute | solution.py:304
  27.8 9.2 %collective-permute-start.15 = (f32[2,64,256]{2,1,0:T(8,128)S(1)}, f32[2,64,256]{2,1,0:T(8,128)S(1)}, u32[]{:S(2)}, u32[]{:S(2)}) collective-permute-start(f32[2,64,256]{2,1,0:T(8,128)S(1)} %pad_maximum_fusion.20), channel_id=1, source_target_pairs={{0,6},{1,7},{2,4},{3,5},{4,2},{5,3},{6,0},{7,1},{8,14},{9,15},{10,... | collective-permute-start | bytes 393224 | tf_op jit(solution)/shard_map/plane3_block0_part1/ppermute | solution.py:304
  29.3 11.3 %collective-permute-start.7 = (f32[2,128,256]{2,1,0:T(8,128)S(1)}, f32[2,128,256]{2,1,0:T(8,128)S(1)}, u32[]{:S(2)}, u32[]{:S(2)}) collective-permute-start(f32[2,128,256]{2,1,0:T(8,128)S(1)} %get-tuple-element.119), channel_id=1, source_target_pairs={{0,2},{1,3},{2,0},{3,1},{4,6},{5,7},{6,4},{7,5},{8,10},{9,11},{10,... | collective-permute-start | bytes 786440 | tf_op jit(solution)/shard_map/plane1_block1/ppermute | solution.py:304
  31.6 9.7 %collective-permute-start.19 = (f32[64,1024]{1,0:T(8,128)S(1)}, f32[64,1024]{1,0:T(8,128)S(1)}, u32[]{:S(2)}, u32[]{:S(2)}) collective-permute-start(f32[64,1024]{1,0:T(8,128)S(1)} %assemble_block0.2.refs_0_), channel_id=1, source_target_pairs={{8,0},{24,16},{9,1},{25,17},{10,2},{26,18},{11,3},{27,19},{12,4},{... | collective-permute-start | bytes 786440 | tf_op jit(solution)/shard_map/down_block0_part0_left2/ppermute | solution.py:310
  34.0 13.6 %collective-permute-start.12 = (f32[2,128,256]{2,1,0:T(8,128)S(1)}, f32[2,128,256]{2,1,0:T(8,128)S(1)}, u32[]{:S(2)}, u32[]{:S(2)}) collective-permute-start(f32[2,128,256]{2,1,0:T(8,128)S(1)} %get-tuple-element.124), channel_id=1, source_target_pairs={{0,4},{1,5},{2,6},{3,7},{4,0},{5,1},{6,2},{7,3},{8,12},{9,13},{10,... | collective-permute-start | bytes 786440 | tf_op jit(solution)/shard_map/plane2_block1/ppermute | solution.py:304
  35.6 12.7 %collective-permute-start.13 = (f32[2,128,256]{2,1,0:T(8,128)S(1)}, f32[2,128,256]{2,1,0:T(8,128)S(1)}, u32[]{:S(2)}, u32[]{:S(2)}) collective-permute-start(f32[2,128,256]{2,1,0:T(8,128)S(1)} %pad_maximum_fusion.9), channel_id=1, source_target_pairs={{0,6},{1,7},{2,4},{3,5},{4,2},{5,3},{6,0},{7,1},{8,14},{9,15},{10,... | collective-permute-start | bytes 786440 | tf_op jit(solution)/shard_map/plane3_block1/ppermute | solution.py:304
  38.5 5.9 %collective-permute-start.18 = (f32[64,1024]{1,0:T(8,128)S(1)}, f32[64,1024]{1,0:T(8,128)S(1)}, u32[]{:S(2)}, u32[]{:S(2)}) collective-permute-start(f32[64,1024]{1,0:T(8,128)S(1)} %assemble_block0.3.refs_0_), channel_id=1, source_target_pairs={{8,0},{24,16},{9,1},{25,17},{10,2},{26,18},{11,3},{27,19},{12,4},{... | collective-permute-start | bytes 786440 | tf_op jit(solution)/shard_map/down_block0_part1_left2/ppermute | solution.py:310
  40.6 21.5 %collective-permute-start.8 = (f32[2,128,256]{2,1,0:T(8,128)S(1)}, f32[2,128,256]{2,1,0:T(8,128)S(1)}, u32[]{:S(2)}, u32[]{:S(2)}) collective-permute-start(f32[2,128,256]{2,1,0:T(8,128)S(1)} %get-tuple-element.120), channel_id=1, source_target_pairs={{0,2},{1,3},{2,0},{3,1},{4,6},{5,7},{6,4},{7,5},{8,10},{9,11},{10,... | collective-permute-start | bytes 786440 | tf_op jit(solution)/shard_map/plane1_block2/ppermute | solution.py:304
  41.3 22.2 %copy-start = (f32[128,1024]{1,0:T(8,128)S(1)}, f32[128,1024]{1,0:T(8,128)}, u32[]{:S(2)}) copy-start(f32[128,1024]{1,0:T(8,128)} %right_ref.15) | copy-start | bytes 1572868
  41.4 22.1 %collective-permute-start.21 = (f32[64,1024]{1,0:T(8,128)S(1)}, f32[64,1024]{1,0:T(8,128)S(1)}, u32[]{:S(2)}, u32[]{:S(2)}) collective-permute-start(f32[64,1024]{1,0:T(8,128)S(1)} %add.12), channel_id=1, source_target_pairs={{16,0},{17,1},{18,2},{19,3},{20,4},{21,5},{22,6},{23,7}} | collective-permute-start | bytes 786440 | tf_op jit(solution)/shard_map/down_block0_part0_left1/ppermute | solution.py:310
  44.4 25.8 %collective-permute-start.28 = (f32[2,128,256]{2,1,0:T(8,128)S(1)}, f32[2,128,256]{2,1,0:T(8,128)S(1)}, u32[]{:S(2)}, u32[]{:S(2)}) collective-permute-start(f32[2,128,256]{2,1,0:T(8,128)S(1)} %get-tuple-element.161), channel_id=1, source_target_pairs={{0,4},{1,5},{2,6},{3,7},{4,0},{5,1},{6,2},{7,3},{8,12},{9,13},{10,... | collective-permute-start | bytes 786440 | tf_op jit(solution)/shard_map/plane2_block2/ppermute | solution.py:304
  47.5 16.1 %collective-permute-start.20 = (f32[64,1024]{1,0:T(8,128)S(1)}, f32[64,1024]{1,0:T(8,128)S(1)}, u32[]{:S(2)}, u32[]{:S(2)}) collective-permute-start(f32[64,1024]{1,0:T(8,128)S(1)} %add.13), channel_id=1, source_target_pairs={{16,0},{17,1},{18,2},{19,3},{20,4},{21,5},{22,6},{23,7}} | collective-permute-start | bytes 786440 | tf_op jit(solution)/shard_map/down_block0_part1_left1/ppermute | solution.py:310
  49.5 20.0 %collective-permute-start.23 = (f32[64,1024]{1,0:T(8,128)S(1)}, f32[64,1024]{1,0:T(8,128)S(1)}, u32[]{:S(2)}, u32[]{:S(2)}) collective-permute-start(f32[64,1024]{1,0:T(8,128)S(1)} %get-tuple-element.176.refs_4_.refs_0_), channel_id=1, source_target_pairs={{24,16},{25,17},{26,18},{27,19},{28,20},{29,21},{30,22},{31,23}} | collective-permute-start | bytes 786440 | tf_op jit(solution)/shard_map/down_block1_part1_left2/ppermute | solution.py:310
  62.1 6.7 %collective-permute-start.24 = (f32[64,1024]{1,0:T(8,128)S(1)}, f32[64,1024]{1,0:T(8,128)S(1)}, u32[]{:S(2)}, u32[]{:S(2)}) collective-permute-start(f32[64,1024]{1,0:T(8,128)S(1)} %get-tuple-element.172.refs_4_.refs_0_), channel_id=1, source_target_pairs={{24,16},{25,17},{26,18},{27,19},{28,20},{29,21},{30,22},{31,23}} | collective-permute-start | bytes 786440 | tf_op jit(solution)/shard_map/down_block1_part0_left2/ppermute | solution.py:310
  63.5 10.0 %collective-permute-start.29 = (f32[2,128,256]{2,1,0:T(8,128)S(1)}, f32[2,128,256]{2,1,0:T(8,128)S(1)}, u32[]{:S(2)}, u32[]{:S(2)}) collective-permute-start(f32[2,128,256]{2,1,0:T(8,128)S(1)} %pad_maximum_fusion.12), channel_id=1, source_target_pairs={{0,6},{1,7},{2,4},{3,5},{4,2},{5,3},{6,0},{7,1},{8,14},{9,15},{10,... | collective-permute-start | bytes 786440 | tf_op jit(solution)/shard_map/plane3_block2/ppermute | solution.py:304
  63.6 12.1 %collective-permute-start.9 = (f32[2,128,256]{2,1,0:T(8,128)S(1)}, f32[2,128,256]{2,1,0:T(8,128)S(1)}, u32[]{:S(2)}, u32[]{:S(2)}) collective-permute-start(f32[2,128,256]{2,1,0:T(8,128)S(1)} %get-tuple-element.121), channel_id=1, source_target_pairs={{0,2},{1,3},{2,0},{3,1},{4,6},{5,7},{6,4},{7,5},{8,10},{9,11},{10,... | collective-permute-start | bytes 786440 | tf_op jit(solution)/shard_map/plane1_block3/ppermute | solution.py:304
  68.8 8.2 %collective-permute-start.27 = (f32[64,1024]{1,0:T(8,128)S(1)}, f32[64,1024]{1,0:T(8,128)S(1)}, u32[]{:S(2)}, u32[]{:S(2)}) collective-permute-start(f32[64,1024]{1,0:T(8,128)S(1)} %add.14), channel_id=1, source_target_pairs={{16,8},{17,9},{18,10},{19,11},{20,12},{21,13},{22,14},{23,15}} | collective-permute-start | bytes 786440 | tf_op jit(solution)/shard_map/down_block1_part0_left1/ppermute | solution.py:310
  69.5 7.5 %collective-permute-start.26 = (f32[64,1024]{1,0:T(8,128)S(1)}, f32[64,1024]{1,0:T(8,128)S(1)}, u32[]{:S(2)}, u32[]{:S(2)}) collective-permute-start(f32[64,1024]{1,0:T(8,128)S(1)} %get-tuple-element.160), channel_id=1, source_target_pairs={{0,8},{1,9},{2,10},{3,11},{4,12},{5,13},{6,14},{7,15}} | collective-permute-start | bytes 786440 | tf_op jit(solution)/shard_map/up_from0_block1_part0/ppermute | solution.py:310
  70.2 7.5 %collective-permute-start.25 = (f32[64,1024]{1,0:T(8,128)S(1)}, f32[64,1024]{1,0:T(8,128)S(1)}, u32[]{:S(2)}, u32[]{:S(2)}) collective-permute-start(f32[64,1024]{1,0:T(8,128)S(1)} %add.15), channel_id=1, source_target_pairs={{16,8},{17,9},{18,10},{19,11},{20,12},{21,13},{22,14},{23,15}} | collective-permute-start | bytes 786440 | tf_op jit(solution)/shard_map/down_block1_part1_left1/ppermute | solution.py:310
  73.4 7.8 %collective-permute-start.22 = (f32[64,1024]{1,0:T(8,128)S(1)}, f32[64,1024]{1,0:T(8,128)S(1)}, u32[]{:S(2)}, u32[]{:S(2)}) collective-permute-start(f32[64,1024]{1,0:T(8,128)S(1)} %get-tuple-element.154), channel_id=1, source_target_pairs={{0,8},{1,9},{2,10},{3,11},{4,12},{5,13},{6,14},{7,15}} | collective-permute-start | bytes 786440 | tf_op jit(solution)/shard_map/up_from0_block1_part1/ppermute | solution.py:310
  75.8 9.2 %collective-permute-start.10 = (f32[2,128,256]{2,1,0:T(8,128)S(1)}, f32[2,128,256]{2,1,0:T(8,128)S(1)}, u32[]{:S(2)}, u32[]{:S(2)}) collective-permute-start(f32[2,128,256]{2,1,0:T(8,128)S(1)} %get-tuple-element.122), channel_id=1, source_target_pairs={{0,4},{1,5},{2,6},{3,7},{4,0},{5,1},{6,2},{7,3},{8,12},{9,13},{10,... | collective-permute-start | bytes 786440 | tf_op jit(solution)/shard_map/plane2_block3/ppermute | solution.py:304
  77.0 8.6 %collective-permute-start.11 = (f32[2,128,256]{2,1,0:T(8,128)S(1)}, f32[2,128,256]{2,1,0:T(8,128)S(1)}, u32[]{:S(2)}, u32[]{:S(2)}) collective-permute-start(f32[2,128,256]{2,1,0:T(8,128)S(1)} %pad_maximum_fusion.6), channel_id=1, source_target_pairs={{0,6},{1,7},{2,4},{3,5},{4,2},{5,3},{6,0},{7,1},{8,14},{9,15},{10,... | collective-permute-start | bytes 786440 | tf_op jit(solution)/shard_map/plane3_block3/ppermute | solution.py:304
  77.0 12.3 %collective-permute-start.31 = (f32[64,1024]{1,0:T(8,128)S(1)}, f32[64,1024]{1,0:T(8,128)S(1)}, u32[]{:S(2)}, u32[]{:S(2)}) collective-permute-start(f32[64,1024]{1,0:T(8,128)S(1)} %onward0_part0.2), channel_id=1, source_target_pairs={{0,16},{1,17},{2,18},{3,19},{4,20},{5,21},{6,22},{7,23}} | collective-permute-start | bytes 786440 | tf_op jit(solution)/shard_map/up_from0_block2_part0/ppermute | solution.py:310
  77.8 13.6 %collective-permute-start.30 = (f32[64,1024]{1,0:T(8,128)S(1)}, f32[64,1024]{1,0:T(8,128)S(1)}, u32[]{:S(2)}, u32[]{:S(2)}) collective-permute-start(f32[64,1024]{1,0:T(8,128)S(1)} %get-tuple-element.190.refs_0_.refs_4_), channel_id=1, source_target_pairs={{24,16},{25,17},{26,18},{27,19},{28,20},{29,21},{30,22},{31,23}} | collective-permute-start | bytes 786440 | tf_op jit(solution)/shard_map/down_block2_part0_left1/ppermute | solution.py:310
  81.2 10.9 %collective-permute-start.32 = (f32[64,1024]{1,0:T(8,128)S(1)}, f32[64,1024]{1,0:T(8,128)S(1)}, u32[]{:S(2)}, u32[]{:S(2)}) collective-permute-start(f32[64,1024]{1,0:T(8,128)S(1)} %get-tuple-element.185), channel_id=1, source_target_pairs={{8,16},{9,17},{10,18},{11,19},{12,20},{13,21},{14,22},{15,23}} | collective-permute-start | bytes 786440 | tf_op jit(solution)/shard_map/up_from1_block2_part0/ppermute | solution.py:310
  85.0 7.8 %collective-permute-start.35 = (f32[64,1024]{1,0:T(8,128)S(1)}, f32[64,1024]{1,0:T(8,128)S(1)}, u32[]{:S(2)}, u32[]{:S(2)}) collective-permute-start(f32[64,1024]{1,0:T(8,128)S(1)} %onward0_part1.2), channel_id=1, source_target_pairs={{0,16},{1,17},{2,18},{3,19},{4,20},{5,21},{6,22},{7,23}} | collective-permute-start | bytes 786440 | tf_op jit(solution)/shard_map/up_from0_block2_part1/ppermute | solution.py:310
  85.6 7.5 %collective-permute-start.34 = (f32[64,1024]{1,0:T(8,128)S(1)}, f32[64,1024]{1,0:T(8,128)S(1)}, u32[]{:S(2)}, u32[]{:S(2)}) collective-permute-start(f32[64,1024]{1,0:T(8,128)S(1)} %get-tuple-element.197.refs_0_.refs_4_), channel_id=1, source_target_pairs={{24,16},{25,17},{26,18},{27,19},{28,20},{29,21},{30,22},{31,23}} | collective-permute-start | bytes 786440 | tf_op jit(solution)/shard_map/down_block2_part1_left1/ppermute | solution.py:310
  89.3 3.8 %collective-permute-start.36 = (f32[64,1024]{1,0:T(8,128)S(1)}, f32[64,1024]{1,0:T(8,128)S(1)}, u32[]{:S(2)}, u32[]{:S(2)}) collective-permute-start(f32[64,1024]{1,0:T(8,128)S(1)} %get-tuple-element.195), channel_id=1, source_target_pairs={{8,16},{9,17},{10,18},{11,19},{12,20},{13,21},{14,22},{15,23}} | collective-permute-start | bytes 786440 | tf_op jit(solution)/shard_map/up_from1_block2_part1/ppermute | solution.py:310
  91.4 1.8 %collective-permute-start.37 = (f32[64,1024]{1,0:T(8,128)S(1)}, f32[64,1024]{1,0:T(8,128)S(1)}, u32[]{:S(2)}, u32[]{:S(2)}) collective-permute-start(f32[64,1024]{1,0:T(8,128)S(1)} %onward0_part0.3), channel_id=1, source_target_pairs={{0,8},{1,9},{2,10},{3,11},{4,12},{5,13},{6,14},{7,15}} | collective-permute-start | bytes 786440 | tf_op jit(solution)/shard_map/up_from0_block3_part0/ppermute | solution.py:310
  92.1 3.7 %collective-permute-start.39 = (f32[64,1024]{1,0:T(8,128)S(1)}, f32[64,1024]{1,0:T(8,128)S(1)}, u32[]{:S(2)}, u32[]{:S(2)}) collective-permute-start(f32[64,1024]{1,0:T(8,128)S(1)} %onward0_part1.3), channel_id=1, source_target_pairs={{0,8},{1,9},{2,10},{3,11},{4,12},{5,13},{6,14},{7,15}} | collective-permute-start | bytes 786440 | tf_op jit(solution)/shard_map/up_from0_block3_part1/ppermute | solution.py:310
  93.2 14.7 %collective-permute-start.38 = (f32[64,1024]{1,0:T(8,128)S(1)}, f32[64,1024]{1,0:T(8,128)S(1)}, u32[]{:S(2)}, u32[]{:S(2)}) collective-permute-start(f32[64,1024]{1,0:T(8,128)S(1)} %onward1_part0.1), channel_id=1, source_target_pairs={{8,24},{9,25},{10,26},{11,27},{12,28},{13,29},{14,30},{15,31}} | collective-permute-start | bytes 786440 | tf_op jit(solution)/shard_map/up_from1_block3_part0/ppermute | solution.py:310
  94.5 21.8 %collective-permute-start.33 = (f32[64,1024]{1,0:T(8,128)S(1)}, f32[64,1024]{1,0:T(8,128)S(1)}, u32[]{:S(2)}, u32[]{:S(2)}) collective-permute-start(f32[64,1024]{1,0:T(8,128)S(1)} %get-tuple-element.194), channel_id=1, source_target_pairs={{16,24},{17,25},{18,26},{19,27},{20,28},{21,29},{22,30},{23,31}} | collective-permute-start | bytes 786440 | tf_op jit(solution)/shard_map/up_from2_block3_part0/ppermute | solution.py:310
  95.8 21.0 %collective-permute-start.41 = (f32[64,1024]{1,0:T(8,128)S(1)}, f32[64,1024]{1,0:T(8,128)S(1)}, u32[]{:S(2)}, u32[]{:S(2)}) collective-permute-start(f32[64,1024]{1,0:T(8,128)S(1)} %onward1_part1.1), channel_id=1, source_target_pairs={{8,24},{9,25},{10,26},{11,27},{12,28},{13,29},{14,30},{15,31}} | collective-permute-start | bytes 786440 | tf_op jit(solution)/shard_map/up_from1_block3_part1/ppermute | solution.py:310
  97.1 23.9 %collective-permute-start.40 = (f32[64,1024]{1,0:T(8,128)S(1)}, f32[64,1024]{1,0:T(8,128)S(1)}, u32[]{:S(2)}, u32[]{:S(2)}) collective-permute-start(f32[64,1024]{1,0:T(8,128)S(1)} %get-tuple-element.207), channel_id=1, source_target_pairs={{16,24},{17,25},{18,26},{19,27},{20,28},{21,29},{22,30},{23,31}} | collective-permute-start | bytes 786440 | tf_op jit(solution)/shard_map/up_from2_block3_part1/ppermute | solution.py:310

commit v4 on v0

v4 whole, which is shorter than its diff:
```python
import functools

import jax
import jax.numpy as jnp
from jax import lax
from jax.experimental import pallas as pl
from jax.experimental.pallas import tpu as pltpu
from jax.sharding import PartitionSpec as P

MIB = 1024 * 1024
STAGE, PAYLOAD, ASSEMBLE, RELAY, SOLVE, PASS, PLANE, DOWN, UP = range(9)
CORES = 2
INDEX_ROWS = 8
SOURCES = 4
PARTS = 2
BATCH = 4
FIRST_MIB, REST_MIB = 52, 40
FLOW_PARTS = (2, 1, 1, 1)
ORDER = (
    (RELAY, 0, 1, 0),
    (ASSEMBLE, 1, 0),
    (SOLVE, 0, 0),
    (ASSEMBLE, 0, 1),
    (RELAY, 1, 1, 0),
    (ASSEMBLE, 2, 0),
    (PASS, 0, 2, 0),
    (RELAY, 0, 1, 1),
    (SOLVE, 1, 0),
    (SOLVE, 0, 1),
    (PASS, 0, 2, 1),
    (ASSEMBLE, 3, 0),
    (PASS, 0, 3, 0),
    (SOLVE, 2, 0),
    (SOLVE, 1, 1),
    (PASS, 1, 3, 0),
    (PASS, 0, 3, 1),
    (SOLVE, 2, 1),
    (PASS, 1, 3, 1),
)
GATES = ((PLANE, 1, 0), (ASSEMBLE, 0, 0), (DOWN, 0, 0, 0), (DOWN, 0, 1, 0))
TIES = {
    (RELAY, 0, 1, 0): ((PLANE, 1, 0),),
    (RELAY, 1, 1, 0): ((PLANE, 2, 0),),
}
COSTS = {}


def params(mib):
    return pltpu.CompilerParams(vmem_limit_bytes=mib * MIB)


def cost(key):
    return pl.CostEstimate(flops=COSTS.get(key, 0), bytes_accessed=0, transcendentals=0)


def in_vmem():
    return pl.BlockSpec(memory_space=pltpu.VMEM)


def in_hbm():
    return pl.BlockSpec(memory_space=pltpu.HBM)


def after(values, earlier):
    values, earlier = tuple(values), tuple(earlier)
    return lax.optimization_barrier(values + earlier)[: len(values)]


def contract(left, right):
    return jnp.dot(left, right, preferred_element_type=jnp.float32)


def group_of(owner_ref, block, count):
    found = jnp.int32(0)
    for place in range(count):
        found = found + jnp.where(owner_ref[0, place] == block, place, 0)
    return found


def payload_kernel(pieces, count, owner_ref, rows_ref, factor_ref, index_ref, *refs):
    outs, (rows_held, factor_held, semaphores) = refs[:-3], refs[-3:]
    tiles, tile_rows, _ = rows_ref.shape
    chips = tiles // CORES
    capacity = factor_ref.shape[1] // count
    own = lax.axis_index("rhs")
    chip, core = lax.div(own, CORES), lax.rem(own, CORES)
    height = rows_held.shape[0] // tiles
    origin = pieces[0][1] * height if height < tile_rows else 0

    def window(block):
        return pl.ds(pl.multiple_of(group_of(owner_ref, block, count) * capacity, capacity), capacity)

    def tile(place):
        chip_tile = jnp.bitwise_xor(chip, place // CORES) * CORES
        return chip_tile + (core if place % CORES == 0 else (CORES - 1) - core)

    windows = [
        pltpu.make_async_copy(
            factor_ref.at[:, window(block)], factor_held.at[position], semaphores.at[position]
        )
        for position, (block, _, _) in enumerate(pieces)
    ]
    loads = [
        pltpu.make_async_copy(
            rows_ref.at[tile(place), pl.ds(origin, height)],
            rows_held.at[pl.ds(place * height, height)],
            semaphores.at[len(pieces) + place],
        )
        for place in range(tiles)
    ]
    for copy in [*windows[:1], *loads, *windows[1:]]:
        copy.start()
    if pieces[0][:2] == (0, 0):
        lists = [index_ref[:, window(block)] for block in range(count)]
        lists.append(jnp.full((INDEX_ROWS - count, capacity), -1, jnp.int32))
        table = jnp.concatenate(lists, axis=0).astype(jnp.float32)
        for out_ref in outs[:CORES]:
            for offset in range(chips):
                out_ref[offset, out_ref.shape[1] - INDEX_ROWS :, :] = table
    batch = min(BATCH, tiles)
    for position, (block, part, parts) in enumerate(pieces):
        windows[position].wait()
        wanted = tile_rows // parts
        for begin in range(0, tiles, batch):
            if position == 0:
                for place in range(begin, begin + batch):
                    loads[place].wait()
            product = contract(
                rows_held[begin * height : (begin + batch) * height], factor_held[position]
            )
            for place in range(begin, begin + batch):
                base = (place - begin) * height + part * wanted - origin
                outs[position * CORES + place % CORES][place // CORES, :wanted, :] = product[
                    base : base + wanted
                ]


def payload(pieces, mib, owner, rows, factor, index, count):
    tiles, tile_rows, depth = rows.shape
    chips = tiles // CORES
    capacity = factor.shape[1] // count
    height = tile_rows // pieces[0][2] if len(pieces) == 1 else tile_rows
    shapes = []
    for block, part, parts in pieces:
        extra = INDEX_ROWS if (block, part) == (0, 0) else 0
        shape = (chips, tile_rows // parts + extra, capacity)
        shapes += [jax.ShapeDtypeStruct(shape, jnp.float32)] * CORES
    outs = pl.pallas_call(
        functools.partial(payload_kernel, pieces, count),
        name="payload",
        out_shape=shapes,
        in_specs=[pl.BlockSpec(memory_space=pltpu.SMEM), in_hbm(), in_hbm(), in_vmem()],
        out_specs=[in_vmem()] * len(shapes),
        scratch_shapes=[
            pltpu.VMEM((tiles * height, depth), rows.dtype),
            pltpu.VMEM((len(pieces), depth, capacity), factor.dtype),
            pltpu.SemaphoreType.DMA((len(pieces) + tiles,)),
        ],
        compiler_params=params(mib),
        cost_estimate=cost((PAYLOAD,)),
    )(owner, rows, factor, index)
    return [outs[place : place + CORES] for place in range(0, len(outs), CORES)]


def assemble_kernel(block, block_size, height, chips, *refs):
    values_refs, index_refs, outs = refs[:chips], refs[chips : 2 * chips], refs[2 * chips :]
    capacity = values_refs[0].shape[2]
    index_row = index_refs[0].shape[1] - INDEX_ROWS + block
    places = lax.broadcasted_iota(jnp.int32, (block_size, capacity), 0)
    sources = [(chip, core) for chip in range(chips) for core in range(CORES)]
    total = None
    for first in range(0, len(sources), SOURCES):
        chosen = sources[first : first + SOURCES]
        values = jnp.concatenate(
            [values_refs[chip][core, :height, :] for chip, core in chosen], axis=1
        )
        spread = jnp.concatenate(
            [
                jnp.where(
                    places == index_refs[chip][core, pl.ds(index_row, 1), :].astype(jnp.int32),
                    1.0,
                    0.0,
                ).astype(jnp.bfloat16)
                for chip, core in chosen
            ],
            axis=1,
        )
        high = values.astype(jnp.bfloat16)
        low = (values - high.astype(jnp.float32)).astype(jnp.bfloat16)
        both = lax.dot_general(
            jnp.concatenate([high, low], axis=0),
            spread,
            (((1,), (1,)), ((), ())),
            preferred_element_type=jnp.float32,
        )
        both = both[:height] + both[height:]
        total = both if total is None else total + both
    part_rows = height // len(outs)
    for part, out_ref in enumerate(outs):
        out_ref[...] = total[part * part_rows : (part + 1) * part_rows]


def assemble(block, arrived, holders, height, parts, block_size):
    chips = len(arrived)
    capacity = arrived[0].shape[2]
    piece = jax.ShapeDtypeStruct((height // parts, block_size), jnp.float32)
    return pl.pallas_call(
        functools.partial(assemble_kernel, block, block_size, height, chips),
        name="assemble",
        out_shape=[piece] * parts,
        in_specs=[in_vmem()] * (2 * chips),
        out_specs=[in_vmem()] * parts,
        compiler_params=params(24),
        cost_estimate=cost((ASSEMBLE, block, 0)),
    )(*arrived, *holders)


def stage_kernel(factor_ref, inverse_ref, *refs):
    outs, semaphores = refs[:-1], refs[-1]
    width = inverse_ref.shape[1]
    sources = [inverse_ref] + [
        factor_ref.at[:, pl.ds(block * width, width)] for block in range(1, len(outs))
    ]
    copies = [
        pltpu.make_async_copy(source, out, semaphores.at[place])
        for place, (source, out) in enumerate(zip(sources, outs))
    ]
    for copy in copies:
        copy.start()
    for copy in copies:
        copy.wait()


def stage(factor, inverse, count):
    depth, width = inverse.shape
    piece = jax.ShapeDtypeStruct((depth, width), inverse.dtype)
    return pl.pallas_call(
        stage_kernel,
        name="stage",
        out_shape=[piece] * count,
        in_specs=[in_hbm()] * 2,
        out_specs=[in_vmem()] * count,
        scratch_shapes=[pltpu.SemaphoreType.DMA((count,))],
        compiler_params=params(16),
        cost_estimate=cost((STAGE,)),
    )(factor, inverse)


def pick(group, part):
    return list(group) if part is None or len(group) == 1 else [group[part]]


def rows_of(refs, part, rows):
    if part is None:
        return refs[0][...] if len(refs) == 1 else jnp.concatenate([ref[...] for ref in refs], axis=0)
    if refs[0].shape[0] == rows:
        return refs[0][...]
    return refs[0][pl.ds(part * rows, rows), :]


def split(refs, counts):
    groups, refs = [], list(refs)
    for count in counts:
        groups.append(refs[:count])
        refs = refs[count:]
    return groups, refs


def station_kernel(station, part, counts, terms, has_next, held, *refs):
    groups, refs = split(refs, counts)
    right, inverse, rest = groups[0], groups[1][0], groups[2:]
    rows = right[0].shape[0] // PARTS
    ready = rest[terms + held :] if held else []
    solved_ref = refs[0].at[pl.ds(part * rows, rows)] if ready else refs[0]
    place = lax.axis_index("col")

    @pl.when(place == station)
    def _():
        reduced = rows_of(right, part, rows)
        for group in rest[:terms]:
            reduced = reduced - rows_of(group, part, rows)
        solved = contract(reduced.astype(jnp.bfloat16), inverse[...])
        solved_ref[...] = solved
        if has_next:
            onward = contract(solved.astype(jnp.bfloat16), rest[terms][0][...])
            for group in rest[terms + 1 :]:
                onward = onward + rows_of(group, part, rows)
            refs[1][...] = onward

    for earlier in range(held):

        @pl.when(place == earlier)
        def _(earlier=earlier):
            solved_ref[...] = rest[terms + earlier][0][...]

    for done, group in enumerate(ready):
        refs[0][pl.ds(done * rows, rows), :] = group[0][...]


def station_step(station, part, right, inverse, terms, factor, extra, held, ready):
    rows, width = right.shape[0] // PARTS, right.shape[1]
    groups = [[right], [inverse], *terms, *([] if factor is None else [[factor]]), *extra, *held, *ready]
    operands = [array for group in groups for array in group]
    piece = jax.ShapeDtypeStruct((rows * (len(ready) + 1), width), jnp.float32)
    count = 1 if factor is None else 2
    return pl.pallas_call(
        functools.partial(
            station_kernel, station, part, [len(group) for group in groups], len(terms),
            factor is not None, len(held),
        ),
        name="solve",
        out_shape=[piece] * count,
        in_specs=[in_vmem()] * len(operands),
        out_specs=[in_vmem()] * count,
        compiler_params=params(16),
        cost_estimate=cost((SOLVE, station, part)),
    )(*operands)


def onward_kernel(station, part, counts, *refs):
    groups, refs = split(refs, counts)

    @pl.when(lax.axis_index("col") == station)
    def _():
        rows = refs[0].shape[0]
        onward = contract(rows_of(groups[0], None, rows).astype(jnp.bfloat16), groups[1][0][...])
        for group in groups[2:]:
            onward = onward + rows_of(group, part, rows)
        refs[0][...] = onward


def onward_step(station, part, solved, factor, extra, key):
    rows, width = sum(array.shape[0] for array in solved), solved[0].shape[1]
    groups = [solved, [factor], *extra]
    operands = [array for group in groups for array in group]
    return pl.pallas_call(
        functools.partial(onward_kernel, station, part, [len(group) for group in groups]),
        name="onward",
        out_shape=jax.ShapeDtypeStruct((rows, width), jnp.float32),
        in_specs=[in_vmem()] * len(operands),
        out_specs=in_vmem(),
        compiler_params=params(16),
        cost_estimate=cost(key),
    )(*operands)


def local(desc_rows, upd_factor, update_index, owner_map, sep_rhs, factor_rows, diag_inverse):
    count = lax.axis_size("col")
    tiles = lax.axis_size("rhs")
    chips = tiles // CORES
    block_size = diag_inverse.shape[0]
    tile_rows = sep_rhs.shape[0]
    flow_parts = [FLOW_PARTS[min(block, len(FLOW_PARTS) - 1)] for block in range(count)]

    results, transfers, token = {}, {}, []
    arrived, partial, flow, sums, held, relayed, weights = {}, {}, {}, {}, {}, {}, {}
    risen = {block: {} for block in range(count)}

    def ordered(key, values):
        wanted = [array for group in values for array in group]
        earlier = list(token)
        for tie in TIES.get(key, ()):
            earlier += transfers.get(tie, [])
        if earlier:
            wanted = list(after(wanted, earlier))
        return split(wanted, [len(group) for group in values])[0]

    def moved(value, pairs, key):
        received = lax.ppermute(value, "col", pairs)
        transfers[key] = [received]
        return received

    def both_cores(mine, other):
        received = lax.ppermute(other, "rhs", [(p, p ^ 1) for p in range(tiles)])
        return [jnp.stack([mine[offset], received[offset]]) for offset in range(chips)]

    def exchange(pieces, gate, key):
        gates = transfers.get(gate) or results.get(gate)
        received = []
        for offset in range(1, chips):
            value = pieces[offset]
            if gates:
                value = after([value], [gates[(offset - 1) % len(gates)]])[0]
            pairs = [(p, p ^ (offset * CORES)) for p in range(tiles)]
            received.append(lax.ppermute(value, "rhs", pairs))
        transfers[key] = received
        arrived[key] = [pieces[0], *received]

    rows = desc_rows[0].reshape(tiles, tile_rows, block_size)
    wanted = [(0, part, PARTS) for part in range(PARTS)]
    wanted += [(block, 0, 1) for block in range(1, count)]
    first = payload(
        tuple(wanted[:1]), FIRST_MIB, owner_map, rows, upd_factor[0], update_index, count
    )
    payloads = [both_cores(*first[0])]
    token += [payloads[0][0]]

    hops = {0: []}
    stride = 1
    while stride < count:
        hops[0].append([(p + stride, p) for p in range(0, count - stride, 2 * stride)])
        stride *= 2
    for block in range(1, count):
        hops[block] = [[(p, p - 1)] for p in range(count - 1, block, -1)]

    def rest():
        late = ordered((PAYLOAD,), [[rows]])[0][0]
        pairs = payload(
            tuple(wanted[1:]), REST_MIB, owner_map, late, upd_factor[0], update_index, count
        )
        results[PAYLOAD] = pairs
        return pairs[0][:1]

    def load():
        groups = ordered((STAGE,), [[factor_rows], [diag_inverse]])
        got = stage(groups[0][0], groups[1][0], count)
        weights.update(enumerate(got))
        return got[:1]

    def send_block(block):
        gate = GATES[min(block, len(GATES) - 1)]
        exchange(payloads[PARTS + block - 1], gate, (PLANE, block, 0))

    def start_flow(block, part):
        flow[block, part] = [partial[block][part]]
        if hops[block]:
            flow[block, part].append(
                moved(partial[block][part], hops[block][0], (DOWN, block, 0, part))
            )

    def assemble_part(part):
        key = (ASSEMBLE, 0, part)
        values = ordered(key, [arrived[PLANE, 0, part], arrived[PLANE, 0, 0]])
        done = assemble(
            0, values[0], values[1], tile_rows // PARTS, flow_parts[0] // PARTS, block_size
        )
        results[key] = done
        if part == 0:
            for mine, other in results[PAYLOAD]:
                payloads.append(both_cores(mine, after([other], done[:1])[0]))
            send_block(1)
        if part + 1 < PARTS:
            exchange(payloads[part + 1], GATES[0], (PLANE, 0, part + 1))
        partial.setdefault(0, []).extend(done)
        for place in range(part * len(done), (part + 1) * len(done)):
            start_flow(0, place)
        return done

    def assemble_block(block):
        key = (ASSEMBLE, block, 0)
        values = ordered(key, [arrived[PLANE, block, 0], arrived[PLANE, 0, 0]])
        done = assemble(block, values[0], values[1], tile_rows, flow_parts[block], block_size)
        results[key] = partial[block] = done
        if block + 1 < count:
            send_block(block + 1)
        for part in range(flow_parts[block]):
            start_flow(block, part)
        return done

    def relay(block, hop, part):
        terms = flow[block, part]
        base = sums.get((block, part), terms[0])
        groups = ordered((RELAY, block, hop, part), [[base], [terms[-1]]])
        value = groups[0][0] + groups[1][0]
        received = moved(value, hops[block][hop], (DOWN, block, hop, part))
        if block == 0:
            flow[block, part] = [*terms, received]
            sums[block, part] = value
        else:
            flow[block, part] = [terms[0], received]
        return [value]

    def solve(station, part):
        last = station + 1 == count
        key = (SOLVE, station, part)
        terms = [[array] for array in flow[station, part if flow_parts[station] > 1 else 0]]
        terms += [[array] for array in risen[station].get(part, [])]
        extra = [] if last else [pick(partial[station + 1], part)]
        groups = ordered(key, [*terms, *extra])
        outs = station_step(
            station, part, sep_rhs, weights[0], groups[: len(terms)],
            None if last else weights[station + 1], groups[len(terms) :],
            [[held[part, k]] for k in range(station)] if last else [],
            [[held[p, station]] for p in range(part)] if last and part + 1 == PARTS else [],
        )
        held[part, station] = outs[0]
        if not last:
            received = moved(
                outs[1], [(station, station + 1)], (UP, station, station + 1, part)
            )
            risen[station + 1].setdefault(part, []).append(received)
        return outs[:1]

    def pass_on(station, block, part):
        key = (PASS, station, block, part)
        onto = block if station + 2 == block else station + 1
        extra = [pick(partial[block], part)]
        if (block, part) in relayed:
            extra.append([relayed.pop((block, part))])
        groups = ordered(key, [[held[part, station]], *extra])
        value = onward_step(station, part, groups[0], weights[block], groups[1:], key)
        received = moved(value, [(station, onto)], (UP, station, block, part))
        if onto == block:
            risen[block].setdefault(part, []).append(received)
        else:
            relayed[block, part] = received
        return [value]

    events = {(PAYLOAD,): rest, (STAGE,): load}
    requires = {}
    for part in range(PARTS):
        events[ASSEMBLE, 0, part] = functools.partial(assemble_part, part)
        requires[ASSEMBLE, 0, part] = [(ASSEMBLE, 0, p) for p in range(part)]
    for block in range(count):
        below = [(ASSEMBLE, b, 0) for b in range(1, min(block + 2, count))]
        if block:
            events[ASSEMBLE, block, 0] = functools.partial(assemble_block, block)
            requires[ASSEMBLE, block, 0] = below[: block - 1]
        for part in range(flow_parts[block]):
            own = below[:block] or [(ASSEMBLE, 0, part * PARTS // flow_parts[0])]
            for hop in range(1, len(hops[block])):
                events[RELAY, block, hop, part] = functools.partial(relay, block, hop, part)
                requires[RELAY, block, hop, part] = own + [
                    (RELAY, block, h, part) for h in range(1, hop)
                ]
        for part in range(PARTS):
            events[SOLVE, block, part] = functools.partial(solve, block, part)
            flowing = part if flow_parts[block] > 1 else 0
            requires[SOLVE, block, part] = [
                *below,
                *([] if block else [(ASSEMBLE, 0, p) for p in range(part + 1)]),
                *[(RELAY, block, hop, flowing) for hop in range(1, len(hops[block]))],
                *[(SOLVE, k, p) for k in range(block) for p in range(part + 1)],
                *[(SOLVE, block, p) for p in range(part)],
                *[(PASS, k, block, part) for k in range(block - 1)],
            ]
            for k in range(block - 1):
                events[PASS, k, block, part] = functools.partial(pass_on, k, block, part)
                requires[PASS, k, block, part] = [
                    *below[:block],
                    *[(SOLVE, k, p) for p in range(part + 1)],
                    *[(PASS, e, block, part) for e in range(k)],
                ]

    def run(key):
        if key in token_of or key not in events:
            return
        for earlier in requires.get(key, ()):
            run(earlier)
        token_of[key] = events[key]()
        token[:] = token_of[key][:1]

    token_of = {}
    exchange(payloads[0], None, (PLANE, 0, 0))
    for key in ((PAYLOAD,), (ASSEMBLE, 0, 0), (STAGE,), *ORDER):
        run(key)
    for part in range(PARTS):
        run((SOLVE, count - 1, part))
    return held[PARTS - 1, count - 1]


def solution(mesh):
    placed = (
        P(("col", "rhs"), None, None),
        P(("col", "rhs"), None, None),
        P(("col", "rhs"), None),
        P(("col", "rhs"), None),
        P("rhs", "col"),
        P("col", None),
        P("col", None),
    )
    return jax.shard_map(
        local, mesh=mesh, in_specs=placed, out_specs=P("rhs", "col"), check_vma=False
    )
```

time: 288 us -> 113 us (0.39)
  waiting for transfers between devices: 184 us -> 46.5 us
  other arithmetic: 54.1 us -> 0.44 us
  starting transfers between devices: 15.6 us -> 46 us
  local copies, waits for them, and re-layouts: 24.5 us -> 1.67 us
  Pallas kernels: 0 us -> 17.7 us
  matrix products: 8.8 us -> 0 us
    all_to_all x2 -> x0, waiting for transfers between devices: 91.3 us -> none  [the longest x1 91.3 us: local(): lax.all_to_all(updates.reshape(col_count * rhs_count, capacity, tile_rows...]
    scatter-add x1 -> x0, other arithmetic: 50.6 us -> none  [local(): jax.ops.segment_sum(arrived.reshape(-1, tile_rows), targets, num_segments...]
    ppermute x3 -> x39, waiting for transfers between devices: 92.9 us -> 46.5 us  [the longest x15 22.6 us: exchange(): received.append(lax.ppermute(value, 'rhs', pairs))]
    ppermute x3 -> x39, starting transfers between devices: 3.84 us -> 46 us  [the longest x19 27.7 us: moved(): received = lax.ppermute(value, 'col', pairs)]
    pallas_call x0 -> x22, Pallas kernels: none -> 17.7 us  [the longest x2 7.57 us: payload(): pl.pallas_call(functools.partial(payload_kernel, pieces, count), name='pa...]
    all_to_all x2 -> x0, starting transfers between devices: 11.7 us -> none  [the longest x1 5.88 us: local(): lax.all_to_all(updates.reshape(col_count * rhs_count, capacity, tile_rows...]
    dot_general x2 -> x0, matrix products: 8.8 us -> none  [the longest x1 5.79 us: local(): jnp.einsum('srn,ngc->gscr', desc_rows[0].reshape(rhs_count, tile_rows, bl...]
    slice x3 -> x10, local copies, waits for them, and re-layouts: 6.93 us -> 0.3 us  [the longest x5 0.15 us: both_cores(): received[offset]]
  transfers between devices with their start and end apart: 5 -> 39, of which waited for: 4 -> 13; matrix products, arithmetic and copies ran while one was open for 6% -> 1% of each run, Pallas kernels for 0% -> 11%
where the time goes in v4:
time: 113 us
  waiting for transfers between devices  46.5 us (41%)
  starting transfers between devices  46 us (41%)
  Pallas kernels  17.7 us (16%)
  local copies, waits for them, and re-layouts  1.67 us (1%)
    ppermute x19, starting transfers between devices, moved(): received = lax.ppermute(value, 'col', pairs)  27.7 us
    ppermute x15, waiting for transfers between devices, exchange(): received.append(lax.ppermute(value, 'rhs', pairs))  22.6 us
    ppermute x19, waiting for transfers between devices, moved(): received = lax.ppermute(value, 'col', pairs)  22.3 us
    ppermute x15, starting transfers between devices, exchange(): received.append(lax.ppermute(value, 'rhs', pairs))  17.5 us
    pallas_call x2, Pallas kernels, payload(): pl.pallas_call(functools.partial(payload_kernel, pieces, count), name='pa...  7.57 us
    pallas_call x5, Pallas kernels, assemble(): pl.pallas_call(functools.partial(assemble_kernel, block, block_size, heig...  6.88 us
  transfers between devices with their start and end apart: 39, of which 13 were waited for; matrix products, arithmetic and copies ran while one was open for 1% of the time, Pallas kernels for 11%

profile of v4, /device:TPU:24, one launch (start us, length us, event | category | flops | bytes accessed | tf_op | source)
XLA Modules:
  0.0 113.0 jit_solution(11795742965517527822)
XLA Ops:
  0.0 0.7 copy-done.5
  0.7 0.7 copy-done.7
  1.3 2.9 %payload.2 = (f32[4,72,256]{2,1,0:T(8,128)S(1)}, f32[4,72,256]{2,1,0:T(8,128)S(1)}) custom-call(s32[1,4]{1,0:T(1,128)S(1)} %copy-done.7, bf16[8,128,1024]{2,1,0:T(8,128)(2,1)} %bitcast.2, bf16[1024,1024]{1,0:T(8,128)(2,1)} %bitcast.4, s32[1,1024]{1,0:T(1,128)S(1)} %copy-done.5), custom_call_target="tpu_custom_call" | custom-call | tf_op jit(solution)/shard_map/payload/pallas_call | solution.py:148
  4.3 0.1 collective-permute-start
  4.4 1.5 %collective-permute-done = f32[4,72,256]{2,1,0:T(8,128)S(1)} collective-permute-done((f32[4,72,256]{2,1,0:T(8,128)S(1)}, f32[4,72,256]{2,1,0:T(8,128)S(1)}, u32[]{:S(2)}, u32[]{:S(2)}) %collective-permute-start) | collective-permute-done | bytes 294944 | tf_op jit(solution)/shard_map/ppermute | solution.py:374
  6.0 1.6 %collective-permute-start.1 = (f32[2,72,256]{2,1,0:T(8,128)S(1)}, f32[2,72,256]{2,1,0:T(8,128)S(1)}, u32[]{:S(2)}, u32[]{:S(2)}) collective-permute-start(f32[2,72,256]{2,1,0:T(8,128)S(1)} %pad_maximum_fusion.13), channel_id=1, source_target_pairs={{0,2},{1,3},{2,0},{3,1},{4,6},{5,7},{6,4},{7,5},{8,10},{9,11},{10,... | collective-permute-start | bytes 442376 | tf_op jit(solution)/shard_map/ppermute | solution.py:385
  7.6 1.6 %collective-permute-start.2 = (f32[2,72,256]{2,1,0:T(8,128)S(1)}, f32[2,72,256]{2,1,0:T(8,128)S(1)}, u32[]{:S(2)}, u32[]{:S(2)}) collective-permute-start(f32[2,72,256]{2,1,0:T(8,128)S(1)} %pad_maximum_fusion.14), channel_id=1, source_target_pairs={{0,4},{1,5},{2,6},{3,7},{4,0},{5,1},{6,2},{7,3},{8,12},{9,13},{10,... | collective-permute-start | bytes 442376 | tf_op jit(solution)/shard_map/ppermute | solution.py:385
  9.2 0.5 collective-permute-start.3
  9.8 4.6 %payload.3 = (f32[4,64,256]{2,1,0:T(8,128)S(1)}, f32[4,64,256]{2,1,0:T(8,128)S(1)}, f32[4,128,256]{2,1,0:T(8,128)S(1)}, f32[4,128,256]{2,1,0:T(8,128)S(1)}, f32[...) custom-call(s32[1,4]{1,0:T(1,128)S(1)} %copy-done.8, ...), custom_call_target="tpu_custom_call" | custom-call | tf_op jit(solution)/shard_map/payload/pallas_call | solution.py:148
  14.5 1.9 %collective-permute-done.2.refs_2_.refs_6_ = f32[2,72,256]{2,1,0:T(8,128)S(1)} collective-permute-done((f32[2,72,256]{2,1,0:T(8,128)S(1)}, f32[2,72,256]{2,1,0:T(8,128)S(1)}, u32[]{:S(2)}, u32[]{:S(2)}) %collective-permute-start.2) | collective-permute-done | bytes 147488 | tf_op jit(solution)/shard_map/ppermute | solution.py:385
  16.4 1.5 %assemble.5.refs_2_ = f32[64,1024]{1,0:T(8,128)S(1)} custom-call(f32[2,72,256]{2,1,0:T(8,128)S(1)} %pad_maximum_fusion.12.refs_0_.refs_4_, f32[2,72,256]{2,1,0:T(8,128)S(1)} %collective-permute-done.1.refs_1_.refs_5_, f32[2,72,256]{2,1,0:T(8,128)S(1)} %collective-permute-done.2.refs_2_.refs_6_, f32[2,72,256]{2,1,0:T(8,128)S(1)} %collective-permute-done.3.refs_3_.refs_7_, ...), custom_call_target="tpu_custom_call" | custom-call | tf_op jit(solution)/shard_map/assemble/pallas_call | solution.py:207
  17.9 0.1 collective-permute-start.14
  18.1 0.6 collective-permute-start.6
  18.6 2.4 %collective-permute-start.5 = (f32[64,1024]{1,0:T(8,128)S(1)}, f32[64,1024]{1,0:T(8,128)S(1)}, u32[]{:S(2)}, u32[]{:S(2)}) collective-permute-start(f32[64,1024]{1,0:T(8,128)S(1)} %assemble.5.refs_2_), channel_id=1, source_target_pairs={{8,0},{24,16},{9,1},{25,17},{10,2},{26,18},{11,3},{27,19},{12,4},{... | collective-permute-start | bytes 786440 | tf_op jit(solution)/shard_map/ppermute | solution.py:369
  21.0 0.1 collective-permute-start.19
  21.1 1.0 stage.1
  22.3 1.2 %collective-permute-start.7 = (f32[2,128,256]{2,1,0:T(8,128)S(1)}, f32[2,128,256]{2,1,0:T(8,128)S(1)}, u32[]{:S(2)}, u32[]{:S(2)}) collective-permute-start(f32[2,128,256]{2,1,0:T(8,128)S(1)} %get-tuple-element.163), channel_id=1, source_target_pairs={{0,2},{1,3},{2,0},{3,1},{4,6},{5,7},{6,4},{7,5},{8,10},{9,11},{10,... | collective-permute-start | bytes 786440 | tf_op jit(solution)/shard_map/ppermute | solution.py:385
  23.5 1.0 collective-permute-start.8
  24.5 1.5 %collective-permute-start.9 = (f32[2,128,256]{2,1,0:T(8,128)S(1)}, f32[2,128,256]{2,1,0:T(8,128)S(1)}, u32[]{:S(2)}, u32[]{:S(2)}) collective-permute-start(f32[2,128,256]{2,1,0:T(8,128)S(1)} %pad_maximum_fusion.4), channel_id=1, source_target_pairs={{0,6},{1,7},{2,4},{3,5},{4,2},{5,3},{6,0},{7,1},{8,14},{9,15},{10,... | collective-permute-start | bytes 786440 | tf_op jit(solution)/shard_map/ppermute | solution.py:385
  26.0 5.4 %collective-permute-done.7.refs_1_ = f32[2,128,256]{2,1,0:T(8,128)S(1)} collective-permute-done((f32[2,128,256]{2,1,0:T(8,128)S(1)}, f32[2,128,256]{2,1,0:T(8,128)S(1)}, u32[]{:S(2)}, u32[]{:S(2)}) %collective-permute-start.7) | collective-permute-done | bytes 262176 | tf_op jit(solution)/shard_map/ppermute | solution.py:385
  31.5 1.2 %collective-permute-start.15 = (f32[2,64,256]{2,1,0:T(8,128)S(1)}, f32[2,64,256]{2,1,0:T(8,128)S(1)}, u32[]{:S(2)}, u32[]{:S(2)}) collective-permute-start(f32[2,64,256]{2,1,0:T(8,128)S(1)} %pad_maximum_fusion.17), channel_id=1, source_target_pairs={{0,2},{1,3},{2,0},{3,1},{4,6},{5,7},{6,4},{7,5},{8,10},{9,11},{10,... | collective-permute-start | bytes 393224 | tf_op jit(solution)/shard_map/ppermute | solution.py:385
  32.7 3.1 %collective-permute-done.8.refs_2_ = f32[2,128,256]{2,1,0:T(8,128)S(1)} collective-permute-done((f32[2,128,256]{2,1,0:T(8,128)S(1)}, f32[2,128,256]{2,1,0:T(8,128)S(1)}, u32[]{:S(2)}, u32[]{:S(2)}) %collective-permute-start.8) | collective-permute-done | bytes 262176 | tf_op jit(solution)/shard_map/ppermute | solution.py:385
  35.8 2.2 %collective-permute-done.9.refs_3_ = f32[2,128,256]{2,1,0:T(8,128)S(1)} collective-permute-done((f32[2,128,256]{2,1,0:T(8,128)S(1)}, f32[2,128,256]{2,1,0:T(8,128)S(1)}, u32[]{:S(2)}, u32[]{:S(2)}) %collective-permute-start.9) | collective-permute-done | bytes 262176 | tf_op jit(solution)/shard_map/ppermute | solution.py:385
  38.1 0.7 collective-permute-start.10
  38.8 0.6 collective-permute-start.16
  39.4 1.5 %collective-permute-start.17 = (f32[2,64,256]{2,1,0:T(8,128)S(1)}, f32[2,64,256]{2,1,0:T(8,128)S(1)}, u32[]{:S(2)}, u32[]{:S(2)}) collective-permute-start(f32[2,64,256]{2,1,0:T(8,128)S(1)} %pad_maximum_fusion.19), channel_id=1, source_target_pairs={{0,6},{1,7},{2,4},{3,5},{4,2},{5,3},{6,0},{7,1},{8,14},{9,15},{10,... | collective-permute-start | bytes 393224 | tf_op jit(solution)/shard_map/ppermute | solution.py:385
  40.9 1.3 %assemble.6.refs_6_.refs_2_ = f32[128,1024]{1,0:T(8,128)S(1)} custom-call(f32[2,128,256]{2,1,0:T(8,128)S(1)} %pad_maximum_fusion.7.refs_0_, f32[2,128,256]{2,1,0:T(8,128)S(1)} %collective-permute-done.7.refs_1_, f32[2,128,256]{2,1,0:T(8,128)S(1)} %collective-permute-done.8.refs_2_, f32[2,128,256]{2,1,0:T(8,128)S(1)} %collective-permute-done.9.refs_3_, ...), custom_call_target="tpu_custom_call" | custom-call | tf_op jit(solution)/shard_map/assemble/pallas_call | solution.py:207
  42.2 2.8 %collective-permute-start.23 = (f32[128,1024]{1,0:T(8,128)S(1)}, f32[128,1024]{1,0:T(8,128)S(1)}, u32[]{:S(2)}, u32[]{:S(2)}) collective-permute-start(f32[128,1024]{1,0:T(8,128)S(1)} %assemble.6.refs_6_.refs_2_), channel_id=1, source_target_pairs={{24,16},{25,17},{26,18},{27,19},{28,20},{29,21},{30,22},{31,23}} | collective-permute-start | bytes 1572872 | tf_op jit(solution)/shard_map/ppermute | solution.py:369
  45.1 1.2 %collective-permute-done.16.refs_2_ = f32[2,64,256]{2,1,0:T(8,128)S(1)} collective-permute-done((f32[2,64,256]{2,1,0:T(8,128)S(1)}, f32[2,64,256]{2,1,0:T(8,128)S(1)}, u32[]{:S(2)}, u32[]{:S(2)}) %collective-permute-start.16) | collective-permute-done | bytes 131104 | tf_op jit(solution)/shard_map/ppermute | solution.py:385
  46.4 0.9 collective-permute-start.20
  47.2 1.0 collective-permute-start.21
  48.2 1.7 %collective-permute-start.22 = (f32[2,128,256]{2,1,0:T(8,128)S(1)}, f32[2,128,256]{2,1,0:T(8,128)S(1)}, u32[]{:S(2)}, u32[]{:S(2)}) collective-permute-start(f32[2,128,256]{2,1,0:T(8,128)S(1)} %pad_maximum_fusion.11), channel_id=1, source_target_pairs={{0,6},{1,7},{2,4},{3,5},{4,2},{5,3},{6,0},{7,1},{8,14},{9,15},{10,... | collective-permute-start | bytes 786440 | tf_op jit(solution)/shard_map/ppermute | solution.py:385
  49.9 1.5 %assemble.7.refs_2_ = f32[64,1024]{1,0:T(8,128)S(1)} custom-call(f32[2,64,256]{2,1,0:T(8,128)S(1)} %pad_maximum_fusion.16.refs_0_, f32[2,64,256]{2,1,0:T(8,128)S(1)} %collective-permute-done.15.refs_1_, f32[2,64,256]{2,1,0:T(8,128)S(1)} %collective-permute-done.16.refs_2_, f32[2,64,256]{2,1,0:T(8,128)S(1)} %collective-permute-done.17.refs_3_, ...), custom_call_target="tpu_custom_call" | custom-call | tf_op jit(solution)/shard_map/assemble/pallas_call | solution.py:207
  51.5 3.3 %collective-permute-done.20.refs_1_ = f32[2,128,256]{2,1,0:T(8,128)S(1)} collective-permute-done((f32[2,128,256]{2,1,0:T(8,128)S(1)}, f32[2,128,256]{2,1,0:T(8,128)S(1)}, u32[]{:S(2)}, u32[]{:S(2)}) %collective-permute-start.20) | collective-permute-done | bytes 262176 | tf_op jit(solution)/shard_map/ppermute | solution.py:385
  54.8 2.6 %collective-permute-start.18 = (f32[64,1024]{1,0:T(8,128)S(1)}, f32[64,1024]{1,0:T(8,128)S(1)}, u32[]{:S(2)}, u32[]{:S(2)}) collective-permute-start(f32[64,1024]{1,0:T(8,128)S(1)} %assemble.7.refs_2_), channel_id=1, source_target_pairs={{8,0},{24,16},{9,1},{25,17},{10,2},{26,18},{11,3},{27,19},{12,4},{... | collective-permute-start | bytes 786440 | tf_op jit(solution)/shard_map/ppermute | solution.py:369
  57.4 1.1 collective-permute-done.21.refs_2_
  58.5 0.7 collective-permute-start.25
  59.3 0.7 collective-permute-start.26
  60.0 1.3 %assemble.8.refs_2_.refs_6_ = f32[128,1024]{1,0:T(8,128)S(1)} custom-call(f32[2,128,256]{2,1,0:T(8,128)S(1)} %pad_maximum_fusion.8.refs_0_, f32[2,128,256]{2,1,0:T(8,128)S(1)} %collective-permute-done.20.refs_1_, f32[2,128,256]{2,1,0:T(8,128)S(1)} %collective-permute-done.21.refs_2_, f32[2,128,256]{2,1,0:T(8,128)S(1)} %collective-permute-done.22.refs_3_, ...), custom_call_target="tpu_custom_call" | custom-call | tf_op jit(solution)/shard_map/assemble/pallas_call | solution.py:207
  61.4 0.7 collective-permute-start.24
  62.1 0.9 collective-permute-start.11
  63.0 1.1 collective-permute-start.12
  64.2 7.2 %collective-permute-start.27 = (f32[128,1024]{1,0:T(8,128)S(1)}, f32[128,1024]{1,0:T(8,128)S(1)}, u32[]{:S(2)}, u32[]{:S(2)}) collective-permute-start(f32[128,1024]{1,0:T(8,128)S(1)} %assemble.8.refs_2_.refs_6_), channel_id=1, source_target_pairs={{24,16},{25,17},{26,18},{27,19},{28,20},{29,21},{30,22},{31,23}} | collective-permute-start | bytes 1572872 | tf_op jit(solution)/shard_map/ppermute | solution.py:369
  71.4 1.4 %collective-permute-start.13 = (f32[2,128,256]{2,1,0:T(8,128)S(1)}, f32[2,128,256]{2,1,0:T(8,128)S(1)}, u32[]{:S(2)}, u32[]{:S(2)}) collective-permute-start(f32[2,128,256]{2,1,0:T(8,128)S(1)} %pad_maximum_fusion.6), channel_id=1, source_target_pairs={{0,6},{1,7},{2,4},{3,5},{4,2},{5,3},{6,0},{7,1},{8,14},{9,15},{10,... | collective-permute-start | bytes 786440 | tf_op jit(solution)/shard_map/ppermute | solution.py:385
  72.8 0.2 solve.9
  73.0 0.7 collective-permute-start.30
  73.7 0.7 collective-permute-start.31
  74.4 4.3 %collective-permute-done.13.refs_3_ = f32[2,128,256]{2,1,0:T(8,128)S(1)} collective-permute-done((f32[2,128,256]{2,1,0:T(8,128)S(1)}, f32[2,128,256]{2,1,0:T(8,128)S(1)}, u32[]{:S(2)}, u32[]{:S(2)}) %collective-permute-start.13) | collective-permute-done | bytes 262176 | tf_op jit(solution)/shard_map/ppermute | solution.py:385
  78.7 0.7 collective-permute-start.29
  79.4 1.3 %assemble.9.refs_2_.refs_7_ = f32[128,1024]{1,0:T(8,128)S(1)} custom-call(f32[2,128,256]{2,1,0:T(8,128)S(1)} %pad_maximum_fusion.refs_0_, f32[2,128,256]{2,1,0:T(8,128)S(1)} %collective-permute-done.11.refs_1_, f32[2,128,256]{2,1,0:T(8,128)S(1)} %collective-permute-done.12.refs_2_, f32[2,128,256]{2,1,0:T(8,128)S(1)} %collective-permute-done.13.refs_3_, ...), custom_call_target="tpu_custom_call" | custom-call | tf_op jit(solution)/shard_map/assemble/pallas_call | solution.py:207
  80.7 0.7 collective-permute-start.33
  81.4 0.7 collective-permute-start.28
  82.2 0.7 collective-permute-start.32
  82.9 0.7 collective-permute-start.35
  83.6 1.3 %collective-permute-start.38 = (f32[64,1024]{1,0:T(8,128)S(1)}, f32[64,1024]{1,0:T(8,128)S(1)}, u32[]{:S(2)}, u32[]{:S(2)}) collective-permute-start(f32[64,1024]{1,0:T(8,128)S(1)} %onward.9), channel_id=1, source_target_pairs={{8,24},{9,25},{10,26},{11,27},{12,28},{13,29},{14,30},{15,31}} | collective-permute-start | bytes 786440 | tf_op jit(solution)/shard_map/ppermute | solution.py:369
  84.9 1.3 %collective-permute-start.37 = (f32[64,1024]{1,0:T(8,128)S(1)}, f32[64,1024]{1,0:T(8,128)S(1)}, u32[]{:S(2)}, u32[]{:S(2)}) collective-permute-start(f32[64,1024]{1,0:T(8,128)S(1)} %get-tuple-element.272), channel_id=1, source_target_pairs={{16,24},{17,25},{18,26},{19,27},{20,28},{21,29},{22,30},{23,31}} | collective-permute-start | bytes 786440 | tf_op jit(solution)/shard_map/ppermute | solution.py:369
  86.3 1.3 %collective-permute-start.34 = (f32[64,1024]{1,0:T(8,128)S(1)}, f32[64,1024]{1,0:T(8,128)S(1)}, u32[]{:S(2)}, u32[]{:S(2)}) collective-permute-start(f32[64,1024]{1,0:T(8,128)S(1)} %get-tuple-element.267), channel_id=1, source_target_pairs={{16,24},{17,25},{18,26},{19,27},{20,28},{21,29},{22,30},{23,31}} | collective-permute-start | bytes 786440 | tf_op jit(solution)/shard_map/ppermute | solution.py:369
  87.6 1.3 %collective-permute-start.36 = (f32[64,1024]{1,0:T(8,128)S(1)}, f32[64,1024]{1,0:T(8,128)S(1)}, u32[]{:S(2)}, u32[]{:S(2)}) collective-permute-start(f32[64,1024]{1,0:T(8,128)S(1)} %onward.11), channel_id=1, source_target_pairs={{8,24},{9,25},{10,26},{11,27},{12,28},{13,29},{14,30},{15,31}} | collective-permute-start | bytes 786440 | tf_op jit(solution)/shard_map/ppermute | solution.py:369
  88.9 9.3 %collective-permute-done.37.refs_3_ = f32[64,1024]{1,0:T(8,128)S(1)} collective-permute-done((f32[64,1024]{1,0:T(8,128)S(1)}, f32[64,1024]{1,0:T(8,128)S(1)}, u32[]{:S(2)}, u32[]{:S(2)}) %collective-permute-start.37) | collective-permute-done | bytes 262176 | tf_op jit(solution)/shard_map/ppermute | solution.py:369
  98.2 8.0 %collective-permute-done.38.refs_4_ = f32[64,1024]{1,0:T(8,128)S(1)} collective-permute-done((f32[64,1024]{1,0:T(8,128)S(1)}, f32[64,1024]{1,0:T(8,128)S(1)}, u32[]{:S(2)}, u32[]{:S(2)}) %collective-permute-start.38) | collective-permute-done | bytes 262176 | tf_op jit(solution)/shard_map/ppermute | solution.py:369
  106.2 0.5 solve.14.refs_8_
  106.7 2.2 %collective-permute-done.34.refs_3_ = f32[64,1024]{1,0:T(8,128)S(1)} collective-permute-done((f32[64,1024]{1,0:T(8,128)S(1)}, f32[64,1024]{1,0:T(8,128)S(1)}, u32[]{:S(2)}, u32[]{:S(2)}) %collective-permute-start.34) | collective-permute-done | bytes 262176 | tf_op jit(solution)/shard_map/ppermute | solution.py:369
  108.9 2.8 %collective-permute-done.36.refs_4_ = f32[64,1024]{1,0:T(8,128)S(1)} collective-permute-done((f32[64,1024]{1,0:T(8,128)S(1)}, f32[64,1024]{1,0:T(8,128)S(1)}, u32[]{:S(2)}, u32[]{:S(2)}) %collective-permute-start.36) | collective-permute-done | bytes 262176 | tf_op jit(solution)/shard_map/ppermute | solution.py:369
  111.7 1.3 %solve.15 = f32[128,1024]{1,0:T(8,128)} custom-call(f32[128,1024]{1,0:T(8,128)S(1)} %copy-done, bf16[1024,1024]{1,0:T(8,128)(2,1)S(1)} %get-tuple-element.156.refs_1_, f32[128,1024]{1,0:T(8,128)S(1)} %assemble.9.refs_2_.refs_7_, f32[64,1024]{1,0:T(8,128)S(1)} %collective-permute-done.34.refs_3_, f32[64,1024]{1,0:T(8,128)S(1)} %collective-permute-done.36.refs_4_, ...), custom_call_target="tpu_custom_call" | custom-call | tf_op jit(solution)/shard_map/solve/pallas_call | solution.py:306
  (84 shorter events, 1.0 us)
Async XLA Ops:
  0.0 0.7 copy-start.5
  0.7 0.7 copy-start.7
  1.3 8.4 %copy-start.3 = (bf16[1,1024,1024]{2,1,0:T(8,128)(2,1)S(1)}, bf16[1,1024,1024]{2,1,0:T(8,128)(2,1)}, u32[]{:S(2)}) copy-start(bf16[1,1024,1024]{2,1,0:T(8,128)(2,1)} %param.8) | copy-start | bytes 6291460
  1.3 19.7 %copy-start.4 = (bf16[1024,1024]{1,0:T(8,128)(2,1)S(1)}, bf16[1024,1024]{1,0:T(8,128)(2,1)}, u32[]{:S(2)}) copy-start(bf16[1024,1024]{1,0:T(8,128)(2,1)} %inverse_ref) | copy-start | bytes 6291460
  4.3 5.5 %copy-start.2 = (bf16[1,1024,1024]{2,1,0:T(8,128)(2,1)S(1)}, bf16[1,1024,1024]{2,1,0:T(8,128)(2,1)}, u32[]{:S(2)}) copy-start(bf16[1,1024,1024]{2,1,0:T(8,128)(2,1)} %param.7) | copy-start | bytes 6291460
  4.3 5.5 %copy-start.6 = (s32[1,1024]{1,0:T(1,128)S(1)}, s32[1,1024]{1,0:T(1,128)}, u32[]{:S(2)}) copy-start(s32[1,1024]{1,0:T(1,128)} %index_ref.3) | copy-start | bytes 12292
  4.3 5.5 %copy-start.8 = (s32[1,4]{1,0:T(1,128)S(1)}, s32[1,4]{1,0:T(1,128)}, u32[]{:S(2)}) copy-start(s32[1,4]{1,0:T(1,128)} %owner_ref.3) | copy-start | bytes 52
  4.3 1.6 %collective-permute-start = (f32[4,72,256]{2,1,0:T(8,128)S(1)}, f32[4,72,256]{2,1,0:T(8,128)S(1)}, u32[]{:S(2)}, u32[]{:S(2)}) collective-permute-start(f32[4,72,256]{2,1,0:T(8,128)S(1)} %get-tuple-element.143), channel_id=1, source_target_pairs={{0,1},{1,0},{2,3},{3,2},{4,5},{5,4},{6,7},{7,6},{8,9},{9,8},{10,11... | collective-permute-start | bytes 884744 | tf_op jit(solution)/shard_map/ppermute | solution.py:374
  6.0 8.5 %collective-permute-start.1 = (f32[2,72,256]{2,1,0:T(8,128)S(1)}, f32[2,72,256]{2,1,0:T(8,128)S(1)}, u32[]{:S(2)}, u32[]{:S(2)}) collective-permute-start(f32[2,72,256]{2,1,0:T(8,128)S(1)} %pad_maximum_fusion.13), channel_id=1, source_target_pairs={{0,2},{1,3},{2,0},{3,1},{4,6},{5,7},{6,4},{7,5},{8,10},{9,11},{10,... | collective-permute-start | bytes 442376 | tf_op jit(solution)/shard_map/ppermute | solution.py:385
  7.6 8.8 %collective-permute-start.2 = (f32[2,72,256]{2,1,0:T(8,128)S(1)}, f32[2,72,256]{2,1,0:T(8,128)S(1)}, u32[]{:S(2)}, u32[]{:S(2)}) collective-permute-start(f32[2,72,256]{2,1,0:T(8,128)S(1)} %pad_maximum_fusion.14), channel_id=1, source_target_pairs={{0,4},{1,5},{2,6},{3,7},{4,0},{5,1},{6,2},{7,3},{8,12},{9,13},{10,... | collective-permute-start | bytes 442376 | tf_op jit(solution)/shard_map/ppermute | solution.py:385
  9.2 7.2 %collective-permute-start.3 = (f32[2,72,256]{2,1,0:T(8,128)S(1)}, f32[2,72,256]{2,1,0:T(8,128)S(1)}, u32[]{:S(2)}, u32[]{:S(2)}) collective-permute-start(f32[2,72,256]{2,1,0:T(8,128)S(1)} %pad_maximum_fusion.15), channel_id=1, source_target_pairs={{0,6},{1,7},{2,4},{3,5},{4,2},{5,3},{6,0},{7,1},{8,14},{9,15},{10,... | collective-permute-start | bytes 442376 | tf_op jit(solution)/shard_map/ppermute | solution.py:385
  9.7 11.4 %copy-start.1 = (bf16[1024,4096]{1,0:T(8,128)(2,1)S(1)}, bf16[1024,4096]{1,0:T(8,128)(2,1)}, u32[]{:S(2)}) copy-start(bf16[1024,4096]{1,0:T(8,128)(2,1)} %factor_ref) | copy-start | bytes 25165828
  17.9 4.2 %collective-permute-start.14 = (f32[4,64,256]{2,1,0:T(8,128)S(1)}, f32[4,64,256]{2,1,0:T(8,128)S(1)}, u32[]{:S(2)}, u32[]{:S(2)}) collective-permute-start(f32[4,64,256]{2,1,0:T(8,128)S(1)} %get-tuple-element.172), channel_id=1, source_target_pairs={{0,1},{1,0},{2,3},{3,2},{4,5},{5,4},{6,7},{7,6},{8,9},{9,8},{10,11... | collective-permute-start | bytes 786440 | tf_op jit(solution)/shard_map/ppermute | solution.py:374
  18.1 4.1 %collective-permute-start.6 = (f32[4,128,256]{2,1,0:T(8,128)S(1)}, f32[4,128,256]{2,1,0:T(8,128)S(1)}, u32[]{:S(2)}, u32[]{:S(2)}) collective-permute-start(f32[4,128,256]{2,1,0:T(8,128)S(1)} %get-tuple-element.162), channel_id=1, source_target_pairs={{0,1},{1,0},{2,3},{3,2},{4,5},{5,4},{6,7},{7,6},{8,9},{9,8},{10,11... | collective-permute-start | bytes 1572872 | tf_op jit(solution)/shard_map/ppermute | solution.py:374
  18.6 14.0 %collective-permute-start.5 = (f32[64,1024]{1,0:T(8,128)S(1)}, f32[64,1024]{1,0:T(8,128)S(1)}, u32[]{:S(2)}, u32[]{:S(2)}) collective-permute-start(f32[64,1024]{1,0:T(8,128)S(1)} %assemble.5.refs_2_), channel_id=1, source_target_pairs={{8,0},{24,16},{9,1},{25,17},{10,2},{26,18},{11,3},{27,19},{12,4},{... | collective-permute-start | bytes 786440 | tf_op jit(solution)/shard_map/ppermute | solution.py:369
  21.0 10.5 %collective-permute-start.19 = (f32[4,128,256]{2,1,0:T(8,128)S(1)}, f32[4,128,256]{2,1,0:T(8,128)S(1)}, u32[]{:S(2)}, u32[]{:S(2)}) collective-permute-start(f32[4,128,256]{2,1,0:T(8,128)S(1)} %get-tuple-element.200), channel_id=1, source_target_pairs={{0,1},{1,0},{2,3},{3,2},{4,5},{5,4},{6,7},{7,6},{8,9},{9,8},{10,11... | collective-permute-start | bytes 1572872 | tf_op jit(solution)/shard_map/ppermute | solution.py:374
  22.3 9.2 %collective-permute-start.7 = (f32[2,128,256]{2,1,0:T(8,128)S(1)}, f32[2,128,256]{2,1,0:T(8,128)S(1)}, u32[]{:S(2)}, u32[]{:S(2)}) collective-permute-start(f32[2,128,256]{2,1,0:T(8,128)S(1)} %get-tuple-element.163), channel_id=1, source_target_pairs={{0,2},{1,3},{2,0},{3,1},{4,6},{5,7},{6,4},{7,5},{8,10},{9,11},{10,... | collective-permute-start | bytes 786440 | tf_op jit(solution)/shard_map/ppermute | solution.py:385
  23.5 12.3 %collective-permute-start.8 = (f32[2,128,256]{2,1,0:T(8,128)S(1)}, f32[2,128,256]{2,1,0:T(8,128)S(1)}, u32[]{:S(2)}, u32[]{:S(2)}) collective-permute-start(f32[2,128,256]{2,1,0:T(8,128)S(1)} %get-tuple-element.164), channel_id=1, source_target_pairs={{0,4},{1,5},{2,6},{3,7},{4,0},{5,1},{6,2},{7,3},{8,12},{9,13},{10,... | collective-permute-start | bytes 786440 | tf_op jit(solution)/shard_map/ppermute | solution.py:385
  24.5 13.5 %collective-permute-start.9 = (f32[2,128,256]{2,1,0:T(8,128)S(1)}, f32[2,128,256]{2,1,0:T(8,128)S(1)}, u32[]{:S(2)}, u32[]{:S(2)}) collective-permute-start(f32[2,128,256]{2,1,0:T(8,128)S(1)} %pad_maximum_fusion.4), channel_id=1, source_target_pairs={{0,6},{1,7},{2,4},{3,5},{4,2},{5,3},{6,0},{7,1},{8,14},{9,15},{10,... | collective-permute-start | bytes 786440 | tf_op jit(solution)/shard_map/ppermute | solution.py:385
  31.5 27.7 %collective-permute-start.4 = (f32[4,128,256]{2,1,0:T(8,128)S(1)}, f32[4,128,256]{2,1,0:T(8,128)S(1)}, u32[]{:S(2)}, u32[]{:S(2)}) collective-permute-start(f32[4,128,256]{2,1,0:T(8,128)S(1)} %get-tuple-element.159), channel_id=1, source_target_pairs={{0,1},{1,0},{2,3},{3,2},{4,5},{5,4},{6,7},{7,6},{8,9},{9,8},{10,11... | collective-permute-start | bytes 1572872 | tf_op jit(solution)/shard_map/ppermute | solution.py:374
  31.5 10.7 %collective-permute-start.15 = (f32[2,64,256]{2,1,0:T(8,128)S(1)}, f32[2,64,256]{2,1,0:T(8,128)S(1)}, u32[]{:S(2)}, u32[]{:S(2)}) collective-permute-start(f32[2,64,256]{2,1,0:T(8,128)S(1)} %pad_maximum_fusion.17), channel_id=1, source_target_pairs={{0,2},{1,3},{2,0},{3,1},{4,6},{5,7},{6,4},{7,5},{8,10},{9,11},{10,... | collective-permute-start | bytes 393224 | tf_op jit(solution)/shard_map/ppermute | solution.py:385
  38.1 10.1 %collective-permute-start.10 = (f32[64,1024]{1,0:T(8,128)S(1)}, f32[64,1024]{1,0:T(8,128)S(1)}, u32[]{:S(2)}, u32[]{:S(2)}) collective-permute-start(f32[64,1024]{1,0:T(8,128)S(1)} %add.9), channel_id=1, source_target_pairs={{16,0},{17,1},{18,2},{19,3},{20,4},{21,5},{22,6},{23,7}} | collective-permute-start | bytes 786440 | tf_op jit(solution)/shard_map/ppermute | solution.py:369
  38.8 11.1 %copy-start = (f32[128,1024]{1,0:T(8,128)S(1)}, f32[128,1024]{1,0:T(8,128)}, u32[]{:S(2)}) copy-start(f32[128,1024]{1,0:T(8,128)} %refs_0_.15) | copy-start | bytes 1572868
  38.8 7.6 %collective-permute-start.16 = (f32[2,64,256]{2,1,0:T(8,128)S(1)}, f32[2,64,256]{2,1,0:T(8,128)S(1)}, u32[]{:S(2)}, u32[]{:S(2)}) collective-permute-start(f32[2,64,256]{2,1,0:T(8,128)S(1)} %pad_maximum_fusion.18), channel_id=1, source_target_pairs={{0,4},{1,5},{2,6},{3,7},{4,0},{5,1},{6,2},{7,3},{8,12},{9,13},{10,... | collective-permute-start | bytes 393224 | tf_op jit(solution)/shard_map/ppermute | solution.py:385
  39.4 7.8 %collective-permute-start.17 = (f32[2,64,256]{2,1,0:T(8,128)S(1)}, f32[2,64,256]{2,1,0:T(8,128)S(1)}, u32[]{:S(2)}, u32[]{:S(2)}) collective-permute-start(f32[2,64,256]{2,1,0:T(8,128)S(1)} %pad_maximum_fusion.19), channel_id=1, source_target_pairs={{0,6},{1,7},{2,4},{3,5},{4,2},{5,3},{6,0},{7,1},{8,14},{9,15},{10,... | collective-permute-start | bytes 393224 | tf_op jit(solution)/shard_map/ppermute | solution.py:385
  42.2 16.2 %collective-permute-start.23 = (f32[128,1024]{1,0:T(8,128)S(1)}, f32[128,1024]{1,0:T(8,128)S(1)}, u32[]{:S(2)}, u32[]{:S(2)}) collective-permute-start(f32[128,1024]{1,0:T(8,128)S(1)} %assemble.6.refs_6_.refs_2_), channel_id=1, source_target_pairs={{24,16},{25,17},{26,18},{27,19},{28,20},{29,21},{30,22},{31,23}} | collective-permute-start | bytes 1572872 | tf_op jit(solution)/shard_map/ppermute | solution.py:369
  46.4 8.4 %collective-permute-start.20 = (f32[2,128,256]{2,1,0:T(8,128)S(1)}, f32[2,128,256]{2,1,0:T(8,128)S(1)}, u32[]{:S(2)}, u32[]{:S(2)}) collective-permute-start(f32[2,128,256]{2,1,0:T(8,128)S(1)} %get-tuple-element.201), channel_id=1, source_target_pairs={{0,2},{1,3},{2,0},{3,1},{4,6},{5,7},{6,4},{7,5},{8,10},{9,11},{10,... | collective-permute-start | bytes 786440 | tf_op jit(solution)/shard_map/ppermute | solution.py:385
  47.2 11.2 %collective-permute-start.21 = (f32[2,128,256]{2,1,0:T(8,128)S(1)}, f32[2,128,256]{2,1,0:T(8,128)S(1)}, u32[]{:S(2)}, u32[]{:S(2)}) collective-permute-start(f32[2,128,256]{2,1,0:T(8,128)S(1)} %get-tuple-element.202), channel_id=1, source_target_pairs={{0,4},{1,5},{2,6},{3,7},{4,0},{5,1},{6,2},{7,3},{8,12},{9,13},{10,... | collective-permute-start | bytes 786440 | tf_op jit(solution)/shard_map/ppermute | solution.py:385
  48.2 10.2 %collective-permute-start.22 = (f32[2,128,256]{2,1,0:T(8,128)S(1)}, f32[2,128,256]{2,1,0:T(8,128)S(1)}, u32[]{:S(2)}, u32[]{:S(2)}) collective-permute-start(f32[2,128,256]{2,1,0:T(8,128)S(1)} %pad_maximum_fusion.11), channel_id=1, source_target_pairs={{0,6},{1,7},{2,4},{3,5},{4,2},{5,3},{6,0},{7,1},{8,14},{9,15},{10,... | collective-permute-start | bytes 786440 | tf_op jit(solution)/shard_map/ppermute | solution.py:385
  54.8 6.6 %collective-permute-start.18 = (f32[64,1024]{1,0:T(8,128)S(1)}, f32[64,1024]{1,0:T(8,128)S(1)}, u32[]{:S(2)}, u32[]{:S(2)}) collective-permute-start(f32[64,1024]{1,0:T(8,128)S(1)} %assemble.7.refs_2_), channel_id=1, source_target_pairs={{8,0},{24,16},{9,1},{25,17},{10,2},{26,18},{11,3},{27,19},{12,4},{... | collective-permute-start | bytes 786440 | tf_op jit(solution)/shard_map/ppermute | solution.py:369
  58.5 12.9 %collective-permute-start.25 = (f32[128,1024]{1,0:T(8,128)S(1)}, f32[128,1024]{1,0:T(8,128)S(1)}, u32[]{:S(2)}, u32[]{:S(2)}) collective-permute-start(f32[128,1024]{1,0:T(8,128)S(1)} %add.10), channel_id=1, source_target_pairs={{16,8},{17,9},{18,10},{19,11},{20,12},{21,13},{22,14},{23,15}} | collective-permute-start | bytes 1572872 | tf_op jit(solution)/shard_map/ppermute | solution.py:369
  59.3 4.9 %collective-permute-start.26 = (f32[64,1024]{1,0:T(8,128)S(1)}, f32[64,1024]{1,0:T(8,128)S(1)}, u32[]{:S(2)}, u32[]{:S(2)}) collective-permute-start(f32[64,1024]{1,0:T(8,128)S(1)} %get-tuple-element.219), channel_id=1, source_target_pairs={{0,8},{1,9},{2,10},{3,11},{4,12},{5,13},{6,14},{7,15}} | collective-permute-start | bytes 786440 | tf_op jit(solution)/shard_map/ppermute | solution.py:369
  61.4 11.6 %collective-permute-start.24 = (f32[64,1024]{1,0:T(8,128)S(1)}, f32[64,1024]{1,0:T(8,128)S(1)}, u32[]{:S(2)}, u32[]{:S(2)}) collective-permute-start(f32[64,1024]{1,0:T(8,128)S(1)} %add.11), channel_id=1, source_target_pairs={{16,0},{17,1},{18,2},{19,3},{20,4},{21,5},{22,6},{23,7}} | collective-permute-start | bytes 786440 | tf_op jit(solution)/shard_map/ppermute | solution.py:369
  62.1 11.6 %collective-permute-start.11 = (f32[2,128,256]{2,1,0:T(8,128)S(1)}, f32[2,128,256]{2,1,0:T(8,128)S(1)}, u32[]{:S(2)}, u32[]{:S(2)}) collective-permute-start(f32[2,128,256]{2,1,0:T(8,128)S(1)} %get-tuple-element.168), channel_id=1, source_target_pairs={{0,2},{1,3},{2,0},{3,1},{4,6},{5,7},{6,4},{7,5},{8,10},{9,11},{10,... | collective-permute-start | bytes 786440 | tf_op jit(solution)/shard_map/ppermute | solution.py:385
  63.0 11.4 %collective-permute-start.12 = (f32[2,128,256]{2,1,0:T(8,128)S(1)}, f32[2,128,256]{2,1,0:T(8,128)S(1)}, u32[]{:S(2)}, u32[]{:S(2)}) collective-permute-start(f32[2,128,256]{2,1,0:T(8,128)S(1)} %get-tuple-element.169), channel_id=1, source_target_pairs={{0,4},{1,5},{2,6},{3,7},{4,0},{5,1},{6,2},{7,3},{8,12},{9,13},{10,... | collective-permute-start | bytes 786440 | tf_op jit(solution)/shard_map/ppermute | solution.py:385
  64.2 18.0 %collective-permute-start.27 = (f32[128,1024]{1,0:T(8,128)S(1)}, f32[128,1024]{1,0:T(8,128)S(1)}, u32[]{:S(2)}, u32[]{:S(2)}) collective-permute-start(f32[128,1024]{1,0:T(8,128)S(1)} %assemble.8.refs_2_.refs_6_), channel_id=1, source_target_pairs={{24,16},{25,17},{26,18},{27,19},{28,20},{29,21},{30,22},{31,23}} | collective-permute-start | bytes 1572872 | tf_op jit(solution)/shard_map/ppermute | solution.py:369
  71.4 7.3 %collective-permute-start.13 = (f32[2,128,256]{2,1,0:T(8,128)S(1)}, f32[2,128,256]{2,1,0:T(8,128)S(1)}, u32[]{:S(2)}, u32[]{:S(2)}) collective-permute-start(f32[2,128,256]{2,1,0:T(8,128)S(1)} %pad_maximum_fusion.6), channel_id=1, source_target_pairs={{0,6},{1,7},{2,4},{3,5},{4,2},{5,3},{6,0},{7,1},{8,14},{9,15},{10,... | collective-permute-start | bytes 786440 | tf_op jit(solution)/shard_map/ppermute | solution.py:385
  73.0 8.4 %collective-permute-start.30 = (f32[64,1024]{1,0:T(8,128)S(1)}, f32[64,1024]{1,0:T(8,128)S(1)}, u32[]{:S(2)}, u32[]{:S(2)}) collective-permute-start(f32[64,1024]{1,0:T(8,128)S(1)} %onward.6), channel_id=1, source_target_pairs={{0,16},{1,17},{2,18},{3,19},{4,20},{5,21},{6,22},{7,23}} | collective-permute-start | bytes 786440 | tf_op jit(solution)/shard_map/ppermute | solution.py:369
  73.7 8.4 %collective-permute-start.31 = (f32[64,1024]{1,0:T(8,128)S(1)}, f32[64,1024]{1,0:T(8,128)S(1)}, u32[]{:S(2)}, u32[]{:S(2)}) collective-permute-start(f32[64,1024]{1,0:T(8,128)S(1)} %get-tuple-element.241), channel_id=1, source_target_pairs={{8,16},{9,17},{10,18},{11,19},{12,20},{13,21},{14,22},{15,23}} | collective-permute-start | bytes 786440 | tf_op jit(solution)/shard_map/ppermute | solution.py:369
  78.7 3.4 %collective-permute-start.29 = (f32[64,1024]{1,0:T(8,128)S(1)}, f32[64,1024]{1,0:T(8,128)S(1)}, u32[]{:S(2)}, u32[]{:S(2)}) collective-permute-start(f32[64,1024]{1,0:T(8,128)S(1)} %get-tuple-element.240), channel_id=1, source_target_pairs={{0,8},{1,9},{2,10},{3,11},{4,12},{5,13},{6,14},{7,15}} | collective-permute-start | bytes 786440 | tf_op jit(solution)/shard_map/ppermute | solution.py:369
  80.7 2.2 %collective-permute-start.33 = (f32[64,1024]{1,0:T(8,128)S(1)}, f32[64,1024]{1,0:T(8,128)S(1)}, u32[]{:S(2)}, u32[]{:S(2)}) collective-permute-start(f32[64,1024]{1,0:T(8,128)S(1)} %onward.8), channel_id=1, source_target_pairs={{0,8},{1,9},{2,10},{3,11},{4,12},{5,13},{6,14},{7,15}} | collective-permute-start | bytes 786440 | tf_op jit(solution)/shard_map/ppermute | solution.py:369
  81.4 4.8 %collective-permute-start.28 = (f32[64,1024]{1,0:T(8,128)S(1)}, f32[64,1024]{1,0:T(8,128)S(1)}, u32[]{:S(2)}, u32[]{:S(2)}) collective-permute-start(f32[64,1024]{1,0:T(8,128)S(1)} %onward.7), channel_id=1, source_target_pairs={{0,16},{1,17},{2,18},{3,19},{4,20},{5,21},{6,22},{7,23}} | collective-permute-start | bytes 786440 | tf_op jit(solution)/shard_map/ppermute | solution.py:369
  82.2 4.0 %collective-permute-start.32 = (f32[64,1024]{1,0:T(8,128)S(1)}, f32[64,1024]{1,0:T(8,128)S(1)}, u32[]{:S(2)}, u32[]{:S(2)}) collective-permute-start(f32[64,1024]{1,0:T(8,128)S(1)} %get-tuple-element.255), channel_id=1, source_target_pairs={{8,16},{9,17},{10,18},{11,19},{12,20},{13,21},{14,22},{15,23}} | collective-permute-start | bytes 786440 | tf_op jit(solution)/shard_map/ppermute | solution.py:369
  82.9 4.6 %collective-permute-start.35 = (f32[64,1024]{1,0:T(8,128)S(1)}, f32[64,1024]{1,0:T(8,128)S(1)}, u32[]{:S(2)}, u32[]{:S(2)}) collective-permute-start(f32[64,1024]{1,0:T(8,128)S(1)} %onward.10), channel_id=1, source_target_pairs={{0,8},{1,9},{2,10},{3,11},{4,12},{5,13},{6,14},{7,15}} | collective-permute-start | bytes 786440 | tf_op jit(solution)/shard_map/ppermute | solution.py:369
  83.6 22.6 %collective-permute-start.38 = (f32[64,1024]{1,0:T(8,128)S(1)}, f32[64,1024]{1,0:T(8,128)S(1)}, u32[]{:S(2)}, u32[]{:S(2)}) collective-permute-start(f32[64,1024]{1,0:T(8,128)S(1)} %onward.9), channel_id=1, source_target_pairs={{8,24},{9,25},{10,26},{11,27},{12,28},{13,29},{14,30},{15,31}} | collective-permute-start | bytes 786440 | tf_op jit(solution)/shard_map/ppermute | solution.py:369
  84.9 13.2 %collective-permute-start.37 = (f32[64,1024]{1,0:T(8,128)S(1)}, f32[64,1024]{1,0:T(8,128)S(1)}, u32[]{:S(2)}, u32[]{:S(2)}) collective-permute-start(f32[64,1024]{1,0:T(8,128)S(1)} %get-tuple-element.272), channel_id=1, source_target_pairs={{16,24},{17,25},{18,26},{19,27},{20,28},{21,29},{22,30},{23,31}} | collective-permute-start | bytes 786440 | tf_op jit(solution)/shard_map/ppermute | solution.py:369
  86.3 22.6 %collective-permute-start.34 = (f32[64,1024]{1,0:T(8,128)S(1)}, f32[64,1024]{1,0:T(8,128)S(1)}, u32[]{:S(2)}, u32[]{:S(2)}) collective-permute-start(f32[64,1024]{1,0:T(8,128)S(1)} %get-tuple-element.267), channel_id=1, source_target_pairs={{16,24},{17,25},{18,26},{19,27},{20,28},{21,29},{22,30},{23,31}} | collective-permute-start | bytes 786440 | tf_op jit(solution)/shard_map/ppermute | solution.py:369
  87.6 24.1 %collective-permute-start.36 = (f32[64,1024]{1,0:T(8,128)S(1)}, f32[64,1024]{1,0:T(8,128)S(1)}, u32[]{:S(2)}, u32[]{:S(2)}) collective-permute-start(f32[64,1024]{1,0:T(8,128)S(1)} %onward.11), channel_id=1, source_target_pairs={{8,24},{9,25},{10,26},{11,27},{12,28},{13,29},{14,30},{15,31}} | collective-permute-start | bytes 786440 | tf_op jit(solution)/shard_map/ppermute | solution.py:369

commit v5 on v4

--- a/solution.py
+++ b/solution.py
@@ -18,17 +18,18 @@
 FLOW_PARTS = (2, 1, 1, 1)
 ORDER = (
     (RELAY, 0, 1, 0),
+    (STAGE,),
     (ASSEMBLE, 1, 0),
+    (ASSEMBLE, 0, 1),
     (SOLVE, 0, 0),
-    (ASSEMBLE, 0, 1),
     (RELAY, 1, 1, 0),
     (ASSEMBLE, 2, 0),
     (PASS, 0, 2, 0),
     (RELAY, 0, 1, 1),
     (SOLVE, 1, 0),
-    (SOLVE, 0, 1),
     (PASS, 0, 2, 1),
     (ASSEMBLE, 3, 0),
+    (SOLVE, 0, 1),
     (PASS, 0, 3, 0),
     (SOLVE, 2, 0),
     (SOLVE, 1, 1),
@@ -527,6 +528,7 @@
             events[SOLVE, block, part] = functools.partial(solve, block, part)
             flowing = part if flow_parts[block] > 1 else 0
             requires[SOLVE, block, part] = [
+                (STAGE,),
                 *below,
                 *([] if block else [(ASSEMBLE, 0, p) for p in range(part + 1)]),
                 *[(RELAY, block, hop, flowing) for hop in range(1, len(hops[block]))],
@@ -552,7 +554,7 @@
 
     token_of = {}
     exchange(payloads[0], None, (PLANE, 0, 0))
-    for key in ((PAYLOAD,), (ASSEMBLE, 0, 0), (STAGE,), *ORDER):
+    for key in ((PAYLOAD,), (ASSEMBLE, 0, 0), *ORDER):
         run(key)
     for part in range(PARTS):
         run((SOLVE, count - 1, part))

time: 113 us -> 113 us (level)
    ppermute x19, starting transfers between devices: 27.7 us -> 26.5 us  [moved(): received = lax.ppermute(value, 'col', pairs)]
  transfers between devices with their start and end apart: 39 -> 39, of which waited for: 13 -> 12; matrix products, arithmetic and copies ran while one was open for 1% -> 1% of each run, Pallas kernels for 11% -> 11%
where the time goes in v5:
time: 113 us; the launch traced here: 112 us
  waiting for transfers between devices  47 us (42%)
  starting transfers between devices  44.9 us (40%)
  Pallas kernels  17.4 us (15%)
  local copies, waits for them, and re-layouts  1.68 us (1%)
    ppermute x19, starting transfers between devices, moved(): received = lax.ppermute(value, 'col', pairs)  26.5 us
    ppermute x15, waiting for transfers between devices, exchange(): received.append(lax.ppermute(value, 'rhs', pairs))  22.7 us
    ppermute x19, waiting for transfers between devices, moved(): received = lax.ppermute(value, 'col', pairs)  22.7 us
    ppermute x15, starting transfers between devices, exchange(): received.append(lax.ppermute(value, 'rhs', pairs))  17.7 us
    pallas_call x2, Pallas kernels, payload(): pl.pallas_call(functools.partial(payload_kernel, pieces, count), name='pa...  7.39 us
    pallas_call x5, Pallas kernels, assemble(): pl.pallas_call(functools.partial(assemble_kernel, block, block_size, heig...  6.88 us
  transfers between devices with their start and end apart: 39, of which 12 were waited for; matrix products, arithmetic and copies ran while one was open for 1% of the time, Pallas kernels for 11%

profile of v5, /device:TPU:24, one launch (start us, length us, event | category | flops | bytes accessed | tf_op | source)
XLA Modules:
  0.0 112.3 jit_solution(5703254843669114478)
XLA Ops:
  0.0 0.7 copy-done.4
  0.7 0.7 copy-done.6
  1.3 2.7 %payload.2 = (f32[4,72,256]{2,1,0:T(8,128)S(1)}, f32[4,72,256]{2,1,0:T(8,128)S(1)}) custom-call(s32[1,4]{1,0:T(1,128)S(1)} %copy-done.6, bf16[8,128,1024]{2,1,0:T(8,128)(2,1)} %bitcast.4, bf16[1024,1024]{1,0:T(8,128)(2,1)} %bitcast.6, s32[1,1024]{1,0:T(1,128)S(1)} %copy-done.4), custom_call_target="tpu_custom_call" | custom-call | tf_op jit(solution)/shard_map/payload/pallas_call | solution.py:149
  4.1 0.1 collective-permute-start
  4.2 1.5 %collective-permute-done = f32[4,72,256]{2,1,0:T(8,128)S(1)} collective-permute-done((f32[4,72,256]{2,1,0:T(8,128)S(1)}, f32[4,72,256]{2,1,0:T(8,128)S(1)}, u32[]{:S(2)}, u32[]{:S(2)}) %collective-permute-start) | collective-permute-done | bytes 294944 | tf_op jit(solution)/shard_map/ppermute | solution.py:375
  5.8 1.6 %collective-permute-start.1 = (f32[2,72,256]{2,1,0:T(8,128)S(1)}, f32[2,72,256]{2,1,0:T(8,128)S(1)}, u32[]{:S(2)}, u32[]{:S(2)}) collective-permute-start(f32[2,72,256]{2,1,0:T(8,128)S(1)} %pad_maximum_fusion.13), channel_id=1, source_target_pairs={{0,2},{1,3},{2,0},{3,1},{4,6},{5,7},{6,4},{7,5},{8,10},{9,11},{10,... | collective-permute-start | bytes 442376 | tf_op jit(solution)/shard_map/ppermute | solution.py:386
  7.4 1.6 %collective-permute-start.2 = (f32[2,72,256]{2,1,0:T(8,128)S(1)}, f32[2,72,256]{2,1,0:T(8,128)S(1)}, u32[]{:S(2)}, u32[]{:S(2)}) collective-permute-start(f32[2,72,256]{2,1,0:T(8,128)S(1)} %pad_maximum_fusion.14), channel_id=1, source_target_pairs={{0,4},{1,5},{2,6},{3,7},{4,0},{5,1},{6,2},{7,3},{8,12},{9,13},{10,... | collective-permute-start | bytes 442376 | tf_op jit(solution)/shard_map/ppermute | solution.py:386
  9.0 0.5 collective-permute-start.3
  9.6 4.6 %payload.3 = (f32[4,64,256]{2,1,0:T(8,128)S(1)}, f32[4,64,256]{2,1,0:T(8,128)S(1)}, f32[4,128,256]{2,1,0:T(8,128)S(1)}, f32[4,128,256]{2,1,0:T(8,128)S(1)}, f32[...) custom-call(s32[1,4]{1,0:T(1,128)S(1)} %copy-done.7, ...), custom_call_target="tpu_custom_call" | custom-call | tf_op jit(solution)/shard_map/payload/pallas_call | solution.py:149
  14.3 1.9 %collective-permute-done.2.refs_2_.refs_6_ = f32[2,72,256]{2,1,0:T(8,128)S(1)} collective-permute-done((f32[2,72,256]{2,1,0:T(8,128)S(1)}, f32[2,72,256]{2,1,0:T(8,128)S(1)}, u32[]{:S(2)}, u32[]{:S(2)}) %collective-permute-start.2) | collective-permute-done | bytes 147488 | tf_op jit(solution)/shard_map/ppermute | solution.py:386
  16.2 1.5 %assemble.5.refs_2_ = f32[64,1024]{1,0:T(8,128)S(1)} custom-call(f32[2,72,256]{2,1,0:T(8,128)S(1)} %pad_maximum_fusion.12.refs_0_.refs_4_, f32[2,72,256]{2,1,0:T(8,128)S(1)} %collective-permute-done.1.refs_1_.refs_5_, f32[2,72,256]{2,1,0:T(8,128)S(1)} %collective-permute-done.2.refs_2_.refs_6_, f32[2,72,256]{2,1,0:T(8,128)S(1)} %collective-permute-done.3.refs_3_.refs_7_, ...), custom_call_target="tpu_custom_call" | custom-call | tf_op jit(solution)/shard_map/assemble/pallas_call | solution.py:208
  17.7 0.1 collective-permute-start.14
  17.9 0.5 collective-permute-start.5
  18.4 2.5 %collective-permute-start.4 = (f32[64,1024]{1,0:T(8,128)S(1)}, f32[64,1024]{1,0:T(8,128)S(1)}, u32[]{:S(2)}, u32[]{:S(2)}) collective-permute-start(f32[64,1024]{1,0:T(8,128)S(1)} %assemble.5.refs_2_), channel_id=1, source_target_pairs={{8,0},{24,16},{9,1},{25,17},{10,2},{26,18},{11,3},{27,19},{12,4},{... | collective-permute-start | bytes 786440 | tf_op jit(solution)/shard_map/ppermute | solution.py:370
  21.0 0.1 collective-permute-start.19
  21.2 1.2 %collective-permute-start.6 = (f32[2,128,256]{2,1,0:T(8,128)S(1)}, f32[2,128,256]{2,1,0:T(8,128)S(1)}, u32[]{:S(2)}, u32[]{:S(2)}) collective-permute-start(f32[2,128,256]{2,1,0:T(8,128)S(1)} %get-tuple-element.157), channel_id=1, source_target_pairs={{0,2},{1,3},{2,0},{3,1},{4,6},{5,7},{6,4},{7,5},{8,10},{9,11},{10,... | collective-permute-start | bytes 786440 | tf_op jit(solution)/shard_map/ppermute | solution.py:386
  22.4 1.0 collective-permute-start.7
  23.4 1.5 %collective-permute-start.8 = (f32[2,128,256]{2,1,0:T(8,128)S(1)}, f32[2,128,256]{2,1,0:T(8,128)S(1)}, u32[]{:S(2)}, u32[]{:S(2)}) collective-permute-start(f32[2,128,256]{2,1,0:T(8,128)S(1)} %pad_maximum_fusion.2), channel_id=1, source_target_pairs={{0,6},{1,7},{2,4},{3,5},{4,2},{5,3},{6,0},{7,1},{8,14},{9,15},{10,... | collective-permute-start | bytes 786440 | tf_op jit(solution)/shard_map/ppermute | solution.py:386
  24.9 5.4 %collective-permute-done.6.refs_1_ = f32[2,128,256]{2,1,0:T(8,128)S(1)} collective-permute-done((f32[2,128,256]{2,1,0:T(8,128)S(1)}, f32[2,128,256]{2,1,0:T(8,128)S(1)}, u32[]{:S(2)}, u32[]{:S(2)}) %collective-permute-start.6) | collective-permute-done | bytes 262176 | tf_op jit(solution)/shard_map/ppermute | solution.py:386
  30.4 1.2 %collective-permute-start.15 = (f32[2,64,256]{2,1,0:T(8,128)S(1)}, f32[2,64,256]{2,1,0:T(8,128)S(1)}, u32[]{:S(2)}, u32[]{:S(2)}) collective-permute-start(f32[2,64,256]{2,1,0:T(8,128)S(1)} %pad_maximum_fusion.17), channel_id=1, source_target_pairs={{0,2},{1,3},{2,0},{3,1},{4,6},{5,7},{6,4},{7,5},{8,10},{9,11},{10,... | collective-permute-start | bytes 393224 | tf_op jit(solution)/shard_map/ppermute | solution.py:386
  31.6 3.2 %collective-permute-done.7.refs_2_ = f32[2,128,256]{2,1,0:T(8,128)S(1)} collective-permute-done((f32[2,128,256]{2,1,0:T(8,128)S(1)}, f32[2,128,256]{2,1,0:T(8,128)S(1)}, u32[]{:S(2)}, u32[]{:S(2)}) %collective-permute-start.7) | collective-permute-done | bytes 262176 | tf_op jit(solution)/shard_map/ppermute | solution.py:386
  34.7 2.2 %collective-permute-done.8.refs_3_ = f32[2,128,256]{2,1,0:T(8,128)S(1)} collective-permute-done((f32[2,128,256]{2,1,0:T(8,128)S(1)}, f32[2,128,256]{2,1,0:T(8,128)S(1)}, u32[]{:S(2)}, u32[]{:S(2)}) %collective-permute-start.8) | collective-permute-done | bytes 262176 | tf_op jit(solution)/shard_map/ppermute | solution.py:386
  37.0 0.7 collective-permute-start.10
  37.7 0.6 collective-permute-start.16
  38.3 1.5 %collective-permute-start.17 = (f32[2,64,256]{2,1,0:T(8,128)S(1)}, f32[2,64,256]{2,1,0:T(8,128)S(1)}, u32[]{:S(2)}, u32[]{:S(2)}) collective-permute-start(f32[2,64,256]{2,1,0:T(8,128)S(1)} %pad_maximum_fusion.19), channel_id=1, source_target_pairs={{0,6},{1,7},{2,4},{3,5},{4,2},{5,3},{6,0},{7,1},{8,14},{9,15},{10,... | collective-permute-start | bytes 393224 | tf_op jit(solution)/shard_map/ppermute | solution.py:386
  39.8 1.0 stage.1
  40.8 1.3 %assemble.6.refs_6_.refs_2_ = f32[128,1024]{1,0:T(8,128)S(1)} custom-call(f32[2,128,256]{2,1,0:T(8,128)S(1)} %pad_maximum_fusion.7.refs_0_, f32[2,128,256]{2,1,0:T(8,128)S(1)} %collective-permute-done.6.refs_1_, f32[2,128,256]{2,1,0:T(8,128)S(1)} %collective-permute-done.7.refs_2_, f32[2,128,256]{2,1,0:T(8,128)S(1)} %collective-permute-done.8.refs_3_, ...), custom_call_target="tpu_custom_call" | custom-call | tf_op jit(solution)/shard_map/assemble/pallas_call | solution.py:208
  42.1 3.0 %collective-permute-start.23 = (f32[128,1024]{1,0:T(8,128)S(1)}, f32[128,1024]{1,0:T(8,128)S(1)}, u32[]{:S(2)}, u32[]{:S(2)}) collective-permute-start(f32[128,1024]{1,0:T(8,128)S(1)} %assemble.6.refs_6_.refs_2_), channel_id=1, source_target_pairs={{24,16},{25,17},{26,18},{27,19},{28,20},{29,21},{30,22},{31,23}} | collective-permute-start | bytes 1572872 | tf_op jit(solution)/shard_map/ppermute | solution.py:370
  45.3 1.5 %collective-permute-start.20 = (f32[2,128,256]{2,1,0:T(8,128)S(1)}, f32[2,128,256]{2,1,0:T(8,128)S(1)}, u32[]{:S(2)}, u32[]{:S(2)}) collective-permute-start(f32[2,128,256]{2,1,0:T(8,128)S(1)} %get-tuple-element.201), channel_id=1, source_target_pairs={{0,2},{1,3},{2,0},{3,1},{4,6},{5,7},{6,4},{7,5},{8,10},{9,11},{10,... | collective-permute-start | bytes 786440 | tf_op jit(solution)/shard_map/ppermute | solution.py:386
  46.8 0.5 collective-permute-start.21
  47.4 1.5 %collective-permute-start.22 = (f32[2,128,256]{2,1,0:T(8,128)S(1)}, f32[2,128,256]{2,1,0:T(8,128)S(1)}, u32[]{:S(2)}, u32[]{:S(2)}) collective-permute-start(f32[2,128,256]{2,1,0:T(8,128)S(1)} %pad_maximum_fusion.11), channel_id=1, source_target_pairs={{0,6},{1,7},{2,4},{3,5},{4,2},{5,3},{6,0},{7,1},{8,14},{9,15},{10,... | collective-permute-start | bytes 786440 | tf_op jit(solution)/shard_map/ppermute | solution.py:386
  48.9 1.5 %assemble.7.refs_2_ = f32[64,1024]{1,0:T(8,128)S(1)} custom-call(f32[2,64,256]{2,1,0:T(8,128)S(1)} %pad_maximum_fusion.16.refs_0_, f32[2,64,256]{2,1,0:T(8,128)S(1)} %collective-permute-done.15.refs_1_, f32[2,64,256]{2,1,0:T(8,128)S(1)} %collective-permute-done.16.refs_2_, f32[2,64,256]{2,1,0:T(8,128)S(1)} %collective-permute-done.17.refs_3_, ...), custom_call_target="tpu_custom_call" | custom-call | tf_op jit(solution)/shard_map/assemble/pallas_call | solution.py:208
  50.5 3.8 %collective-permute-done.20.refs_1_ = f32[2,128,256]{2,1,0:T(8,128)S(1)} collective-permute-done((f32[2,128,256]{2,1,0:T(8,128)S(1)}, f32[2,128,256]{2,1,0:T(8,128)S(1)}, u32[]{:S(2)}, u32[]{:S(2)}) %collective-permute-start.20) | collective-permute-done | bytes 262176 | tf_op jit(solution)/shard_map/ppermute | solution.py:386
  54.2 1.8 %collective-permute-start.18 = (f32[64,1024]{1,0:T(8,128)S(1)}, f32[64,1024]{1,0:T(8,128)S(1)}, u32[]{:S(2)}, u32[]{:S(2)}) collective-permute-start(f32[64,1024]{1,0:T(8,128)S(1)} %assemble.7.refs_2_), channel_id=1, source_target_pairs={{8,0},{24,16},{9,1},{25,17},{10,2},{26,18},{11,3},{27,19},{12,4},{... | collective-permute-start | bytes 786440 | tf_op jit(solution)/shard_map/ppermute | solution.py:370
  56.1 2.1 %collective-permute-done.21.refs_2_ = f32[2,128,256]{2,1,0:T(8,128)S(1)} collective-permute-done((f32[2,128,256]{2,1,0:T(8,128)S(1)}, f32[2,128,256]{2,1,0:T(8,128)S(1)}, u32[]{:S(2)}, u32[]{:S(2)}) %collective-permute-start.21) | collective-permute-done | bytes 262176 | tf_op jit(solution)/shard_map/ppermute | solution.py:386
  58.2 0.1 add.10
  58.3 0.7 collective-permute-start.25
  59.0 0.7 collective-permute-start.26
  59.8 1.3 %assemble.8.refs_2_.refs_6_ = f32[128,1024]{1,0:T(8,128)S(1)} custom-call(f32[2,128,256]{2,1,0:T(8,128)S(1)} %pad_maximum_fusion.8.refs_0_, f32[2,128,256]{2,1,0:T(8,128)S(1)} %collective-permute-done.20.refs_1_, f32[2,128,256]{2,1,0:T(8,128)S(1)} %collective-permute-done.21.refs_2_, f32[2,128,256]{2,1,0:T(8,128)S(1)} %collective-permute-done.22.refs_3_, ...), custom_call_target="tpu_custom_call" | custom-call | tf_op jit(solution)/shard_map/assemble/pallas_call | solution.py:208
  61.2 0.7 collective-permute-start.24
  61.9 0.7 collective-permute-start.11
  62.6 1.2 %collective-permute-start.12 = (f32[2,128,256]{2,1,0:T(8,128)S(1)}, f32[2,128,256]{2,1,0:T(8,128)S(1)}, u32[]{:S(2)}, u32[]{:S(2)}) collective-permute-start(f32[2,128,256]{2,1,0:T(8,128)S(1)} %get-tuple-element.169), channel_id=1, source_target_pairs={{0,4},{1,5},{2,6},{3,7},{4,0},{5,1},{6,2},{7,3},{8,12},{9,13},{10,... | collective-permute-start | bytes 786440 | tf_op jit(solution)/shard_map/ppermute | solution.py:386
  63.8 6.5 %collective-permute-start.27 = (f32[128,1024]{1,0:T(8,128)S(1)}, f32[128,1024]{1,0:T(8,128)S(1)}, u32[]{:S(2)}, u32[]{:S(2)}) collective-permute-start(f32[128,1024]{1,0:T(8,128)S(1)} %assemble.8.refs_2_.refs_6_), channel_id=1, source_target_pairs={{24,16},{25,17},{26,18},{27,19},{28,20},{29,21},{30,22},{31,23}} | collective-permute-start | bytes 1572872 | tf_op jit(solution)/shard_map/ppermute | solution.py:370
  70.3 1.6 %collective-permute-start.13 = (f32[2,128,256]{2,1,0:T(8,128)S(1)}, f32[2,128,256]{2,1,0:T(8,128)S(1)}, u32[]{:S(2)}, u32[]{:S(2)}) collective-permute-start(f32[2,128,256]{2,1,0:T(8,128)S(1)} %pad_maximum_fusion.6), channel_id=1, source_target_pairs={{0,6},{1,7},{2,4},{3,5},{4,2},{5,3},{6,0},{7,1},{8,14},{9,15},{10,... | collective-permute-start | bytes 786440 | tf_op jit(solution)/shard_map/ppermute | solution.py:386
  71.9 0.2 solve.9
  72.1 0.7 collective-permute-start.30
  72.9 0.7 collective-permute-start.31
  73.6 4.1 %collective-permute-done.13.refs_3_ = f32[2,128,256]{2,1,0:T(8,128)S(1)} collective-permute-done((f32[2,128,256]{2,1,0:T(8,128)S(1)}, f32[2,128,256]{2,1,0:T(8,128)S(1)}, u32[]{:S(2)}, u32[]{:S(2)}) %collective-permute-start.13) | collective-permute-done | bytes 262176 | tf_op jit(solution)/shard_map/ppermute | solution.py:386
  77.6 0.7 collective-permute-start.29
  78.3 1.3 %assemble.9.refs_2_.refs_7_ = f32[128,1024]{1,0:T(8,128)S(1)} custom-call(f32[2,128,256]{2,1,0:T(8,128)S(1)} %pad_maximum_fusion.3.refs_0_, f32[2,128,256]{2,1,0:T(8,128)S(1)} %collective-permute-done.11.refs_1_, f32[2,128,256]{2,1,0:T(8,128)S(1)} %collective-permute-done.12.refs_2_, f32[2,128,256]{2,1,0:T(8,128)S(1)} %collective-permute-done.13.refs_3_, ...), custom_call_target="tpu_custom_call" | custom-call | tf_op jit(solution)/shard_map/assemble/pallas_call | solution.py:208
  79.6 0.7 collective-permute-start.33
  80.3 0.7 collective-permute-start.28
  81.1 0.7 collective-permute-start.32
  81.8 0.7 collective-permute-start.35
  82.5 1.3 %collective-permute-start.38 = (f32[64,1024]{1,0:T(8,128)S(1)}, f32[64,1024]{1,0:T(8,128)S(1)}, u32[]{:S(2)}, u32[]{:S(2)}) collective-permute-start(f32[64,1024]{1,0:T(8,128)S(1)} %onward.9), channel_id=1, source_target_pairs={{8,24},{9,25},{10,26},{11,27},{12,28},{13,29},{14,30},{15,31}} | collective-permute-start | bytes 786440 | tf_op jit(solution)/shard_map/ppermute | solution.py:370
  83.8 1.3 %collective-permute-start.37 = (f32[64,1024]{1,0:T(8,128)S(1)}, f32[64,1024]{1,0:T(8,128)S(1)}, u32[]{:S(2)}, u32[]{:S(2)}) collective-permute-start(f32[64,1024]{1,0:T(8,128)S(1)} %get-tuple-element.272), channel_id=1, source_target_pairs={{16,24},{17,25},{18,26},{19,27},{20,28},{21,29},{22,30},{23,31}} | collective-permute-start | bytes 786440 | tf_op jit(solution)/shard_map/ppermute | solution.py:370
  85.2 1.3 %collective-permute-start.34 = (f32[64,1024]{1,0:T(8,128)S(1)}, f32[64,1024]{1,0:T(8,128)S(1)}, u32[]{:S(2)}, u32[]{:S(2)}) collective-permute-start(f32[64,1024]{1,0:T(8,128)S(1)} %get-tuple-element.267), channel_id=1, source_target_pairs={{16,24},{17,25},{18,26},{19,27},{20,28},{21,29},{22,30},{23,31}} | collective-permute-start | bytes 786440 | tf_op jit(solution)/shard_map/ppermute | solution.py:370
  86.5 1.3 %collective-permute-start.36 = (f32[64,1024]{1,0:T(8,128)S(1)}, f32[64,1024]{1,0:T(8,128)S(1)}, u32[]{:S(2)}, u32[]{:S(2)}) collective-permute-start(f32[64,1024]{1,0:T(8,128)S(1)} %onward.11), channel_id=1, source_target_pairs={{8,24},{9,25},{10,26},{11,27},{12,28},{13,29},{14,30},{15,31}} | collective-permute-start | bytes 786440 | tf_op jit(solution)/shard_map/ppermute | solution.py:370
  87.8 11.4 %collective-permute-done.37.refs_3_ = f32[64,1024]{1,0:T(8,128)S(1)} collective-permute-done((f32[64,1024]{1,0:T(8,128)S(1)}, f32[64,1024]{1,0:T(8,128)S(1)}, u32[]{:S(2)}, u32[]{:S(2)}) %collective-permute-start.37) | collective-permute-done | bytes 262176 | tf_op jit(solution)/shard_map/ppermute | solution.py:370
  99.2 6.2 %collective-permute-done.38.refs_4_ = f32[64,1024]{1,0:T(8,128)S(1)} collective-permute-done((f32[64,1024]{1,0:T(8,128)S(1)}, f32[64,1024]{1,0:T(8,128)S(1)}, u32[]{:S(2)}, u32[]{:S(2)}) %collective-permute-start.38) | collective-permute-done | bytes 262176 | tf_op jit(solution)/shard_map/ppermute | solution.py:370
  105.4 0.5 solve.14.refs_8_
  105.9 2.3 %collective-permute-done.34.refs_3_ = f32[64,1024]{1,0:T(8,128)S(1)} collective-permute-done((f32[64,1024]{1,0:T(8,128)S(1)}, f32[64,1024]{1,0:T(8,128)S(1)}, u32[]{:S(2)}, u32[]{:S(2)}) %collective-permute-start.34) | collective-permute-done | bytes 262176 | tf_op jit(solution)/shard_map/ppermute | solution.py:370
  108.2 2.8 %collective-permute-done.36.refs_4_ = f32[64,1024]{1,0:T(8,128)S(1)} collective-permute-done((f32[64,1024]{1,0:T(8,128)S(1)}, f32[64,1024]{1,0:T(8,128)S(1)}, u32[]{:S(2)}, u32[]{:S(2)}) %collective-permute-start.36) | collective-permute-done | bytes 262176 | tf_op jit(solution)/shard_map/ppermute | solution.py:370
  111.0 1.3 %solve.15 = f32[128,1024]{1,0:T(8,128)} custom-call(f32[128,1024]{1,0:T(8,128)S(1)} %copy-done, bf16[1024,1024]{1,0:T(8,128)(2,1)S(1)} %get-tuple-element.164.refs_1_, f32[128,1024]{1,0:T(8,128)S(1)} %assemble.9.refs_2_.refs_7_, f32[64,1024]{1,0:T(8,128)S(1)} %collective-permute-done.34.refs_3_, f32[64,1024]{1,0:T(8,128)S(1)} %collective-permute-done.36.refs_4_, ...), custom_call_target="tpu_custom_call" | custom-call | tf_op jit(solution)/shard_map/solve/pallas_call | solution.py:307
  (87 shorter events, 1.0 us)
Async XLA Ops:
  0.0 0.7 copy-start.4
  0.7 0.7 copy-start.6
  1.3 8.2 %copy-start.2 = (bf16[1,1024,1024]{2,1,0:T(8,128)(2,1)S(1)}, bf16[1,1024,1024]{2,1,0:T(8,128)(2,1)}, u32[]{:S(2)}) copy-start(bf16[1,1024,1024]{2,1,0:T(8,128)(2,1)} %param.8) | copy-start | bytes 6291460
  4.1 5.5 %copy-start.1 = (bf16[1,1024,1024]{2,1,0:T(8,128)(2,1)S(1)}, bf16[1,1024,1024]{2,1,0:T(8,128)(2,1)}, u32[]{:S(2)}) copy-start(bf16[1,1024,1024]{2,1,0:T(8,128)(2,1)} %param.7) | copy-start | bytes 6291460
  4.1 5.5 %copy-start.5 = (s32[1,1024]{1,0:T(1,128)S(1)}, s32[1,1024]{1,0:T(1,128)}, u32[]{:S(2)}) copy-start(s32[1,1024]{1,0:T(1,128)} %index_ref.3) | copy-start | bytes 12292
  4.1 5.5 %copy-start.7 = (s32[1,4]{1,0:T(1,128)S(1)}, s32[1,4]{1,0:T(1,128)}, u32[]{:S(2)}) copy-start(s32[1,4]{1,0:T(1,128)} %owner_ref.3) | copy-start | bytes 52
  4.1 1.6 %collective-permute-start = (f32[4,72,256]{2,1,0:T(8,128)S(1)}, f32[4,72,256]{2,1,0:T(8,128)S(1)}, u32[]{:S(2)}, u32[]{:S(2)}) collective-permute-start(f32[4,72,256]{2,1,0:T(8,128)S(1)} %get-tuple-element.143), channel_id=1, source_target_pairs={{0,1},{1,0},{2,3},{3,2},{4,5},{5,4},{6,7},{7,6},{8,9},{9,8},{10,11... | collective-permute-start | bytes 884744 | tf_op jit(solution)/shard_map/ppermute | solution.py:375
  5.8 8.5 %collective-permute-start.1 = (f32[2,72,256]{2,1,0:T(8,128)S(1)}, f32[2,72,256]{2,1,0:T(8,128)S(1)}, u32[]{:S(2)}, u32[]{:S(2)}) collective-permute-start(f32[2,72,256]{2,1,0:T(8,128)S(1)} %pad_maximum_fusion.13), channel_id=1, source_target_pairs={{0,2},{1,3},{2,0},{3,1},{4,6},{5,7},{6,4},{7,5},{8,10},{9,11},{10,... | collective-permute-start | bytes 442376 | tf_op jit(solution)/shard_map/ppermute | solution.py:386
  7.4 8.8 %collective-permute-start.2 = (f32[2,72,256]{2,1,0:T(8,128)S(1)}, f32[2,72,256]{2,1,0:T(8,128)S(1)}, u32[]{:S(2)}, u32[]{:S(2)}) collective-permute-start(f32[2,72,256]{2,1,0:T(8,128)S(1)} %pad_maximum_fusion.14), channel_id=1, source_target_pairs={{0,4},{1,5},{2,6},{3,7},{4,0},{5,1},{6,2},{7,3},{8,12},{9,13},{10,... | collective-permute-start | bytes 442376 | tf_op jit(solution)/shard_map/ppermute | solution.py:386
  9.0 30.8 %slice-start = ((s8[8388608]{0:T(1024)(128)(4,1)}), s8[4194304]{0:T(1024)(128)(4,1)S(1)}, s32[]{:S(2)}) async-start(s8[8388608]{0:T(1024)(128)(4,1)} %bitcast.2), calls=%async_computation | async-start | bytes 8388608
  9.0 7.2 %collective-permute-start.3 = (f32[2,72,256]{2,1,0:T(8,128)S(1)}, f32[2,72,256]{2,1,0:T(8,128)S(1)}, u32[]{:S(2)}, u32[]{:S(2)}) collective-permute-start(f32[2,72,256]{2,1,0:T(8,128)S(1)} %pad_maximum_fusion.15), channel_id=1, source_target_pairs={{0,6},{1,7},{2,4},{3,5},{4,2},{5,3},{6,0},{7,1},{8,14},{9,15},{10,... | collective-permute-start | bytes 442376 | tf_op jit(solution)/shard_map/ppermute | solution.py:386
  17.7 3.3 %collective-permute-start.14 = (f32[4,64,256]{2,1,0:T(8,128)S(1)}, f32[4,64,256]{2,1,0:T(8,128)S(1)}, u32[]{:S(2)}, u32[]{:S(2)}) collective-permute-start(f32[4,64,256]{2,1,0:T(8,128)S(1)} %get-tuple-element.172), channel_id=1, source_target_pairs={{0,1},{1,0},{2,3},{3,2},{4,5},{5,4},{6,7},{7,6},{8,9},{9,8},{10,11... | collective-permute-start | bytes 786440 | tf_op jit(solution)/shard_map/ppermute | solution.py:375
  17.8 22.0 %slice-start.1 = ((s8[8388608]{0:T(1024)(128)(4,1)}), s8[4194304]{0:T(1024)(128)(4,1)S(1)}, s32[]{:S(2)}) async-start(s8[8388608]{0:T(1024)(128)(4,1)} %bitcast.2), calls=%async_computation.1 | async-start | bytes 8388608
  17.9 3.2 %collective-permute-start.5 = (f32[4,128,256]{2,1,0:T(8,128)S(1)}, f32[4,128,256]{2,1,0:T(8,128)S(1)}, u32[]{:S(2)}, u32[]{:S(2)}) collective-permute-start(f32[4,128,256]{2,1,0:T(8,128)S(1)} %get-tuple-element.156), channel_id=1, source_target_pairs={{0,1},{1,0},{2,3},{3,2},{4,5},{5,4},{6,7},{7,6},{8,9},{9,8},{10,11... | collective-permute-start | bytes 1572872 | tf_op jit(solution)/shard_map/ppermute | solution.py:375
  18.4 13.1 %collective-permute-start.4 = (f32[64,1024]{1,0:T(8,128)S(1)}, f32[64,1024]{1,0:T(8,128)S(1)}, u32[]{:S(2)}, u32[]{:S(2)}) collective-permute-start(f32[64,1024]{1,0:T(8,128)S(1)} %assemble.5.refs_2_), channel_id=1, source_target_pairs={{8,0},{24,16},{9,1},{25,17},{10,2},{26,18},{11,3},{27,19},{12,4},{... | collective-permute-start | bytes 786440 | tf_op jit(solution)/shard_map/ppermute | solution.py:370
  21.0 9.4 %collective-permute-start.19 = (f32[4,128,256]{2,1,0:T(8,128)S(1)}, f32[4,128,256]{2,1,0:T(8,128)S(1)}, u32[]{:S(2)}, u32[]{:S(2)}) collective-permute-start(f32[4,128,256]{2,1,0:T(8,128)S(1)} %get-tuple-element.200), channel_id=1, source_target_pairs={{0,1},{1,0},{2,3},{3,2},{4,5},{5,4},{6,7},{7,6},{8,9},{9,8},{10,11... | collective-permute-start | bytes 1572872 | tf_op jit(solution)/shard_map/ppermute | solution.py:375
  21.1 18.7 %copy-start.3 = (bf16[1024,1024]{1,0:T(8,128)(2,1)S(1)}, bf16[1024,1024]{1,0:T(8,128)(2,1)}, u32[]{:S(2)}) copy-start(bf16[1024,1024]{1,0:T(8,128)(2,1)} %inverse_ref) | copy-start | bytes 6291460
  21.2 9.2 %collective-permute-start.6 = (f32[2,128,256]{2,1,0:T(8,128)S(1)}, f32[2,128,256]{2,1,0:T(8,128)S(1)}, u32[]{:S(2)}, u32[]{:S(2)}) collective-permute-start(f32[2,128,256]{2,1,0:T(8,128)S(1)} %get-tuple-element.157), channel_id=1, source_target_pairs={{0,2},{1,3},{2,0},{3,1},{4,6},{5,7},{6,4},{7,5},{8,10},{9,11},{10,... | collective-permute-start | bytes 786440 | tf_op jit(solution)/shard_map/ppermute | solution.py:386
  22.4 12.3 %collective-permute-start.7 = (f32[2,128,256]{2,1,0:T(8,128)S(1)}, f32[2,128,256]{2,1,0:T(8,128)S(1)}, u32[]{:S(2)}, u32[]{:S(2)}) collective-permute-start(f32[2,128,256]{2,1,0:T(8,128)S(1)} %get-tuple-element.158), channel_id=1, source_target_pairs={{0,4},{1,5},{2,6},{3,7},{4,0},{5,1},{6,2},{7,3},{8,12},{9,13},{10,... | collective-permute-start | bytes 786440 | tf_op jit(solution)/shard_map/ppermute | solution.py:386
  23.4 13.5 %collective-permute-start.8 = (f32[2,128,256]{2,1,0:T(8,128)S(1)}, f32[2,128,256]{2,1,0:T(8,128)S(1)}, u32[]{:S(2)}, u32[]{:S(2)}) collective-permute-start(f32[2,128,256]{2,1,0:T(8,128)S(1)} %pad_maximum_fusion.2), channel_id=1, source_target_pairs={{0,6},{1,7},{2,4},{3,5},{4,2},{5,3},{6,0},{7,1},{8,14},{9,15},{10,... | collective-permute-start | bytes 786440 | tf_op jit(solution)/shard_map/ppermute | solution.py:386
  30.4 28.6 %collective-permute-start.9 = (f32[4,128,256]{2,1,0:T(8,128)S(1)}, f32[4,128,256]{2,1,0:T(8,128)S(1)}, u32[]{:S(2)}, u32[]{:S(2)}) collective-permute-start(f32[4,128,256]{2,1,0:T(8,128)S(1)} %get-tuple-element.167), channel_id=1, source_target_pairs={{0,1},{1,0},{2,3},{3,2},{4,5},{5,4},{6,7},{7,6},{8,9},{9,8},{10,11... | collective-permute-start | bytes 1572872 | tf_op jit(solution)/shard_map/ppermute | solution.py:375
  30.4 11.7 %collective-permute-start.15 = (f32[2,64,256]{2,1,0:T(8,128)S(1)}, f32[2,64,256]{2,1,0:T(8,128)S(1)}, u32[]{:S(2)}, u32[]{:S(2)}) collective-permute-start(f32[2,64,256]{2,1,0:T(8,128)S(1)} %pad_maximum_fusion.17), channel_id=1, source_target_pairs={{0,2},{1,3},{2,0},{3,1},{4,6},{5,7},{6,4},{7,5},{8,10},{9,11},{10,... | collective-permute-start | bytes 393224 | tf_op jit(solution)/shard_map/ppermute | solution.py:386
  37.0 10.4 %collective-permute-start.10 = (f32[64,1024]{1,0:T(8,128)S(1)}, f32[64,1024]{1,0:T(8,128)S(1)}, u32[]{:S(2)}, u32[]{:S(2)}) collective-permute-start(f32[64,1024]{1,0:T(8,128)S(1)} %add.9), channel_id=1, source_target_pairs={{16,0},{17,1},{18,2},{19,3},{20,4},{21,5},{22,6},{23,7}} | collective-permute-start | bytes 786440 | tf_op jit(solution)/shard_map/ppermute | solution.py:370
  37.7 7.6 %collective-permute-start.16 = (f32[2,64,256]{2,1,0:T(8,128)S(1)}, f32[2,64,256]{2,1,0:T(8,128)S(1)}, u32[]{:S(2)}, u32[]{:S(2)}) collective-permute-start(f32[2,64,256]{2,1,0:T(8,128)S(1)} %pad_maximum_fusion.18), channel_id=1, source_target_pairs={{0,4},{1,5},{2,6},{3,7},{4,0},{5,1},{6,2},{7,3},{8,12},{9,13},{10,... | collective-permute-start | bytes 393224 | tf_op jit(solution)/shard_map/ppermute | solution.py:386
  38.3 8.5 %collective-permute-start.17 = (f32[2,64,256]{2,1,0:T(8,128)S(1)}, f32[2,64,256]{2,1,0:T(8,128)S(1)}, u32[]{:S(2)}, u32[]{:S(2)}) collective-permute-start(f32[2,64,256]{2,1,0:T(8,128)S(1)} %pad_maximum_fusion.19), channel_id=1, source_target_pairs={{0,6},{1,7},{2,4},{3,5},{4,2},{5,3},{6,0},{7,1},{8,14},{9,15},{10,... | collective-permute-start | bytes 393224 | tf_op jit(solution)/shard_map/ppermute | solution.py:386
  42.1 16.1 %collective-permute-start.23 = (f32[128,1024]{1,0:T(8,128)S(1)}, f32[128,1024]{1,0:T(8,128)S(1)}, u32[]{:S(2)}, u32[]{:S(2)}) collective-permute-start(f32[128,1024]{1,0:T(8,128)S(1)} %assemble.6.refs_6_.refs_2_), channel_id=1, source_target_pairs={{24,16},{25,17},{26,18},{27,19},{28,20},{29,21},{30,22},{31,23}} | collective-permute-start | bytes 1572872 | tf_op jit(solution)/shard_map/ppermute | solution.py:370
  45.2 5.2 %copy-start = (f32[128,1024]{1,0:T(8,128)S(1)}, f32[128,1024]{1,0:T(8,128)}, u32[]{:S(2)}) copy-start(f32[128,1024]{1,0:T(8,128)} %refs_0_.15) | copy-start | bytes 1572868
  45.3 9.0 %collective-permute-start.20 = (f32[2,128,256]{2,1,0:T(8,128)S(1)}, f32[2,128,256]{2,1,0:T(8,128)S(1)}, u32[]{:S(2)}, u32[]{:S(2)}) collective-permute-start(f32[2,128,256]{2,1,0:T(8,128)S(1)} %get-tuple-element.201), channel_id=1, source_target_pairs={{0,2},{1,3},{2,0},{3,1},{4,6},{5,7},{6,4},{7,5},{8,10},{9,11},{10,... | collective-permute-start | bytes 786440 | tf_op jit(solution)/shard_map/ppermute | solution.py:386
  46.8 11.4 %collective-permute-start.21 = (f32[2,128,256]{2,1,0:T(8,128)S(1)}, f32[2,128,256]{2,1,0:T(8,128)S(1)}, u32[]{:S(2)}, u32[]{:S(2)}) collective-permute-start(f32[2,128,256]{2,1,0:T(8,128)S(1)} %get-tuple-element.202), channel_id=1, source_target_pairs={{0,4},{1,5},{2,6},{3,7},{4,0},{5,1},{6,2},{7,3},{8,12},{9,13},{10,... | collective-permute-start | bytes 786440 | tf_op jit(solution)/shard_map/ppermute | solution.py:386
  47.4 10.9 %collective-permute-start.22 = (f32[2,128,256]{2,1,0:T(8,128)S(1)}, f32[2,128,256]{2,1,0:T(8,128)S(1)}, u32[]{:S(2)}, u32[]{:S(2)}) collective-permute-start(f32[2,128,256]{2,1,0:T(8,128)S(1)} %pad_maximum_fusion.11), channel_id=1, source_target_pairs={{0,6},{1,7},{2,4},{3,5},{4,2},{5,3},{6,0},{7,1},{8,14},{9,15},{10,... | collective-permute-start | bytes 786440 | tf_op jit(solution)/shard_map/ppermute | solution.py:386
  54.2 6.9 %collective-permute-start.18 = (f32[64,1024]{1,0:T(8,128)S(1)}, f32[64,1024]{1,0:T(8,128)S(1)}, u32[]{:S(2)}, u32[]{:S(2)}) collective-permute-start(f32[64,1024]{1,0:T(8,128)S(1)} %assemble.7.refs_2_), channel_id=1, source_target_pairs={{8,0},{24,16},{9,1},{25,17},{10,2},{26,18},{11,3},{27,19},{12,4},{... | collective-permute-start | bytes 786440 | tf_op jit(solution)/shard_map/ppermute | solution.py:370
  58.3 12.0 %collective-permute-start.25 = (f32[128,1024]{1,0:T(8,128)S(1)}, f32[128,1024]{1,0:T(8,128)S(1)}, u32[]{:S(2)}, u32[]{:S(2)}) collective-permute-start(f32[128,1024]{1,0:T(8,128)S(1)} %add.10), channel_id=1, source_target_pairs={{16,8},{17,9},{18,10},{19,11},{20,12},{21,13},{22,14},{23,15}} | collective-permute-start | bytes 1572872 | tf_op jit(solution)/shard_map/ppermute | solution.py:370
  59.0 4.8 %collective-permute-start.26 = (f32[64,1024]{1,0:T(8,128)S(1)}, f32[64,1024]{1,0:T(8,128)S(1)}, u32[]{:S(2)}, u32[]{:S(2)}) collective-permute-start(f32[64,1024]{1,0:T(8,128)S(1)} %get-tuple-element.219), channel_id=1, source_target_pairs={{0,8},{1,9},{2,10},{3,11},{4,12},{5,13},{6,14},{7,15}} | collective-permute-start | bytes 786440 | tf_op jit(solution)/shard_map/ppermute | solution.py:370
  61.2 11.0 %collective-permute-start.24 = (f32[64,1024]{1,0:T(8,128)S(1)}, f32[64,1024]{1,0:T(8,128)S(1)}, u32[]{:S(2)}, u32[]{:S(2)}) collective-permute-start(f32[64,1024]{1,0:T(8,128)S(1)} %add.11), channel_id=1, source_target_pairs={{16,0},{17,1},{18,2},{19,3},{20,4},{21,5},{22,6},{23,7}} | collective-permute-start | bytes 786440 | tf_op jit(solution)/shard_map/ppermute | solution.py:370
  61.9 11.0 %collective-permute-start.11 = (f32[2,128,256]{2,1,0:T(8,128)S(1)}, f32[2,128,256]{2,1,0:T(8,128)S(1)}, u32[]{:S(2)}, u32[]{:S(2)}) collective-permute-start(f32[2,128,256]{2,1,0:T(8,128)S(1)} %get-tuple-element.168), channel_id=1, source_target_pairs={{0,2},{1,3},{2,0},{3,1},{4,6},{5,7},{6,4},{7,5},{8,10},{9,11},{10,... | collective-permute-start | bytes 786440 | tf_op jit(solution)/shard_map/ppermute | solution.py:386
  62.6 11.0 %collective-permute-start.12 = (f32[2,128,256]{2,1,0:T(8,128)S(1)}, f32[2,128,256]{2,1,0:T(8,128)S(1)}, u32[]{:S(2)}, u32[]{:S(2)}) collective-permute-start(f32[2,128,256]{2,1,0:T(8,128)S(1)} %get-tuple-element.169), channel_id=1, source_target_pairs={{0,4},{1,5},{2,6},{3,7},{4,0},{5,1},{6,2},{7,3},{8,12},{9,13},{10,... | collective-permute-start | bytes 786440 | tf_op jit(solution)/shard_map/ppermute | solution.py:386
  63.8 17.2 %collective-permute-start.27 = (f32[128,1024]{1,0:T(8,128)S(1)}, f32[128,1024]{1,0:T(8,128)S(1)}, u32[]{:S(2)}, u32[]{:S(2)}) collective-permute-start(f32[128,1024]{1,0:T(8,128)S(1)} %assemble.8.refs_2_.refs_6_), channel_id=1, source_target_pairs={{24,16},{25,17},{26,18},{27,19},{28,20},{29,21},{30,22},{31,23}} | collective-permute-start | bytes 1572872 | tf_op jit(solution)/shard_map/ppermute | solution.py:370
  70.3 7.3 %collective-permute-start.13 = (f32[2,128,256]{2,1,0:T(8,128)S(1)}, f32[2,128,256]{2,1,0:T(8,128)S(1)}, u32[]{:S(2)}, u32[]{:S(2)}) collective-permute-start(f32[2,128,256]{2,1,0:T(8,128)S(1)} %pad_maximum_fusion.6), channel_id=1, source_target_pairs={{0,6},{1,7},{2,4},{3,5},{4,2},{5,3},{6,0},{7,1},{8,14},{9,15},{10,... | collective-permute-start | bytes 786440 | tf_op jit(solution)/shard_map/ppermute | solution.py:386
  72.1 8.2 %collective-permute-start.30 = (f32[64,1024]{1,0:T(8,128)S(1)}, f32[64,1024]{1,0:T(8,128)S(1)}, u32[]{:S(2)}, u32[]{:S(2)}) collective-permute-start(f32[64,1024]{1,0:T(8,128)S(1)} %onward.6), channel_id=1, source_target_pairs={{0,16},{1,17},{2,18},{3,19},{4,20},{5,21},{6,22},{7,23}} | collective-permute-start | bytes 786440 | tf_op jit(solution)/shard_map/ppermute | solution.py:370
  72.9 8.2 %collective-permute-start.31 = (f32[64,1024]{1,0:T(8,128)S(1)}, f32[64,1024]{1,0:T(8,128)S(1)}, u32[]{:S(2)}, u32[]{:S(2)}) collective-permute-start(f32[64,1024]{1,0:T(8,128)S(1)} %get-tuple-element.241), channel_id=1, source_target_pairs={{8,16},{9,17},{10,18},{11,19},{12,20},{13,21},{14,22},{15,23}} | collective-permute-start | bytes 786440 | tf_op jit(solution)/shard_map/ppermute | solution.py:370
  77.6 3.4 %collective-permute-start.29 = (f32[64,1024]{1,0:T(8,128)S(1)}, f32[64,1024]{1,0:T(8,128)S(1)}, u32[]{:S(2)}, u32[]{:S(2)}) collective-permute-start(f32[64,1024]{1,0:T(8,128)S(1)} %get-tuple-element.240), channel_id=1, source_target_pairs={{0,8},{1,9},{2,10},{3,11},{4,12},{5,13},{6,14},{7,15}} | collective-permute-start | bytes 786440 | tf_op jit(solution)/shard_map/ppermute | solution.py:370
  79.6 2.2 %collective-permute-start.33 = (f32[64,1024]{1,0:T(8,128)S(1)}, f32[64,1024]{1,0:T(8,128)S(1)}, u32[]{:S(2)}, u32[]{:S(2)}) collective-permute-start(f32[64,1024]{1,0:T(8,128)S(1)} %onward.8), channel_id=1, source_target_pairs={{0,8},{1,9},{2,10},{3,11},{4,12},{5,13},{6,14},{7,15}} | collective-permute-start | bytes 786440 | tf_op jit(solution)/shard_map/ppermute | solution.py:370
  80.3 4.8 %collective-permute-start.28 = (f32[64,1024]{1,0:T(8,128)S(1)}, f32[64,1024]{1,0:T(8,128)S(1)}, u32[]{:S(2)}, u32[]{:S(2)}) collective-permute-start(f32[64,1024]{1,0:T(8,128)S(1)} %onward.7), channel_id=1, source_target_pairs={{0,16},{1,17},{2,18},{3,19},{4,20},{5,21},{6,22},{7,23}} | collective-permute-start | bytes 786440 | tf_op jit(solution)/shard_map/ppermute | solution.py:370
  81.1 4.0 %collective-permute-start.32 = (f32[64,1024]{1,0:T(8,128)S(1)}, f32[64,1024]{1,0:T(8,128)S(1)}, u32[]{:S(2)}, u32[]{:S(2)}) collective-permute-start(f32[64,1024]{1,0:T(8,128)S(1)} %get-tuple-element.255), channel_id=1, source_target_pairs={{8,16},{9,17},{10,18},{11,19},{12,20},{13,21},{14,22},{15,23}} | collective-permute-start | bytes 786440 | tf_op jit(solution)/shard_map/ppermute | solution.py:370
  81.8 4.6 %collective-permute-start.35 = (f32[64,1024]{1,0:T(8,128)S(1)}, f32[64,1024]{1,0:T(8,128)S(1)}, u32[]{:S(2)}, u32[]{:S(2)}) collective-permute-start(f32[64,1024]{1,0:T(8,128)S(1)} %onward.10), channel_id=1, source_target_pairs={{0,8},{1,9},{2,10},{3,11},{4,12},{5,13},{6,14},{7,15}} | collective-permute-start | bytes 786440 | tf_op jit(solution)/shard_map/ppermute | solution.py:370
  82.5 22.9 %collective-permute-start.38 = (f32[64,1024]{1,0:T(8,128)S(1)}, f32[64,1024]{1,0:T(8,128)S(1)}, u32[]{:S(2)}, u32[]{:S(2)}) collective-permute-start(f32[64,1024]{1,0:T(8,128)S(1)} %onward.9), channel_id=1, source_target_pairs={{8,24},{9,25},{10,26},{11,27},{12,28},{13,29},{14,30},{15,31}} | collective-permute-start | bytes 786440 | tf_op jit(solution)/shard_map/ppermute | solution.py:370
  83.8 15.4 %collective-permute-start.37 = (f32[64,1024]{1,0:T(8,128)S(1)}, f32[64,1024]{1,0:T(8,128)S(1)}, u32[]{:S(2)}, u32[]{:S(2)}) collective-permute-start(f32[64,1024]{1,0:T(8,128)S(1)} %get-tuple-element.272), channel_id=1, source_target_pairs={{16,24},{17,25},{18,26},{19,27},{20,28},{21,29},{22,30},{23,31}} | collective-permute-start | bytes 786440 | tf_op jit(solution)/shard_map/ppermute | solution.py:370
  85.2 23.0 %collective-permute-start.34 = (f32[64,1024]{1,0:T(8,128)S(1)}, f32[64,1024]{1,0:T(8,128)S(1)}, u32[]{:S(2)}, u32[]{:S(2)}) collective-permute-start(f32[64,1024]{1,0:T(8,128)S(1)} %get-tuple-element.267), channel_id=1, source_target_pairs={{16,24},{17,25},{18,26},{19,27},{20,28},{21,29},{22,30},{23,31}} | collective-permute-start | bytes 786440 | tf_op jit(solution)/shard_map/ppermute | solution.py:370
  86.5 24.4 %collective-permute-start.36 = (f32[64,1024]{1,0:T(8,128)S(1)}, f32[64,1024]{1,0:T(8,128)S(1)}, u32[]{:S(2)}, u32[]{:S(2)}) collective-permute-start(f32[64,1024]{1,0:T(8,128)S(1)} %onward.11), channel_id=1, source_target_pairs={{8,24},{9,25},{10,26},{11,27},{12,28},{13,29},{14,30},{15,31}} | collective-permute-start | bytes 786440 | tf_op jit(solution)/shard_map/ppermute | solution.py:370

commit v6 on v5

--- a/solution.py
+++ b/solution.py
@@ -28,22 +28,21 @@
     (RELAY, 0, 1, 1),
     (SOLVE, 1, 0),
     (PASS, 0, 2, 1),
+    (SOLVE, 2, 0),
     (ASSEMBLE, 3, 0),
     (SOLVE, 0, 1),
     (PASS, 0, 3, 0),
-    (SOLVE, 2, 0),
     (SOLVE, 1, 1),
     (PASS, 1, 3, 0),
     (PASS, 0, 3, 1),
     (SOLVE, 2, 1),
     (PASS, 1, 3, 1),
 )
-GATES = ((PLANE, 1, 0), (ASSEMBLE, 0, 0), (DOWN, 0, 0, 0), (DOWN, 0, 1, 0))
+GATES = ((ASSEMBLE, 0, 0), (PLANE, 0, 0), (DOWN, 0, 0, 0), (DOWN, 0, 1, 0))
 TIES = {
     (RELAY, 0, 1, 0): ((PLANE, 1, 0),),
-    (RELAY, 1, 1, 0): ((PLANE, 2, 0),),
 }
-COSTS = {}
+COSTS = {(PAYLOAD,): 2000000000}
 
 
 def params(mib):

time: 113 us -> 112 us (level)
    ppermute x19, starting transfers between devices: 26.5 us -> 24.1 us  [moved(): received = lax.ppermute(value, 'col', pairs)]
    ppermute x15, starting transfers between devices: 17.7 us -> 19.3 us  [exchange(): received.append(lax.ppermute(value, 'rhs', pairs))]
where the time goes in v6:
time: 112 us; the launch traced here: 111 us
  waiting for transfers between devices  46.9 us (42%)
  starting transfers between devices  44.1 us (39%)
  Pallas kernels  17.2 us (15%)
  local copies, waits for them, and re-layouts  1.69 us (2%)
    ppermute x19, starting transfers between devices, moved(): received = lax.ppermute(value, 'col', pairs)  24.1 us
    ppermute x19, waiting for transfers between devices, moved(): received = lax.ppermute(value, 'col', pairs)  23.3 us
    ppermute x15, waiting for transfers between devices, exchange(): received.append(lax.ppermute(value, 'rhs', pairs))  22.1 us
    ppermute x15, starting transfers between devices, exchange(): received.append(lax.ppermute(value, 'rhs', pairs))  19.3 us
    pallas_call x2, Pallas kernels, payload(): pl.pallas_call(functools.partial(payload_kernel, pieces, count), name='pa...  7.38 us
    pallas_call x5, Pallas kernels, assemble(): pl.pallas_call(functools.partial(assemble_kernel, block, block_size, heig...  6.87 us
  transfers between devices with their start and end apart: 39, of which 12 were waited for; matrix products, arithmetic and copies ran while one was open for 1% of the time, Pallas kernels for 11%

profile of v6, /device:TPU:24, one launch (start us, length us, event | category | flops | bytes accessed | tf_op | source)
XLA Modules:
  0.0 111.2 jit_solution(11738263801738676915)
XLA Ops:
  0.0 0.7 copy-done.4
  0.7 0.7 copy-done.6
  1.3 2.7 %payload.2 = (f32[4,72,256]{2,1,0:T(8,128)S(1)}, f32[4,72,256]{2,1,0:T(8,128)S(1)}) custom-call(s32[1,4]{1,0:T(1,128)S(1)} %copy-done.6, bf16[8,128,1024]{2,1,0:T(8,128)(2,1)} %bitcast.4, bf16[1024,1024]{1,0:T(8,128)(2,1)} %bitcast.6, s32[1,1024]{1,0:T(1,128)S(1)} %copy-done.4), custom_call_target="tpu_custom_call" | custom-call | flops 2000000000 | tf_op jit(solution)/shard_map/payload/pallas_call | solution.py:148
  4.1 0.1 collective-permute-start
  4.2 1.5 %collective-permute-done = f32[4,72,256]{2,1,0:T(8,128)S(1)} collective-permute-done((f32[4,72,256]{2,1,0:T(8,128)S(1)}, f32[4,72,256]{2,1,0:T(8,128)S(1)}, u32[]{:S(2)}, u32[]{:S(2)}) %collective-permute-start) | collective-permute-done | bytes 294944 | tf_op jit(solution)/shard_map/ppermute | solution.py:374
  5.8 1.6 %collective-permute-start.1 = (f32[2,72,256]{2,1,0:T(8,128)S(1)}, f32[2,72,256]{2,1,0:T(8,128)S(1)}, u32[]{:S(2)}, u32[]{:S(2)}) collective-permute-start(f32[2,72,256]{2,1,0:T(8,128)S(1)} %pad_maximum_fusion.13), channel_id=1, source_target_pairs={{0,2},{1,3},{2,0},{3,1},{4,6},{5,7},{6,4},{7,5},{8,10},{9,11},{10,... | collective-permute-start | bytes 442376 | tf_op jit(solution)/shard_map/ppermute | solution.py:385
  7.4 1.6 %collective-permute-start.2 = (f32[2,72,256]{2,1,0:T(8,128)S(1)}, f32[2,72,256]{2,1,0:T(8,128)S(1)}, u32[]{:S(2)}, u32[]{:S(2)}) collective-permute-start(f32[2,72,256]{2,1,0:T(8,128)S(1)} %pad_maximum_fusion.14), channel_id=1, source_target_pairs={{0,4},{1,5},{2,6},{3,7},{4,0},{5,1},{6,2},{7,3},{8,12},{9,13},{10,... | collective-permute-start | bytes 442376 | tf_op jit(solution)/shard_map/ppermute | solution.py:385
  9.0 0.5 collective-permute-start.3
  9.6 0.0 slice-start
  9.6 4.6 %payload.3 = (f32[4,64,256]{2,1,0:T(8,128)S(1)}, f32[4,64,256]{2,1,0:T(8,128)S(1)}, f32[4,128,256]{2,1,0:T(8,128)S(1)}, f32[4,128,256]{2,1,0:T(8,128)S(1)}, f32[...) custom-call(s32[1,4]{1,0:T(1,128)S(1)} %copy-done.7, ...), custom_call_target="tpu_custom_call" | custom-call | flops 2000000000 | tf_op jit(solution)/shard_map/payload/pallas_call | solution.py:148
  14.4 1.9 %collective-permute-done.2.refs_2_.refs_6_ = f32[2,72,256]{2,1,0:T(8,128)S(1)} collective-permute-done((f32[2,72,256]{2,1,0:T(8,128)S(1)}, f32[2,72,256]{2,1,0:T(8,128)S(1)}, u32[]{:S(2)}, u32[]{:S(2)}) %collective-permute-start.2) | collective-permute-done | bytes 147488 | tf_op jit(solution)/shard_map/ppermute | solution.py:385
  16.2 1.5 %assemble.5.refs_2_ = f32[64,1024]{1,0:T(8,128)S(1)} custom-call(f32[2,72,256]{2,1,0:T(8,128)S(1)} %pad_maximum_fusion.12.refs_0_.refs_4_, f32[2,72,256]{2,1,0:T(8,128)S(1)} %collective-permute-done.1.refs_1_.refs_5_, f32[2,72,256]{2,1,0:T(8,128)S(1)} %collective-permute-done.2.refs_2_.refs_6_, f32[2,72,256]{2,1,0:T(8,128)S(1)} %collective-permute-done.3.refs_3_.refs_7_, ...), custom_call_target="tpu_custom_call" | custom-call | tf_op jit(solution)/shard_map/assemble/pallas_call | solution.py:207
  17.7 0.1 collective-permute-start.5
  17.8 0.5 collective-permute-start.14
  18.4 2.4 %collective-permute-start.4 = (f32[64,1024]{1,0:T(8,128)S(1)}, f32[64,1024]{1,0:T(8,128)S(1)}, u32[]{:S(2)}, u32[]{:S(2)}) collective-permute-start(f32[64,1024]{1,0:T(8,128)S(1)} %assemble.5.refs_2_), channel_id=1, source_target_pairs={{8,0},{24,16},{9,1},{25,17},{10,2},{26,18},{11,3},{27,19},{12,4},{... | collective-permute-start | bytes 786440 | tf_op jit(solution)/shard_map/ppermute | solution.py:369
  20.8 0.1 collective-permute-start.19
  21.0 1.2 %collective-permute-start.6 = (f32[2,128,256]{2,1,0:T(8,128)S(1)}, f32[2,128,256]{2,1,0:T(8,128)S(1)}, u32[]{:S(2)}, u32[]{:S(2)}) collective-permute-start(f32[2,128,256]{2,1,0:T(8,128)S(1)} %get-tuple-element.157), channel_id=1, source_target_pairs={{0,2},{1,3},{2,0},{3,1},{4,6},{5,7},{6,4},{7,5},{8,10},{9,11},{10,... | collective-permute-start | bytes 786440 | tf_op jit(solution)/shard_map/ppermute | solution.py:385
  22.2 0.9 collective-permute-start.7
  23.1 1.5 %collective-permute-start.8 = (f32[2,128,256]{2,1,0:T(8,128)S(1)}, f32[2,128,256]{2,1,0:T(8,128)S(1)}, u32[]{:S(2)}, u32[]{:S(2)}) collective-permute-start(f32[2,128,256]{2,1,0:T(8,128)S(1)} %pad_maximum_fusion.2), channel_id=1, source_target_pairs={{0,6},{1,7},{2,4},{3,5},{4,2},{5,3},{6,0},{7,1},{8,14},{9,15},{10,... | collective-permute-start | bytes 786440 | tf_op jit(solution)/shard_map/ppermute | solution.py:385
  24.7 1.8 %collective-permute-done.4.refs_3_ = f32[64,1024]{1,0:T(8,128)S(1)} collective-permute-done((f32[64,1024]{1,0:T(8,128)S(1)}, f32[64,1024]{1,0:T(8,128)S(1)}, u32[]{:S(2)}, u32[]{:S(2)}) %collective-permute-start.4) | collective-permute-done | bytes 262176 | tf_op jit(solution)/shard_map/ppermute | solution.py:369
  26.5 3.6 %collective-permute-done.6.refs_1_ = f32[2,128,256]{2,1,0:T(8,128)S(1)} collective-permute-done((f32[2,128,256]{2,1,0:T(8,128)S(1)}, f32[2,128,256]{2,1,0:T(8,128)S(1)}, u32[]{:S(2)}, u32[]{:S(2)}) %collective-permute-start.6) | collective-permute-done | bytes 262176 | tf_op jit(solution)/shard_map/ppermute | solution.py:385
  30.2 1.2 %collective-permute-start.15 = (f32[2,64,256]{2,1,0:T(8,128)S(1)}, f32[2,64,256]{2,1,0:T(8,128)S(1)}, u32[]{:S(2)}, u32[]{:S(2)}) collective-permute-start(f32[2,64,256]{2,1,0:T(8,128)S(1)} %get-tuple-element.173), channel_id=1, source_target_pairs={{0,2},{1,3},{2,0},{3,1},{4,6},{5,7},{6,4},{7,5},{8,10},{9,11},{10,... | collective-permute-start | bytes 393224 | tf_op jit(solution)/shard_map/ppermute | solution.py:385
  31.3 3.1 %collective-permute-done.7.refs_2_ = f32[2,128,256]{2,1,0:T(8,128)S(1)} collective-permute-done((f32[2,128,256]{2,1,0:T(8,128)S(1)}, f32[2,128,256]{2,1,0:T(8,128)S(1)}, u32[]{:S(2)}, u32[]{:S(2)}) %collective-permute-start.7) | collective-permute-done | bytes 262176 | tf_op jit(solution)/shard_map/ppermute | solution.py:385
  34.4 2.9 %collective-permute-start.16 = (f32[2,64,256]{2,1,0:T(8,128)S(1)}, f32[2,64,256]{2,1,0:T(8,128)S(1)}, u32[]{:S(2)}, u32[]{:S(2)}) collective-permute-start(f32[2,64,256]{2,1,0:T(8,128)S(1)} %get-tuple-element.174), channel_id=1, source_target_pairs={{0,4},{1,5},{2,6},{3,7},{4,0},{5,1},{6,2},{7,3},{8,12},{9,13},{10,... | collective-permute-start | bytes 393224 | tf_op jit(solution)/shard_map/ppermute | solution.py:385
  37.4 1.0 stage.1
  38.4 1.3 %assemble.6.refs_6_.refs_2_ = f32[128,1024]{1,0:T(8,128)S(1)} custom-call(f32[2,128,256]{2,1,0:T(8,128)S(1)} %pad_maximum_fusion.7.refs_0_, f32[2,128,256]{2,1,0:T(8,128)S(1)} %collective-permute-done.6.refs_1_, f32[2,128,256]{2,1,0:T(8,128)S(1)} %collective-permute-done.7.refs_2_, f32[2,128,256]{2,1,0:T(8,128)S(1)} %collective-permute-done.8.refs_3_, ...), custom_call_target="tpu_custom_call" | custom-call | tf_op jit(solution)/shard_map/assemble/pallas_call | solution.py:207
  39.7 1.3 %collective-permute-start.23 = (f32[128,1024]{1,0:T(8,128)S(1)}, f32[128,1024]{1,0:T(8,128)S(1)}, u32[]{:S(2)}, u32[]{:S(2)}) collective-permute-start(f32[128,1024]{1,0:T(8,128)S(1)} %assemble.6.refs_6_.refs_2_), channel_id=1, source_target_pairs={{24,16},{25,17},{26,18},{27,19},{28,20},{29,21},{30,22},{31,23}} | collective-permute-start | bytes 1572872 | tf_op jit(solution)/shard_map/ppermute | solution.py:369
  41.1 0.8 collective-permute-start.10
  41.9 1.3 %collective-permute-start.17 = (f32[2,64,256]{2,1,0:T(8,128)S(1)}, f32[2,64,256]{2,1,0:T(8,128)S(1)}, u32[]{:S(2)}, u32[]{:S(2)}) collective-permute-start(f32[2,64,256]{2,1,0:T(8,128)S(1)} %pad_maximum_fusion.19), channel_id=1, source_target_pairs={{0,6},{1,7},{2,4},{3,5},{4,2},{5,3},{6,0},{7,1},{8,14},{9,15},{10,... | collective-permute-start | bytes 393224 | tf_op jit(solution)/shard_map/ppermute | solution.py:385
  43.3 0.7 collective-permute-start.20
  44.0 5.3 %collective-permute-done.17.refs_3_ = f32[2,64,256]{2,1,0:T(8,128)S(1)} collective-permute-done((f32[2,64,256]{2,1,0:T(8,128)S(1)}, f32[2,64,256]{2,1,0:T(8,128)S(1)}, u32[]{:S(2)}, u32[]{:S(2)}) %collective-permute-start.17) | collective-permute-done | bytes 131104 | tf_op jit(solution)/shard_map/ppermute | solution.py:385
  49.3 0.4 collective-permute-start.21
  49.7 1.5 %assemble.7.refs_2_ = f32[64,1024]{1,0:T(8,128)S(1)} custom-call(f32[2,64,256]{2,1,0:T(8,128)S(1)} %pad_maximum_fusion.16.refs_0_, f32[2,64,256]{2,1,0:T(8,128)S(1)} %collective-permute-done.15.refs_1_, f32[2,64,256]{2,1,0:T(8,128)S(1)} %collective-permute-done.16.refs_2_, f32[2,64,256]{2,1,0:T(8,128)S(1)} %collective-permute-done.17.refs_3_, ...), custom_call_target="tpu_custom_call" | custom-call | tf_op jit(solution)/shard_map/assemble/pallas_call | solution.py:207
  51.2 2.3 %collective-permute-start.22 = (f32[2,128,256]{2,1,0:T(8,128)S(1)}, f32[2,128,256]{2,1,0:T(8,128)S(1)}, u32[]{:S(2)}, u32[]{:S(2)}) collective-permute-start(f32[2,128,256]{2,1,0:T(8,128)S(1)} %pad_maximum_fusion.11), channel_id=1, source_target_pairs={{0,6},{1,7},{2,4},{3,5},{4,2},{5,3},{6,0},{7,1},{8,14},{9,15},{10,... | collective-permute-start | bytes 786440 | tf_op jit(solution)/shard_map/ppermute | solution.py:385
  53.6 2.2 %collective-permute-start.18 = (f32[64,1024]{1,0:T(8,128)S(1)}, f32[64,1024]{1,0:T(8,128)S(1)}, u32[]{:S(2)}, u32[]{:S(2)}) collective-permute-start(f32[64,1024]{1,0:T(8,128)S(1)} %assemble.7.refs_2_), channel_id=1, source_target_pairs={{8,0},{24,16},{9,1},{25,17},{10,2},{26,18},{11,3},{27,19},{12,4},{... | collective-permute-start | bytes 786440 | tf_op jit(solution)/shard_map/ppermute | solution.py:369
  55.8 0.1 add.10
  55.8 0.7 collective-permute-start.25
  56.7 0.8 collective-permute-start.11
  57.5 2.8 %collective-permute-done.21.refs_2_ = f32[2,128,256]{2,1,0:T(8,128)S(1)} collective-permute-done((f32[2,128,256]{2,1,0:T(8,128)S(1)}, f32[2,128,256]{2,1,0:T(8,128)S(1)}, u32[]{:S(2)}, u32[]{:S(2)}) %collective-permute-start.21) | collective-permute-done | bytes 262176 | tf_op jit(solution)/shard_map/ppermute | solution.py:385
  60.3 0.7 collective-permute-start.26
  61.0 1.3 %assemble.8.refs_2_.refs_6_ = f32[128,1024]{1,0:T(8,128)S(1)} custom-call(f32[2,128,256]{2,1,0:T(8,128)S(1)} %pad_maximum_fusion.8.refs_0_, f32[2,128,256]{2,1,0:T(8,128)S(1)} %collective-permute-done.20.refs_1_, f32[2,128,256]{2,1,0:T(8,128)S(1)} %collective-permute-done.21.refs_2_, f32[2,128,256]{2,1,0:T(8,128)S(1)} %collective-permute-done.22.refs_3_, ...), custom_call_target="tpu_custom_call" | custom-call | tf_op jit(solution)/shard_map/assemble/pallas_call | solution.py:207
  62.3 0.7 collective-permute-start.24
  63.0 5.5 %collective-permute-start.27 = (f32[128,1024]{1,0:T(8,128)S(1)}, f32[128,1024]{1,0:T(8,128)S(1)}, u32[]{:S(2)}, u32[]{:S(2)}) collective-permute-start(f32[128,1024]{1,0:T(8,128)S(1)} %assemble.8.refs_2_.refs_6_), channel_id=1, source_target_pairs={{24,16},{25,17},{26,18},{27,19},{28,20},{29,21},{30,22},{31,23}} | collective-permute-start | bytes 1572872 | tf_op jit(solution)/shard_map/ppermute | solution.py:369
  68.6 0.3 collective-permute-start.12
  68.9 2.1 %collective-permute-start.13 = (f32[2,128,256]{2,1,0:T(8,128)S(1)}, f32[2,128,256]{2,1,0:T(8,128)S(1)}, u32[]{:S(2)}, u32[]{:S(2)}) collective-permute-start(f32[2,128,256]{2,1,0:T(8,128)S(1)} %pad_maximum_fusion.6), channel_id=1, source_target_pairs={{0,6},{1,7},{2,4},{3,5},{4,2},{5,3},{6,0},{7,1},{8,14},{9,15},{10,... | collective-permute-start | bytes 786440 | tf_op jit(solution)/shard_map/ppermute | solution.py:385
  71.1 0.7 collective-permute-start.30
  71.7 0.7 collective-permute-start.31
  72.5 5.3 %collective-permute-done.12.refs_2_ = f32[2,128,256]{2,1,0:T(8,128)S(1)} collective-permute-done((f32[2,128,256]{2,1,0:T(8,128)S(1)}, f32[2,128,256]{2,1,0:T(8,128)S(1)}, u32[]{:S(2)}, u32[]{:S(2)}) %collective-permute-start.12) | collective-permute-done | bytes 262176 | tf_op jit(solution)/shard_map/ppermute | solution.py:385
  77.8 0.7 collective-permute-start.29
  78.5 1.3 %assemble.9.refs_7_.refs_2_ = f32[128,1024]{1,0:T(8,128)S(1)} custom-call(f32[2,128,256]{2,1,0:T(8,128)S(1)} %pad_maximum_fusion.3.refs_0_, f32[2,128,256]{2,1,0:T(8,128)S(1)} %collective-permute-done.11.refs_1_, f32[2,128,256]{2,1,0:T(8,128)S(1)} %collective-permute-done.12.refs_2_, f32[2,128,256]{2,1,0:T(8,128)S(1)} %collective-permute-done.13.refs_3_, ...), custom_call_target="tpu_custom_call" | custom-call | tf_op jit(solution)/shard_map/assemble/pallas_call | solution.py:207
  79.9 0.7 collective-permute-start.33
  80.6 0.7 collective-permute-start.28
  81.3 0.7 collective-permute-start.32
  82.0 0.7 collective-permute-start.35
  82.7 1.3 %collective-permute-start.37 = (f32[64,1024]{1,0:T(8,128)S(1)}, f32[64,1024]{1,0:T(8,128)S(1)}, u32[]{:S(2)}, u32[]{:S(2)}) collective-permute-start(f32[64,1024]{1,0:T(8,128)S(1)} %get-tuple-element.272), channel_id=1, source_target_pairs={{16,24},{17,25},{18,26},{19,27},{20,28},{21,29},{22,30},{23,31}} | collective-permute-start | bytes 786440 | tf_op jit(solution)/shard_map/ppermute | solution.py:369
  84.0 1.3 %collective-permute-start.38 = (f32[64,1024]{1,0:T(8,128)S(1)}, f32[64,1024]{1,0:T(8,128)S(1)}, u32[]{:S(2)}, u32[]{:S(2)}) collective-permute-start(f32[64,1024]{1,0:T(8,128)S(1)} %onward.9), channel_id=1, source_target_pairs={{8,24},{9,25},{10,26},{11,27},{12,28},{13,29},{14,30},{15,31}} | collective-permute-start | bytes 786440 | tf_op jit(solution)/shard_map/ppermute | solution.py:369
  85.4 1.3 %collective-permute-start.34 = (f32[64,1024]{1,0:T(8,128)S(1)}, f32[64,1024]{1,0:T(8,128)S(1)}, u32[]{:S(2)}, u32[]{:S(2)}) collective-permute-start(f32[64,1024]{1,0:T(8,128)S(1)} %get-tuple-element.267), channel_id=1, source_target_pairs={{16,24},{17,25},{18,26},{19,27},{20,28},{21,29},{22,30},{23,31}} | collective-permute-start | bytes 786440 | tf_op jit(solution)/shard_map/ppermute | solution.py:369
  86.7 1.3 %collective-permute-start.36 = (f32[64,1024]{1,0:T(8,128)S(1)}, f32[64,1024]{1,0:T(8,128)S(1)}, u32[]{:S(2)}, u32[]{:S(2)}) collective-permute-start(f32[64,1024]{1,0:T(8,128)S(1)} %onward.11), channel_id=1, source_target_pairs={{8,24},{9,25},{10,26},{11,27},{12,28},{13,29},{14,30},{15,31}} | collective-permute-start | bytes 786440 | tf_op jit(solution)/shard_map/ppermute | solution.py:369
  88.0 8.0 %collective-permute-done.37.refs_3_ = f32[64,1024]{1,0:T(8,128)S(1)} collective-permute-done((f32[64,1024]{1,0:T(8,128)S(1)}, f32[64,1024]{1,0:T(8,128)S(1)}, u32[]{:S(2)}, u32[]{:S(2)}) %collective-permute-start.37) | collective-permute-done | bytes 262176 | tf_op jit(solution)/shard_map/ppermute | solution.py:369
  96.0 8.4 %collective-permute-done.38.refs_4_ = f32[64,1024]{1,0:T(8,128)S(1)} collective-permute-done((f32[64,1024]{1,0:T(8,128)S(1)}, f32[64,1024]{1,0:T(8,128)S(1)}, u32[]{:S(2)}, u32[]{:S(2)}) %collective-permute-start.38) | collective-permute-done | bytes 262176 | tf_op jit(solution)/shard_map/ppermute | solution.py:369
  104.3 0.5 solve.14.refs_8_
  104.8 2.3 %collective-permute-done.34.refs_3_ = f32[64,1024]{1,0:T(8,128)S(1)} collective-permute-done((f32[64,1024]{1,0:T(8,128)S(1)}, f32[64,1024]{1,0:T(8,128)S(1)}, u32[]{:S(2)}, u32[]{:S(2)}) %collective-permute-start.34) | collective-permute-done | bytes 262176 | tf_op jit(solution)/shard_map/ppermute | solution.py:369
  107.1 2.8 %collective-permute-done.36.refs_4_ = f32[64,1024]{1,0:T(8,128)S(1)} collective-permute-done((f32[64,1024]{1,0:T(8,128)S(1)}, f32[64,1024]{1,0:T(8,128)S(1)}, u32[]{:S(2)}, u32[]{:S(2)}) %collective-permute-start.36) | collective-permute-done | bytes 262176 | tf_op jit(solution)/shard_map/ppermute | solution.py:369
  109.9 1.3 %solve.15 = f32[128,1024]{1,0:T(8,128)} custom-call(f32[128,1024]{1,0:T(8,128)S(1)} %copy-done, bf16[1024,1024]{1,0:T(8,128)(2,1)S(1)} %get-tuple-element.164.refs_1_, f32[128,1024]{1,0:T(8,128)S(1)} %assemble.9.refs_7_.refs_2_, f32[64,1024]{1,0:T(8,128)S(1)} %collective-permute-done.34.refs_3_, f32[64,1024]{1,0:T(8,128)S(1)} %collective-permute-done.36.refs_4_, ...), custom_call_target="tpu_custom_call" | custom-call | tf_op jit(solution)/shard_map/solve/pallas_call | solution.py:306
  (86 shorter events, 1.0 us)
Async XLA Ops:
  0.0 0.7 copy-start.4
  0.7 0.7 copy-start.6
  1.3 8.2 %copy-start.3 = (bf16[1,1024,1024]{2,1,0:T(8,128)(2,1)S(1)}, bf16[1,1024,1024]{2,1,0:T(8,128)(2,1)}, u32[]{:S(2)}) copy-start(bf16[1,1024,1024]{2,1,0:T(8,128)(2,1)} %param.8) | copy-start | bytes 6291460
  4.1 5.5 %copy-start.2 = (bf16[1,1024,1024]{2,1,0:T(8,128)(2,1)S(1)}, bf16[1,1024,1024]{2,1,0:T(8,128)(2,1)}, u32[]{:S(2)}) copy-start(bf16[1,1024,1024]{2,1,0:T(8,128)(2,1)} %param.7) | copy-start | bytes 6291460
  4.1 5.5 %copy-start.5 = (s32[1,1024]{1,0:T(1,128)S(1)}, s32[1,1024]{1,0:T(1,128)}, u32[]{:S(2)}) copy-start(s32[1,1024]{1,0:T(1,128)} %index_ref.3) | copy-start | bytes 12292
  4.1 5.5 %copy-start.7 = (s32[1,4]{1,0:T(1,128)S(1)}, s32[1,4]{1,0:T(1,128)}, u32[]{:S(2)}) copy-start(s32[1,4]{1,0:T(1,128)} %owner_ref.3) | copy-start | bytes 52
  4.1 1.6 %collective-permute-start = (f32[4,72,256]{2,1,0:T(8,128)S(1)}, f32[4,72,256]{2,1,0:T(8,128)S(1)}, u32[]{:S(2)}, u32[]{:S(2)}) collective-permute-start(f32[4,72,256]{2,1,0:T(8,128)S(1)} %get-tuple-element.143), channel_id=1, source_target_pairs={{0,1},{1,0},{2,3},{3,2},{4,5},{5,4},{6,7},{7,6},{8,9},{9,8},{10,11... | collective-permute-start | bytes 884744 | tf_op jit(solution)/shard_map/ppermute | solution.py:374
  5.8 8.5 %collective-permute-start.1 = (f32[2,72,256]{2,1,0:T(8,128)S(1)}, f32[2,72,256]{2,1,0:T(8,128)S(1)}, u32[]{:S(2)}, u32[]{:S(2)}) collective-permute-start(f32[2,72,256]{2,1,0:T(8,128)S(1)} %pad_maximum_fusion.13), channel_id=1, source_target_pairs={{0,2},{1,3},{2,0},{3,1},{4,6},{5,7},{6,4},{7,5},{8,10},{9,11},{10,... | collective-permute-start | bytes 442376 | tf_op jit(solution)/shard_map/ppermute | solution.py:385
  7.4 8.8 %collective-permute-start.2 = (f32[2,72,256]{2,1,0:T(8,128)S(1)}, f32[2,72,256]{2,1,0:T(8,128)S(1)}, u32[]{:S(2)}, u32[]{:S(2)}) collective-permute-start(f32[2,72,256]{2,1,0:T(8,128)S(1)} %pad_maximum_fusion.14), channel_id=1, source_target_pairs={{0,4},{1,5},{2,6},{3,7},{4,0},{5,1},{6,2},{7,3},{8,12},{9,13},{10,... | collective-permute-start | bytes 442376 | tf_op jit(solution)/shard_map/ppermute | solution.py:385
  9.0 7.2 %collective-permute-start.3 = (f32[2,72,256]{2,1,0:T(8,128)S(1)}, f32[2,72,256]{2,1,0:T(8,128)S(1)}, u32[]{:S(2)}, u32[]{:S(2)}) collective-permute-start(f32[2,72,256]{2,1,0:T(8,128)S(1)} %pad_maximum_fusion.15), channel_id=1, source_target_pairs={{0,6},{1,7},{2,4},{3,5},{4,2},{5,3},{6,0},{7,1},{8,14},{9,15},{10,... | collective-permute-start | bytes 442376 | tf_op jit(solution)/shard_map/ppermute | solution.py:385
  9.6 27.7 %slice-start = ((s8[8388608]{0:T(1024)(128)(4,1)}), s8[4194304]{0:T(1024)(128)(4,1)S(1)}, s32[]{:S(2)}) async-start(s8[8388608]{0:T(1024)(128)(4,1)} %bitcast.2), calls=%async_computation | async-start | bytes 8388608
  14.3 23.0 %slice-start.1 = ((s8[8388608]{0:T(1024)(128)(4,1)}), s8[4194304]{0:T(1024)(128)(4,1)S(1)}, s32[]{:S(2)}) async-start(s8[8388608]{0:T(1024)(128)(4,1)} %bitcast.2), calls=%async_computation.1 | async-start | bytes 8388608
  17.7 3.1 %collective-permute-start.5 = (f32[4,128,256]{2,1,0:T(8,128)S(1)}, f32[4,128,256]{2,1,0:T(8,128)S(1)}, u32[]{:S(2)}, u32[]{:S(2)}) collective-permute-start(f32[4,128,256]{2,1,0:T(8,128)S(1)} %get-tuple-element.156), channel_id=1, source_target_pairs={{0,1},{1,0},{2,3},{3,2},{4,5},{5,4},{6,7},{7,6},{8,9},{9,8},{10,11... | collective-permute-start | bytes 1572872 | tf_op jit(solution)/shard_map/ppermute | solution.py:374
  17.8 3.0 %collective-permute-start.14 = (f32[4,64,256]{2,1,0:T(8,128)S(1)}, f32[4,64,256]{2,1,0:T(8,128)S(1)}, u32[]{:S(2)}, u32[]{:S(2)}) collective-permute-start(f32[4,64,256]{2,1,0:T(8,128)S(1)} %get-tuple-element.172), channel_id=1, source_target_pairs={{0,1},{1,0},{2,3},{3,2},{4,5},{5,4},{6,7},{7,6},{8,9},{9,8},{10,11... | collective-permute-start | bytes 786440 | tf_op jit(solution)/shard_map/ppermute | solution.py:374
  18.4 8.2 %collective-permute-start.4 = (f32[64,1024]{1,0:T(8,128)S(1)}, f32[64,1024]{1,0:T(8,128)S(1)}, u32[]{:S(2)}, u32[]{:S(2)}) collective-permute-start(f32[64,1024]{1,0:T(8,128)S(1)} %assemble.5.refs_2_), channel_id=1, source_target_pairs={{8,0},{24,16},{9,1},{25,17},{10,2},{26,18},{11,3},{27,19},{12,4},{... | collective-permute-start | bytes 786440 | tf_op jit(solution)/shard_map/ppermute | solution.py:369
  20.8 20.3 %collective-permute-start.19 = (f32[4,128,256]{2,1,0:T(8,128)S(1)}, f32[4,128,256]{2,1,0:T(8,128)S(1)}, u32[]{:S(2)}, u32[]{:S(2)}) collective-permute-start(f32[4,128,256]{2,1,0:T(8,128)S(1)} %get-tuple-element.200), channel_id=1, source_target_pairs={{0,1},{1,0},{2,3},{3,2},{4,5},{5,4},{6,7},{7,6},{8,9},{9,8},{10,11... | collective-permute-start | bytes 1572872 | tf_op jit(solution)/shard_map/ppermute | solution.py:374
  20.9 16.4 %copy-start.1 = (bf16[1024,1024]{1,0:T(8,128)(2,1)S(1)}, bf16[1024,1024]{1,0:T(8,128)(2,1)}, u32[]{:S(2)}) copy-start(bf16[1024,1024]{1,0:T(8,128)(2,1)} %inverse_ref) | copy-start | bytes 6291460
  21.0 9.2 %collective-permute-start.6 = (f32[2,128,256]{2,1,0:T(8,128)S(1)}, f32[2,128,256]{2,1,0:T(8,128)S(1)}, u32[]{:S(2)}, u32[]{:S(2)}) collective-permute-start(f32[2,128,256]{2,1,0:T(8,128)S(1)} %get-tuple-element.157), channel_id=1, source_target_pairs={{0,2},{1,3},{2,0},{3,1},{4,6},{5,7},{6,4},{7,5},{8,10},{9,11},{10,... | collective-permute-start | bytes 786440 | tf_op jit(solution)/shard_map/ppermute | solution.py:385
  22.2 12.2 %collective-permute-start.7 = (f32[2,128,256]{2,1,0:T(8,128)S(1)}, f32[2,128,256]{2,1,0:T(8,128)S(1)}, u32[]{:S(2)}, u32[]{:S(2)}) collective-permute-start(f32[2,128,256]{2,1,0:T(8,128)S(1)} %get-tuple-element.158), channel_id=1, source_target_pairs={{0,4},{1,5},{2,6},{3,7},{4,0},{5,1},{6,2},{7,3},{8,12},{9,13},{10,... | collective-permute-start | bytes 786440 | tf_op jit(solution)/shard_map/ppermute | solution.py:385
  23.1 14.2 %collective-permute-start.8 = (f32[2,128,256]{2,1,0:T(8,128)S(1)}, f32[2,128,256]{2,1,0:T(8,128)S(1)}, u32[]{:S(2)}, u32[]{:S(2)}) collective-permute-start(f32[2,128,256]{2,1,0:T(8,128)S(1)} %pad_maximum_fusion.2), channel_id=1, source_target_pairs={{0,6},{1,7},{2,4},{3,5},{4,2},{5,3},{6,0},{7,1},{8,14},{9,15},{10,... | collective-permute-start | bytes 786440 | tf_op jit(solution)/shard_map/ppermute | solution.py:385
  26.5 29.3 %collective-permute-start.9 = (f32[4,128,256]{2,1,0:T(8,128)S(1)}, f32[4,128,256]{2,1,0:T(8,128)S(1)}, u32[]{:S(2)}, u32[]{:S(2)}) collective-permute-start(f32[4,128,256]{2,1,0:T(8,128)S(1)} %get-tuple-element.167), channel_id=1, source_target_pairs={{0,1},{1,0},{2,3},{3,2},{4,5},{5,4},{6,7},{7,6},{8,9},{9,8},{10,11... | collective-permute-start | bytes 1572872 | tf_op jit(solution)/shard_map/ppermute | solution.py:374
  30.2 11.8 %collective-permute-start.15 = (f32[2,64,256]{2,1,0:T(8,128)S(1)}, f32[2,64,256]{2,1,0:T(8,128)S(1)}, u32[]{:S(2)}, u32[]{:S(2)}) collective-permute-start(f32[2,64,256]{2,1,0:T(8,128)S(1)} %get-tuple-element.173), channel_id=1, source_target_pairs={{0,2},{1,3},{2,0},{3,1},{4,6},{5,7},{6,4},{7,5},{8,10},{9,11},{10,... | collective-permute-start | bytes 393224 | tf_op jit(solution)/shard_map/ppermute | solution.py:385
  34.4 8.9 %collective-permute-start.16 = (f32[2,64,256]{2,1,0:T(8,128)S(1)}, f32[2,64,256]{2,1,0:T(8,128)S(1)}, u32[]{:S(2)}, u32[]{:S(2)}) collective-permute-start(f32[2,64,256]{2,1,0:T(8,128)S(1)} %get-tuple-element.174), channel_id=1, source_target_pairs={{0,4},{1,5},{2,6},{3,7},{4,0},{5,1},{6,2},{7,3},{8,12},{9,13},{10,... | collective-permute-start | bytes 393224 | tf_op jit(solution)/shard_map/ppermute | solution.py:385
  39.7 13.9 %collective-permute-start.23 = (f32[128,1024]{1,0:T(8,128)S(1)}, f32[128,1024]{1,0:T(8,128)S(1)}, u32[]{:S(2)}, u32[]{:S(2)}) collective-permute-start(f32[128,1024]{1,0:T(8,128)S(1)} %assemble.6.refs_6_.refs_2_), channel_id=1, source_target_pairs={{24,16},{25,17},{26,18},{27,19},{28,20},{29,21},{30,22},{31,23}} | collective-permute-start | bytes 1572872 | tf_op jit(solution)/shard_map/ppermute | solution.py:369
  41.0 12.6 %copy-start = (f32[128,1024]{1,0:T(8,128)S(1)}, f32[128,1024]{1,0:T(8,128)}, u32[]{:S(2)}) copy-start(f32[128,1024]{1,0:T(8,128)} %refs_0_.15) | copy-start | bytes 1572868
  41.1 10.2 %collective-permute-start.10 = (f32[64,1024]{1,0:T(8,128)S(1)}, f32[64,1024]{1,0:T(8,128)S(1)}, u32[]{:S(2)}, u32[]{:S(2)}) collective-permute-start(f32[64,1024]{1,0:T(8,128)S(1)} %add.9), channel_id=1, source_target_pairs={{16,0},{17,1},{18,2},{19,3},{20,4},{21,5},{22,6},{23,7}} | collective-permute-start | bytes 786440 | tf_op jit(solution)/shard_map/ppermute | solution.py:369
  41.9 7.4 %collective-permute-start.17 = (f32[2,64,256]{2,1,0:T(8,128)S(1)}, f32[2,64,256]{2,1,0:T(8,128)S(1)}, u32[]{:S(2)}, u32[]{:S(2)}) collective-permute-start(f32[2,64,256]{2,1,0:T(8,128)S(1)} %pad_maximum_fusion.19), channel_id=1, source_target_pairs={{0,6},{1,7},{2,4},{3,5},{4,2},{5,3},{6,0},{7,1},{8,14},{9,15},{10,... | collective-permute-start | bytes 393224 | tf_op jit(solution)/shard_map/ppermute | solution.py:385
  43.3 13.3 %collective-permute-start.20 = (f32[2,128,256]{2,1,0:T(8,128)S(1)}, f32[2,128,256]{2,1,0:T(8,128)S(1)}, u32[]{:S(2)}, u32[]{:S(2)}) collective-permute-start(f32[2,128,256]{2,1,0:T(8,128)S(1)} %get-tuple-element.201), channel_id=1, source_target_pairs={{0,2},{1,3},{2,0},{3,1},{4,6},{5,7},{6,4},{7,5},{8,10},{9,11},{10,... | collective-permute-start | bytes 786440 | tf_op jit(solution)/shard_map/ppermute | solution.py:385
  49.3 11.0 %collective-permute-start.21 = (f32[2,128,256]{2,1,0:T(8,128)S(1)}, f32[2,128,256]{2,1,0:T(8,128)S(1)}, u32[]{:S(2)}, u32[]{:S(2)}) collective-permute-start(f32[2,128,256]{2,1,0:T(8,128)S(1)} %get-tuple-element.202), channel_id=1, source_target_pairs={{0,4},{1,5},{2,6},{3,7},{4,0},{5,1},{6,2},{7,3},{8,12},{9,13},{10,... | collective-permute-start | bytes 786440 | tf_op jit(solution)/shard_map/ppermute | solution.py:385
  51.2 9.8 %collective-permute-start.22 = (f32[2,128,256]{2,1,0:T(8,128)S(1)}, f32[2,128,256]{2,1,0:T(8,128)S(1)}, u32[]{:S(2)}, u32[]{:S(2)}) collective-permute-start(f32[2,128,256]{2,1,0:T(8,128)S(1)} %pad_maximum_fusion.11), channel_id=1, source_target_pairs={{0,6},{1,7},{2,4},{3,5},{4,2},{5,3},{6,0},{7,1},{8,14},{9,15},{10,... | collective-permute-start | bytes 786440 | tf_op jit(solution)/shard_map/ppermute | solution.py:385
  53.6 8.7 %collective-permute-start.18 = (f32[64,1024]{1,0:T(8,128)S(1)}, f32[64,1024]{1,0:T(8,128)S(1)}, u32[]{:S(2)}, u32[]{:S(2)}) collective-permute-start(f32[64,1024]{1,0:T(8,128)S(1)} %assemble.7.refs_2_), channel_id=1, source_target_pairs={{8,0},{24,16},{9,1},{25,17},{10,2},{26,18},{11,3},{27,19},{12,4},{... | collective-permute-start | bytes 786440 | tf_op jit(solution)/shard_map/ppermute | solution.py:369
  55.8 13.1 %collective-permute-start.25 = (f32[128,1024]{1,0:T(8,128)S(1)}, f32[128,1024]{1,0:T(8,128)S(1)}, u32[]{:S(2)}, u32[]{:S(2)}) collective-permute-start(f32[128,1024]{1,0:T(8,128)S(1)} %add.10), channel_id=1, source_target_pairs={{16,8},{17,9},{18,10},{19,11},{20,12},{21,13},{22,14},{23,15}} | collective-permute-start | bytes 1572872 | tf_op jit(solution)/shard_map/ppermute | solution.py:369
  56.7 14.4 %collective-permute-start.11 = (f32[2,128,256]{2,1,0:T(8,128)S(1)}, f32[2,128,256]{2,1,0:T(8,128)S(1)}, u32[]{:S(2)}, u32[]{:S(2)}) collective-permute-start(f32[2,128,256]{2,1,0:T(8,128)S(1)} %get-tuple-element.168), channel_id=1, source_target_pairs={{0,2},{1,3},{2,0},{3,1},{4,6},{5,7},{6,4},{7,5},{8,10},{9,11},{10,... | collective-permute-start | bytes 786440 | tf_op jit(solution)/shard_map/ppermute | solution.py:385
  60.3 8.3 %collective-permute-start.26 = (f32[64,1024]{1,0:T(8,128)S(1)}, f32[64,1024]{1,0:T(8,128)S(1)}, u32[]{:S(2)}, u32[]{:S(2)}) collective-permute-start(f32[64,1024]{1,0:T(8,128)S(1)} %get-tuple-element.219), channel_id=1, source_target_pairs={{0,8},{1,9},{2,10},{3,11},{4,12},{5,13},{6,14},{7,15}} | collective-permute-start | bytes 786440 | tf_op jit(solution)/shard_map/ppermute | solution.py:369
  62.3 9.4 %collective-permute-start.24 = (f32[64,1024]{1,0:T(8,128)S(1)}, f32[64,1024]{1,0:T(8,128)S(1)}, u32[]{:S(2)}, u32[]{:S(2)}) collective-permute-start(f32[64,1024]{1,0:T(8,128)S(1)} %add.11), channel_id=1, source_target_pairs={{16,0},{17,1},{18,2},{19,3},{20,4},{21,5},{22,6},{23,7}} | collective-permute-start | bytes 786440 | tf_op jit(solution)/shard_map/ppermute | solution.py:369
  63.0 16.8 %collective-permute-start.27 = (f32[128,1024]{1,0:T(8,128)S(1)}, f32[128,1024]{1,0:T(8,128)S(1)}, u32[]{:S(2)}, u32[]{:S(2)}) collective-permute-start(f32[128,1024]{1,0:T(8,128)S(1)} %assemble.8.refs_2_.refs_6_), channel_id=1, source_target_pairs={{24,16},{25,17},{26,18},{27,19},{28,20},{29,21},{30,22},{31,23}} | collective-permute-start | bytes 1572872 | tf_op jit(solution)/shard_map/ppermute | solution.py:369
  68.6 9.2 %collective-permute-start.12 = (f32[2,128,256]{2,1,0:T(8,128)S(1)}, f32[2,128,256]{2,1,0:T(8,128)S(1)}, u32[]{:S(2)}, u32[]{:S(2)}) collective-permute-start(f32[2,128,256]{2,1,0:T(8,128)S(1)} %get-tuple-element.169), channel_id=1, source_target_pairs={{0,4},{1,5},{2,6},{3,7},{4,0},{5,1},{6,2},{7,3},{8,12},{9,13},{10,... | collective-permute-start | bytes 786440 | tf_op jit(solution)/shard_map/ppermute | solution.py:385
  68.9 8.9 %collective-permute-start.13 = (f32[2,128,256]{2,1,0:T(8,128)S(1)}, f32[2,128,256]{2,1,0:T(8,128)S(1)}, u32[]{:S(2)}, u32[]{:S(2)}) collective-permute-start(f32[2,128,256]{2,1,0:T(8,128)S(1)} %pad_maximum_fusion.6), channel_id=1, source_target_pairs={{0,6},{1,7},{2,4},{3,5},{4,2},{5,3},{6,0},{7,1},{8,14},{9,15},{10,... | collective-permute-start | bytes 786440 | tf_op jit(solution)/shard_map/ppermute | solution.py:385
  71.1 8.7 %collective-permute-start.30 = (f32[64,1024]{1,0:T(8,128)S(1)}, f32[64,1024]{1,0:T(8,128)S(1)}, u32[]{:S(2)}, u32[]{:S(2)}) collective-permute-start(f32[64,1024]{1,0:T(8,128)S(1)} %onward.6), channel_id=1, source_target_pairs={{0,16},{1,17},{2,18},{3,19},{4,20},{5,21},{6,22},{7,23}} | collective-permute-start | bytes 786440 | tf_op jit(solution)/shard_map/ppermute | solution.py:369
  71.7 8.1 %collective-permute-start.31 = (f32[64,1024]{1,0:T(8,128)S(1)}, f32[64,1024]{1,0:T(8,128)S(1)}, u32[]{:S(2)}, u32[]{:S(2)}) collective-permute-start(f32[64,1024]{1,0:T(8,128)S(1)} %get-tuple-element.241), channel_id=1, source_target_pairs={{8,16},{9,17},{10,18},{11,19},{12,20},{13,21},{14,22},{15,23}} | collective-permute-start | bytes 786440 | tf_op jit(solution)/shard_map/ppermute | solution.py:369
  77.8 3.4 %collective-permute-start.29 = (f32[64,1024]{1,0:T(8,128)S(1)}, f32[64,1024]{1,0:T(8,128)S(1)}, u32[]{:S(2)}, u32[]{:S(2)}) collective-permute-start(f32[64,1024]{1,0:T(8,128)S(1)} %get-tuple-element.240), channel_id=1, source_target_pairs={{0,8},{1,9},{2,10},{3,11},{4,12},{5,13},{6,14},{7,15}} | collective-permute-start | bytes 786440 | tf_op jit(solution)/shard_map/ppermute | solution.py:369
  79.9 2.1 %collective-permute-start.33 = (f32[64,1024]{1,0:T(8,128)S(1)}, f32[64,1024]{1,0:T(8,128)S(1)}, u32[]{:S(2)}, u32[]{:S(2)}) collective-permute-start(f32[64,1024]{1,0:T(8,128)S(1)} %onward.8), channel_id=1, source_target_pairs={{0,8},{1,9},{2,10},{3,11},{4,12},{5,13},{6,14},{7,15}} | collective-permute-start | bytes 786440 | tf_op jit(solution)/shard_map/ppermute | solution.py:369
  80.6 4.8 %collective-permute-start.28 = (f32[64,1024]{1,0:T(8,128)S(1)}, f32[64,1024]{1,0:T(8,128)S(1)}, u32[]{:S(2)}, u32[]{:S(2)}) collective-permute-start(f32[64,1024]{1,0:T(8,128)S(1)} %onward.7), channel_id=1, source_target_pairs={{0,16},{1,17},{2,18},{3,19},{4,20},{5,21},{6,22},{7,23}} | collective-permute-start | bytes 786440 | tf_op jit(solution)/shard_map/ppermute | solution.py:369
  81.3 4.0 %collective-permute-start.32 = (f32[64,1024]{1,0:T(8,128)S(1)}, f32[64,1024]{1,0:T(8,128)S(1)}, u32[]{:S(2)}, u32[]{:S(2)}) collective-permute-start(f32[64,1024]{1,0:T(8,128)S(1)} %get-tuple-element.255), channel_id=1, source_target_pairs={{8,16},{9,17},{10,18},{11,19},{12,20},{13,21},{14,22},{15,23}} | collective-permute-start | bytes 786440 | tf_op jit(solution)/shard_map/ppermute | solution.py:369
  82.0 4.6 %collective-permute-start.35 = (f32[64,1024]{1,0:T(8,128)S(1)}, f32[64,1024]{1,0:T(8,128)S(1)}, u32[]{:S(2)}, u32[]{:S(2)}) collective-permute-start(f32[64,1024]{1,0:T(8,128)S(1)} %onward.10), channel_id=1, source_target_pairs={{0,8},{1,9},{2,10},{3,11},{4,12},{5,13},{6,14},{7,15}} | collective-permute-start | bytes 786440 | tf_op jit(solution)/shard_map/ppermute | solution.py:369
  82.7 13.2 %collective-permute-start.37 = (f32[64,1024]{1,0:T(8,128)S(1)}, f32[64,1024]{1,0:T(8,128)S(1)}, u32[]{:S(2)}, u32[]{:S(2)}) collective-permute-start(f32[64,1024]{1,0:T(8,128)S(1)} %get-tuple-element.272), channel_id=1, source_target_pairs={{16,24},{17,25},{18,26},{19,27},{20,28},{21,29},{22,30},{23,31}} | collective-permute-start | bytes 786440 | tf_op jit(solution)/shard_map/ppermute | solution.py:369
  84.0 20.3 %collective-permute-start.38 = (f32[64,1024]{1,0:T(8,128)S(1)}, f32[64,1024]{1,0:T(8,128)S(1)}, u32[]{:S(2)}, u32[]{:S(2)}) collective-permute-start(f32[64,1024]{1,0:T(8,128)S(1)} %onward.9), channel_id=1, source_target_pairs={{8,24},{9,25},{10,26},{11,27},{12,28},{13,29},{14,30},{15,31}} | collective-permute-start | bytes 786440 | tf_op jit(solution)/shard_map/ppermute | solution.py:369
  85.4 21.7 %collective-permute-start.34 = (f32[64,1024]{1,0:T(8,128)S(1)}, f32[64,1024]{1,0:T(8,128)S(1)}, u32[]{:S(2)}, u32[]{:S(2)}) collective-permute-start(f32[64,1024]{1,0:T(8,128)S(1)} %get-tuple-element.267), channel_id=1, source_target_pairs={{16,24},{17,25},{18,26},{19,27},{20,28},{21,29},{22,30},{23,31}} | collective-permute-start | bytes 786440 | tf_op jit(solution)/shard_map/ppermute | solution.py:369
  86.7 23.2 %collective-permute-start.36 = (f32[64,1024]{1,0:T(8,128)S(1)}, f32[64,1024]{1,0:T(8,128)S(1)}, u32[]{:S(2)}, u32[]{:S(2)}) collective-permute-start(f32[64,1024]{1,0:T(8,128)S(1)} %onward.11), channel_id=1, source_target_pairs={{8,24},{9,25},{10,26},{11,27},{12,28},{13,29},{14,30},{15,31}} | collective-permute-start | bytes 786440 | tf_op jit(solution)/shard_map/ppermute | solution.py:369
